TPU v7x, 32 devices: a whole 2x2x4 slice. The times are simulated.
32 devices in a mesh: shard: 4 (over z), tensor: 4 (over y, x), section: 2 (over core).
Axes of the slice: x: 2, y: 2, z: 4, core: 2. Of those that a mesh axis runs over, the one named last changes fastest.
Arguments:
- grad_parts: bfloat16 [8, 32, 1024, 1024], P(('tensor', 'section'), None, 'shard')
- weights: bfloat16 [32, 1024, 1024], P(None, 'shard', ('tensor', 'section')), may hold values from -6 to 6
- adam_m: float32 [32, 1024, 1024], P(None, 'shard', ('tensor', 'section'))
- adam_v: float32 [32, 1024, 1024], P(None, 'shard', ('tensor', 'section')), may hold values from 0.01 to 1
- left_stat: float32 [96, 1024, 1024], P('shard', None, ('tensor', 'section')), may hold values from -18 to 18
- right_stat: float32 [96, 1024, 1024], P('shard', None, ('tensor', 'section')), may hold values from -18 to 18
- left_root: bfloat16 [32, 1024, 1024], P(None, 'shard', ('tensor', 'section')), as said below
- right_root: bfloat16 [32, 1024, 1024], P(None, 'shard', ('tensor', 'section')), as said below
- block_owner: int32 [32], replicated, may hold values from 0 to 3, as said below
- block_matrix: int32 [32], replicated, may hold values from 0 to 4, as said below
- factors: float32 [832, 2048], P('shard', ('tensor', 'section')), may hold values from -6 to 6
- factor_grad: bfloat16 [832, 2048], P('shard', ('tensor', 'section')), may hold values from -6 to 6
- factor_m: float32 [832, 2048], P('shard', ('tensor', 'section')), may hold values from -3 to 3
- factor_v: float32 [832, 2048], P('shard', ('tensor', 'section')), may hold values from 0.2 to 2
Outputs:
- new_weights: bfloat16 [32, 1024, 1024], P(None, 'shard')
- adam_m_new: float32 [32, 1024, 1024], P(None, 'shard', ('tensor', 'section'))
- adam_v_new: float32 [32, 1024, 1024], P(None, 'shard', ('tensor', 'section'))
- left_new: float32 [96, 1024, 1024], P('shard', None, ('tensor', 'section'))
- right_new: float32 [96, 1024, 1024], P('shard', None, ('tensor', 'section'))
- factors_new: float32 [832, 2048], P('shard', ('tensor', 'section'))
- factor_m_new: float32 [832, 2048], P('shard', ('tensor', 'section'))
- factor_v_new: float32 [832, 2048], P('shard', ('tensor', 'section'))
Inputs may be any that keep to these rules, and one draw needn't show every extreme that they name: `block_owner`: no owner holds more than 24 blocks, and some owner holds exactly 24. `block_matrix`: matrices 0 to 3 hold 4 blocks each, all other blocks belong to matrix 4. `left_root`: every block is symmetric. `right_root`: every block is symmetric.
All inputs are finite; a program needn't handle non-finite values.
Results may differ from a plain program's by a relative error of at most 0.014.
Values may be sent and summed in bfloat16 or wider, within the bound.
No kernel may reach another device: no remote copies, remote signals or barrier semaphores. Data moves between devices by JAX's collectives and lax.ppermute only.
A program may use at most 384 MiB of HBM per device.

v0:
```python
import functools

import jax
import jax.numpy as jnp
from jax import lax
from jax.experimental import pallas as pl
from jax.experimental.pallas import tpu as pltpu
from jax.sharding import PartitionSpec as P

MATS = 5

BETA_ONE = 0.9
BETA_TWO = 0.95
BETA_STAT = 0.95
LEARNING = 0.1
DECAY_RATE = 0.1
EPSILON = 1e-08
FLOOR_RATE = 1e-06
CORRECT_ONE = 1.0 - 0.9**10
CORRECT_TWO = 1.0 - 0.95**10

GROUP = ("tensor", "section")
ALL = ("shard", "tensor", "section")
VMEM_LIMIT = 48 * 1024 * 1024
LANES = 128
SMALL = pl.CostEstimate(flops=0, bytes_accessed=0, transcendentals=0)


def params():
    return pltpu.CompilerParams(vmem_limit_bytes=VMEM_LIMIT)


def adam_direction(grad_float, moment, second):
    moment_new = BETA_ONE * moment + (1.0 - BETA_ONE) * grad_float
    second_new = BETA_TWO * second + (1.0 - BETA_TWO) * grad_float * grad_float
    direction = moment_new / CORRECT_ONE / (jnp.sqrt(second_new / CORRECT_TWO) + EPSILON)
    return (moment_new, second_new, direction)


def copy_blocks(pairs, held, arrived, left):
    into = [
        pltpu.make_async_copy(source, held.at[i], arrived.at[i])
        for i, (source, _) in enumerate(pairs)
    ]
    out_of = [
        pltpu.make_async_copy(held.at[i], target, left.at[i]) for i, (_, target) in enumerate(pairs)
    ]
    for copy in into:
        copy.start()
    for arrival, copy in zip(into, out_of):
        arrival.wait()
        copy.start()
    for copy in out_of:
        copy.wait()


def copy_scratch(count, tile, kind):
    return [
        pltpu.VMEM((count,) + tile, kind),
        pltpu.SemaphoreType.DMA((count,)),
        pltpu.SemaphoreType.DMA((count,)),
    ]


def reorder_kernel(order, blocks, out, held, arrived, left):
    pairs = [(blocks.at[order[i]], out.at[i]) for i in range(out.shape[0])]
    copy_blocks(pairs, held, arrived, left)


def reorder(blocks, order):
    count, tile = order.shape[0], blocks.shape[1:]
    return pl.pallas_call(
        reorder_kernel,
        grid_spec=pltpu.PrefetchScalarGridSpec(
            num_scalar_prefetch=1,
            grid=(1,),
            in_specs=[pl.BlockSpec(memory_space=pl.ANY)],
            out_specs=pl.BlockSpec(memory_space=pl.ANY),
            scratch_shapes=copy_scratch(count, tile, blocks.dtype),
        ),
        out_shape=jax.ShapeDtypeStruct((count,) + tile, blocks.dtype),
        compiler_params=params(),
        cost_estimate=SMALL,
    )(order, blocks)


def place_kernel(sources, target, *refs):
    out, held, arrived, left = refs[-4:]
    blocks = [ref.at[i] for ref in refs[:sources] for i in range(ref.shape[0])]
    pairs = [(block, out.at[target[i]]) for i, block in enumerate(blocks)]
    copy_blocks(pairs, held, arrived, left)


def place_blocks(arrays, target, total, earlier):
    tile, kind = arrays[0].shape[1:], arrays[0].dtype
    inputs = list(arrays) + list(earlier)
    return pl.pallas_call(
        functools.partial(place_kernel, len(arrays)),
        grid_spec=pltpu.PrefetchScalarGridSpec(
            num_scalar_prefetch=1,
            grid=(1,),
            in_specs=[pl.BlockSpec(memory_space=pl.ANY)] * len(inputs),
            out_specs=pl.BlockSpec(memory_space=pl.ANY),
            scratch_shapes=copy_scratch(target.shape[0], tile, kind),
        ),
        out_shape=jax.ShapeDtypeStruct((total,) + tile, kind),
        input_output_aliases={1 + len(arrays) + i: i for i in range(len(earlier))},
        compiler_params=params(),
        cost_estimate=SMALL,
    )(target, *inputs)


def adam_kernel(place, grad, moment, second, moment_out, second_out, total):
    moment_new, second_new, direction = adam_direction(
        grad[0].astype(jnp.float32), moment[0], second[0]
    )
    moment_out[0] = moment_new
    second_out[0] = second_new
    total[0] = jnp.sum(direction * direction, axis=0, keepdims=True)


def adam(grad_tiles, place, moment, second):
    count, rows, cols = moment.shape
    own = pl.BlockSpec((1, rows, cols), lambda i, place: (i, 0, 0))
    return pl.pallas_call(
        adam_kernel,
        grid_spec=pltpu.PrefetchScalarGridSpec(
            num_scalar_prefetch=1,
            grid=(count,),
            in_specs=[
                pl.BlockSpec((1, rows, cols), lambda i, place: (place[i], 0, 0)),
                own,
                own,
            ],
            out_specs=[own, own, pl.BlockSpec((1, 1, cols), lambda i, place: (i, 0, 0))],
        ),
        out_shape=[
            jax.ShapeDtypeStruct(moment.shape, jnp.float32),
            jax.ShapeDtypeStruct(moment.shape, jnp.float32),
            jax.ShapeDtypeStruct((count, 1, cols), jnp.float32),
        ],
        compiler_params=params(),
        cost_estimate=SMALL,
    )(place, grad_tiles, moment, second)


def gram_kernel(chosen, grad, out):
    parts, _, rows, width = grad.shape
    size = parts * rows
    whole = grad[:, 0].reshape(size, width)
    turned = whole.T
    step = 2 * LANES
    for start in range(0, size, step):
        left = lax.dot_general(
            whole,
            whole[start : start + step, :],
            (((1,), (1,)), ((), ())),
            preferred_element_type=jnp.float32,
        ).astype(jnp.bfloat16)
        right = lax.dot_general(
            turned,
            whole[:, start : start + step],
            (((1,), (0,)), ((), ())),
            preferred_element_type=jnp.float32,
        ).astype(jnp.bfloat16)
        for half in range(2):
            slab = start // LANES + half
            out[slab, 0, 0] = left[:, half * LANES : (half + 1) * LANES]
            out[slab, 0, 1] = right[:, half * LANES : (half + 1) * LANES]


def grams(grad_blocks, chosen):
    shards, per, rows, width = grad_blocks.shape
    size = shards * rows
    slabs = size // LANES
    count = chosen.shape[0]
    return pl.pallas_call(
        gram_kernel,
        grid_spec=pltpu.PrefetchScalarGridSpec(
            num_scalar_prefetch=1,
            grid=(count,),
            in_specs=[
                pl.BlockSpec((shards, 1, rows, width), lambda j, chosen: (0, chosen[j], 0, 0))
            ],
            out_specs=pl.BlockSpec(
                (slabs, 1, 2, size, LANES), lambda j, chosen: (0, j, 0, 0, 0)
            ),
        ),
        out_shape=jax.ShapeDtypeStruct((slabs, count, 2, size, LANES), jnp.bfloat16),
        compiler_params=params(),
        cost_estimate=SMALL,
    )(chosen, grad_blocks)


def stat_kernel(
    base, source, entry, filled, left_stat, right_stat, left_gram, right_gram, *refs
):
    left_out, right_out = refs[-2:]
    full = filled[pl.program_id(0)] > 0
    left = left_gram[0, 0, 0].astype(jnp.float32)
    right = right_gram[0, 0, 0].astype(jnp.float32)
    left_out[0] = BETA_STAT * left_stat[0] + jnp.where(full, (1.0 - BETA_STAT) * left, 0.0)
    right_out[0] = BETA_STAT * right_stat[0] + jnp.where(full, (1.0 - BETA_STAT) * right, 0.0)


def refresh(left_stat, right_stat, received, base, source, entry, filled, earlier):
    slots, size, cols = left_stat.shape
    count = source.shape[0]
    own = pl.BlockSpec((1, size, cols), lambda r, base, source, entry, filled: (base[0] + r, 0, 0))
    gram = (1, 1, 1, size, cols)
    shape = jax.ShapeDtypeStruct(left_stat.shape, jnp.float32)
    return pl.pallas_call(
        stat_kernel,
        grid_spec=pltpu.PrefetchScalarGridSpec(
            num_scalar_prefetch=4,
            grid=(count,),
            in_specs=[
                own,
                own,
                pl.BlockSpec(
                    gram, lambda r, base, source, entry, filled: (source[r], entry[r], 0, 0, 0)
                ),
                pl.BlockSpec(
                    gram, lambda r, base, source, entry, filled: (source[r], entry[r], 1, 0, 0)
                ),
            ]
            + [pl.BlockSpec(memory_space=pl.ANY)] * len(earlier),
            out_specs=[own, own],
        ),
        out_shape=[shape, shape],
        input_output_aliases={8 + i: i for i in range(len(earlier))},
        compiler_params=params(),
        cost_estimate=SMALL,
    )(
        base.reshape(1), source, entry, filled, left_stat, right_stat, received, received, *earlier
    )


def left_product(left, grad):
    slabs, _, rows, _ = left.shape
    left_rows = jnp.concatenate([left[s, 0] for s in range(slabs)], axis=1)
    whole = grad[:, 0].reshape(grad.shape[0] * rows, grad.shape[3])
    return jnp.dot(left_rows, whole, preferred_element_type=jnp.float32).astype(jnp.bfloat16)


def precond_kernel(left, grad, right, out, total):
    slabs, _, rows, cols = left.shape
    parts = grad.shape[0]
    mixed = left_product(left, grad)
    total[...] = jnp.zeros_like(total)
    step = 2
    for start in range(0, slabs, step):
        columns = jnp.concatenate(
            [right[:, s, 0].reshape(parts * rows, cols) for s in range(start, start + step)], axis=1
        )
        piece = jnp.dot(mixed, columns, preferred_element_type=jnp.float32)
        out[0, :, start * cols : (start + step) * cols] = piece.astype(jnp.bfloat16)
        square = jnp.sum(piece * piece, axis=0, keepdims=True)
        total[0] += square[:, :cols] + square[:, cols:]


def tile_sources(mine, count, spread):
    found = {(mine, b): (0, spread * b) for b in range(count)}
    for hop in range(1, count):
        for i in range(count - hop):
            if mine + hop < count:
                found[mine + hop, (mine + hop + i) % count] = (hop, spread * i)
            if mine - hop >= 0:
                found[mine - hop, (mine - hop - i) % count] = (count - 1 + hop, spread * i)
    return found


def precond_tiles_kernel(me, left, grad, *refs):
    rights, out, total = refs[:-2], refs[-2], refs[-1]
    slabs, _, rows, cols = left.shape
    parts = grad.shape[0]
    spread = slabs // parts
    mixed = left_product(left, grad)
    total[...] = jnp.zeros_like(total)
    for mine in range(parts):

        @pl.when(me[0] == mine)
        def _(mine=mine):
            found = tile_sources(mine, parts, spread)
            for b in range(parts):
                piece = jnp.zeros((rows, spread * cols), jnp.float32)
                for a in range(parts):
                    turned = (a, b) not in found
                    array, first = found[(b, a) if turned else (a, b)]
                    tile = jnp.concatenate(
                        [rights[array][first + s, 0] for s in range(spread)], axis=1
                    )
                    piece += lax.dot_general(
                        mixed[:, a * rows : (a + 1) * rows],
                        tile,
                        (((1,), (1 if turned else 0,)), ((), ())),
                        preferred_element_type=jnp.float32,
                    )
                out[0, :, b * rows : (b + 1) * rows] = piece.astype(jnp.bfloat16)
                square = jnp.sum(piece * piece, axis=0, keepdims=True)
                total[0] += sum(square[:, s * cols : (s + 1) * cols] for s in range(spread))


def first_hop(right):
    slabs, per, rows, cols = right.shape
    count, me = lax.axis_size("shard"), lax.axis_index("shard")
    spread = slabs // count
    lane = jnp.arange(spread * (count - 1), dtype=jnp.int32)
    moved = []
    for sign in (1, -1):
        tiles = (me + sign * (lane // spread)) % count
        picked = reorder(right.reshape(slabs, per * rows, cols), tiles * spread + lane % spread)
        moved.append(picked.reshape(lane.shape[0], per, rows, cols))
    return hop(moved)


def hop(moved):
    count = lax.axis_size("shard")
    down = [(a, a - 1) for a in range(1, count)]
    up = [(a, a + 1) for a in range(count - 1)]
    return lax.ppermute(moved[0], "shard", down), lax.ppermute(moved[1], "shard", up)


def next_hop(moved, spread):
    return hop([part[: part.shape[0] - spread] for part in moved])


def precondition(left, start, grad_blocks, rights):
    shards, count, rows, width = grad_blocks.shape
    slabs, _, _, cols = left.shape
    size = shards * rows
    whole = len(rights) == 1
    if whole:
        right_specs = [pl.BlockSpec((shards, slabs, 1, rows, cols), lambda m, me: (0, 0, start + m, 0, 0))]
    else:
        right_specs = [
            pl.BlockSpec((right.shape[0], 1, rows, cols), lambda m, me: (0, start + m, 0, 0))
            for right in rights
        ]
    body = precond_tiles_kernel
    if whole:
        body = lambda me, *refs: precond_kernel(*refs)
    return pl.pallas_call(
        body,
        grid_spec=pltpu.PrefetchScalarGridSpec(
            num_scalar_prefetch=1,
            grid=(count,),
            in_specs=[
                pl.BlockSpec((slabs, 1, rows, cols), lambda m, me: (0, start + m, 0, 0)),
                pl.BlockSpec((shards, 1, rows, width), lambda m, me: (0, m, 0, 0)),
            ]
            + right_specs,
            out_specs=[
                pl.BlockSpec((1, rows, width), lambda m, me: (m, 0, 0)),
                pl.BlockSpec((1, 1, cols), lambda m, me: (m, 0, 0)),
            ],
        ),
        out_shape=[
            jax.ShapeDtypeStruct((count, rows, width), jnp.bfloat16),
            jax.ShapeDtypeStruct((count, 1, cols), jnp.float32),
        ],
        compiler_params=params(),
        cost_estimate=SMALL,
    )(lax.axis_index("shard").reshape(1), left, grad_blocks, *rights)


def update_kernel(scale, weights, precond, out):
    slabs = weights.shape[0]
    factor = scale[pl.program_id(0)]
    old = jnp.concatenate([weights[s, 0] for s in range(slabs)], axis=1).astype(jnp.float32)
    step = factor * precond[0].astype(jnp.float32) + DECAY_RATE * old
    out[0] = (old - LEARNING * step).astype(jnp.bfloat16)


def update(weights, start, precond, scale):
    slabs, _, rows, cols = weights.shape
    count = precond.shape[0]
    width = slabs * cols
    own = pl.BlockSpec((1, rows, width), lambda m, scale: (m, 0, 0))
    return pl.pallas_call(
        update_kernel,
        grid_spec=pltpu.PrefetchScalarGridSpec(
            num_scalar_prefetch=1,
            grid=(count,),
            in_specs=[
                pl.BlockSpec((slabs, 1, rows, cols), lambda m, scale: (0, start + m, 0, 0)),
                own,
            ],
            out_specs=own,
        ),
        out_shape=jax.ShapeDtypeStruct((count, rows, width), jnp.bfloat16),
        compiler_params=params(),
        cost_estimate=SMALL,
    )(scale, weights, precond)


def pair_kernel(picked, first, second, third, fourth, received, send_a, keep_a, send_b, keep_b):
    half = first.shape[1] // 2
    added = [
        (own[0].astype(jnp.float32) + received[u].astype(jnp.float32)).astype(jnp.bfloat16)
        for u, own in enumerate((first, second, third, fourth))
    ]
    for ref, chosen, start in (
        (send_a, (1, 3), 0),
        (keep_a, (0, 2), 0),
        (send_b, (2, 3), half),
        (keep_b, (0, 1), half),
    ):
        for i, u in enumerate(chosen):
            ref[i, 0] = added[u][start : start + half]


def add_pair(partials, received, picked):
    _, rows, width = partials.shape
    count = received.shape[0] // 4
    half = jax.ShapeDtypeStruct((2, count, rows // 2, width), partials.dtype)

    def own(u):
        return pl.BlockSpec((1, rows, width), lambda i, picked: (picked[4 * i + u], 0, 0))

    return pl.pallas_call(
        pair_kernel,
        grid_spec=pltpu.PrefetchScalarGridSpec(
            num_scalar_prefetch=1,
            grid=(count,),
            in_specs=[own(0), own(1), own(2), own(3)]
            + [pl.BlockSpec((4, rows, width), lambda i, picked: (i, 0, 0))],
            out_specs=[pl.BlockSpec((2, 1, rows // 2, width), lambda i, picked: (0, i, 0, 0))] * 4,
        ),
        out_shape=[half] * 4,
        compiler_params=params(),
        cost_estimate=SMALL,
    )(picked, partials, partials, partials, partials, received)


def add(one, two):
    return (one.astype(jnp.float32) + two.astype(jnp.float32)).astype(jnp.bfloat16)


def swap(array, bit):
    devices = lax.axis_size("tensor")
    return lax.ppermute(array, "tensor", [(t, t ^ bit) for t in range(devices)])


def swap_core(array):
    return lax.ppermute(array, "section", [(0, 1), (1, 0)])


def pick(picked):
    core = lax.axis_index("section")
    relative = jnp.arange(4, dtype=jnp.int32) ^ lax.axis_index("tensor")
    mine = jnp.take(picked, relative * 2 + core, axis=0).T.reshape(-1)
    other = jnp.take(picked, relative * 2 + 1 - core, axis=0).T.reshape(-1)
    return mine, other


def first_sums(partials, sent, mine):
    received = swap_core(sent)
    send_a, keep_a, send_b, keep_b = add_pair(partials, received, mine)
    return add(keep_a, swap(send_a, 1)), add(keep_b, swap(send_b, 2))


def last_sums(sum_a, sum_b):
    last_a = add(sum_a[0], swap(sum_a[1], 2))
    last_b = add(sum_b[0], swap(sum_b[1], 1))
    return jnp.concatenate([last_a, last_b], axis=1)


def gather_blocks(first, second, by_entry, early_work, finish):
    total = by_entry.size
    cut = first.shape[0]
    tensor, core = lax.axis_index("tensor"), lax.axis_index("section")
    x_first, y_second = swap(first, 1), swap(second, 2)
    y_first, x_second = swap(first, 2), swap(second, 1)
    x_first, y_second, early_work = lax.optimization_barrier((x_first, y_second, early_work))
    d_first, d_second = swap(x_first, 2), swap(y_second, 1)

    def targets(bits, core):
        places = [by_entry[(tensor ^ bit) * 2 + core] for bit in bits]
        return [piece for place in places for piece in (place[:cut], place[cut:])]

    near = [first, second, x_first, x_second, y_first, y_second]
    near_target = targets((0, 1, 2), core) + targets((0, 1, 2), 1 - core)
    near = near + [swap_core(piece) for piece in near]
    placed = place_blocks(near, jnp.concatenate(near_target), total, [])
    late_work = finish(early_work)
    d_first, d_second, placed, late_work = lax.optimization_barrier(
        (d_first, d_second, placed, late_work)
    )
    far = [d_first, d_second]
    far_target = targets((3,), core) + targets((3,), 1 - core)
    far = far + [swap_core(piece) for piece in far]
    return place_blocks(far, jnp.concatenate(far_target), total, [placed]), late_work


def shards(
    grad_parts,
    weights,
    adam_m,
    adam_v,
    left_stat,
    right_stat,
    left_root,
    right_root,
    block_owner,
    block_matrix,
    factors,
    factor_grad,
    factor_m,
    factor_v,
):
    capacity = left_stat.shape[0]
    blocks, rows, cols = weights.shape
    size = left_stat.shape[1]
    group = size // cols
    per = blocks // group
    sends = -(-capacity // group)
    owner_index = lax.axis_index("shard")
    group_index = lax.axis_index(GROUP)
    owner_count = lax.axis_size("shard")

    ids = jnp.arange(blocks, dtype=jnp.int32)
    owners = jnp.arange(owner_count, dtype=jnp.int32)
    loads = jnp.sum((block_owner[None, :] == owners[:, None]).astype(jnp.int32), axis=1)
    heavy = jnp.min(jnp.where(loads == jnp.max(loads), owners, owner_count))
    turn = (block_owner - heavy) % owner_count
    own_turn = (owner_index - heavy) % owner_count
    before = (turn[None, :] < turn[:, None]) | (
        (turn[None, :] == turn[:, None]) & (ids[None, :] < ids[:, None])
    )
    position = jnp.sum(before.astype(jnp.int32), axis=1)
    place = (position % group) * per + position // group
    order = jnp.sum(jnp.where(place[None, :] == ids[:, None], ids[None, :], 0), axis=1)

    first = jnp.sum((turn < own_turn).astype(jnp.int32))
    held = jnp.sum((turn == own_turn).astype(jnp.int32))
    early = sends - 1 if blocks - capacity <= group else 0
    is_heavy = own_turn == 0
    own_entry = (first - group_index + group - 1) // group

    def deal(tiles):
        return lax.all_to_all(
            tiles.reshape(group, per, rows, cols), GROUP, split_axis=0, concat_axis=0, tiled=True
        )

    by_entry = order.reshape(group, per)
    partials = grad_parts[0]
    cuts = [(0, early), (early, per)] if early else [(0, per)]
    orders = [pick(by_entry[:, a:b]) for a, b in cuts]
    right_dealt = deal(reorder(right_root, order))
    sent = [reorder(partials, other) for _, other in orders]
    right_dealt, sent[-1] = lax.optimization_barrier((right_dealt, sent[-1]))
    if early and owner_count == 4 and rows * owner_count == size:
        spread = group // owner_count
        near = first_hop(right_dealt)
        sums = first_sums(partials, sent[0], orders[0][0])
        sums, near = lax.optimization_barrier((sums, near))
        gradient = [last_sums(*sums)]
        middle = next_hop(near, spread)
        sums = first_sums(partials, sent[1], orders[1][0])
        sums, middle = lax.optimization_barrier((sums, middle))
        gradient.append(last_sums(*sums))
        far = next_hop(middle, spread)
        downs, ups = zip(near, middle, far)
        rights = [right_dealt, *downs, *ups]
    else:
        gradient = [
            last_sums(*first_sums(partials, part, mine)) for part, (mine, _) in zip(sent, orders)
        ]
        rights = [lax.all_gather(right_dealt, "shard", axis=0)]
    gradient = [lax.optimization_barrier(part) for part in gradient]
    grad_blocks = [lax.all_gather(part, "shard", axis=0) for part in gradient]
    left_dealt = deal(reorder(left_root, order))
    weights_dealt = deal(reorder(weights, order))
    tiles = jnp.concatenate(gradient, axis=0).reshape(per, rows, group, cols)
    tiles = deal(jnp.transpose(tiles, (2, 0, 1, 3)))

    if early:
        grad_blocks[0], left_dealt, weights_dealt, tiles = lax.optimization_barrier(
            (grad_blocks[0], left_dealt, weights_dealt, tiles)
        )
        slabs = grams(grad_blocks[0], jnp.arange(early, dtype=jnp.int32))
        slabs, left_dealt, tiles = lax.optimization_barrier((slabs, left_dealt, tiles))
        received = lax.all_to_all(slabs, GROUP, split_axis=0, concat_axis=0, tiled=True)
    adam_m_new, adam_v_new, adam_total = adam(
        tiles.reshape(blocks, rows, cols), place, adam_m, adam_v
    )
    pieces = [precondition(left_dealt, 0, grad_blocks[0], rights)]
    if early:
        grad_blocks[1], adam_total, pieces[0] = lax.optimization_barrier(
            (grad_blocks[1], adam_total, pieces[0])
        )
        pieces.append(precondition(left_dealt, early, grad_blocks[1], rights))
    entry = jnp.where(is_heavy, early, own_entry) - early
    last_slabs = grams(grad_blocks[-1], jnp.clip(entry, 0, per - 1 - early).reshape(1))
    precond_total = jnp.concatenate([total for _, total in pieces], axis=0)

    matrix_range = jnp.arange(MATS, dtype=jnp.int32)
    onehot = (block_matrix[:, None] == matrix_range[None, :]).astype(jnp.float32)
    own_order = lax.dynamic_slice_in_dim(order, group_index * per, per)
    own_onehot = jnp.sum(
        jnp.where((own_order[:, None] == ids[None, :])[:, :, None], onehot[None, :, :], 0.0), axis=1
    )
    adam_part = jnp.sum(jnp.sum(adam_total, axis=(1, 2))[:, None] * onehot, axis=0)
    shampoo_part = jnp.sum(jnp.sum(precond_total, axis=(1, 2))[:, None] * own_onehot, axis=0)
    parts = jnp.pad(jnp.stack([adam_part, shampoo_part]), ((0, 6), (0, LANES - MATS)))
    if early:
        received, last_slabs, parts = lax.optimization_barrier((received, last_slabs, parts))
    devices = owner_count * group
    parts = lax.all_to_all(
        jnp.broadcast_to(parts[None], (devices,) + parts.shape), ALL, 0, 0, tiled=True
    )
    adam_norm, shampoo_norm = jnp.sum(parts, axis=0)[:2, :MATS]
    counts = jnp.sum(onehot, axis=0) * float(size * size)
    graft_scale = jnp.sqrt(adam_norm / (shampoo_norm + FLOOR_RATE * counts))
    block_scale = jnp.sum(own_onehot * graft_scale[None, :], axis=1)

    last = lax.all_to_all(last_slabs, GROUP, split_axis=0, concat_axis=0, tiled=True)
    updated = [
        update(weights_dealt, a, piece, block_scale[a:b])
        for (a, b), (piece, _) in zip(cuts, pieces)
    ]
    if len(updated) == 1:
        updated = [updated[0][: per // 2], updated[0][per // 2 :]]
    stats = ()
    if early:
        ranks = jnp.arange(early * group, dtype=jnp.int32)
        base = jnp.where(is_heavy, 0, capacity - early * group)
        filled = jnp.where(is_heavy, 1, 0) * jnp.ones_like(ranks)
        stats = refresh(
            left_stat, right_stat, received, base, ranks % group, ranks // group, filled, stats
        )
    base = jnp.where(is_heavy, early * group, 0)
    ranks = base + jnp.arange(capacity - early * group, dtype=jnp.int32)
    filled = (ranks < held).astype(jnp.int32)
    source = (first + ranks) % group
    nothing = jnp.zeros_like(ranks)
    finish = lambda earlier: refresh(
        left_stat, right_stat, last, base, source, nothing, filled, earlier
    )
    new_weights, (left_new, right_new) = gather_blocks(*updated, by_entry, stats, finish)

    factor_m_new, factor_v_new, factor_step = adam_direction(
        factor_grad.astype(jnp.float32), factor_m, factor_v
    )
    factors_new = factors - LEARNING * (factor_step + DECAY_RATE * factors)
    return (
        new_weights,
        adam_m_new,
        adam_v_new,
        left_new,
        right_new,
        factors_new,
        factor_m_new,
        factor_v_new,
    )


def solution(mesh):
    tile = P(None, "shard", GROUP)
    stat = P("shard", None, GROUP)
    factor = P("shard", GROUP)
    in_specs = (P(GROUP, None, "shard", None), tile, tile, tile, stat, stat, tile, tile, P(), P())
    out_specs = (P(None, "shard", None), tile, tile, stat, stat)
    return jax.shard_map(
        shards,
        mesh=mesh,
        in_specs=in_specs + (factor,) * 4,
        out_specs=out_specs + (factor,) * 3,
        check_vma=False,
    )
```

profile of v0, /device:TPU:0, one launch (start us, length us, event | category | flops | bytes accessed | tf_op | source)
XLA Modules:
  0.0 537.8 jit_solution(16779302904852848651)
XLA Ops:
  8.6 1.3 fusion.10
  10.5 2.0 fusion.18
  14.4 4.2 shard_map.197
  19.1 7.3 %shard_map.199 = bf16[32,256,128]{2,1,0:T(8,128)(2,1)S(1)} custom-call(s32[32]{0:T(128)S(1)} %select_reduce_fusion.order, bf16[32,256,128]{2,1,0:T(8,128)(2,1)S(1)} %copy-done.14), custom_call_target="tpu_custom_call" | custom-call | tf_op jit(solution)/shard_map/pallas_call | solution.py:72
  26.4 1.3 copy-done.8
  27.7 4.8 all-to-all-start
  34.2 4.1 shard_map.200
  38.3 5.4 %shard_map.198 = (bf16[2,2,128,1024]{3,2,1,0:T(8,128)(2,1)S(1)}, bf16[2,2,128,1024]{3,2,1,0:T(8,128)(2,1)S(1)}, bf16[2,2,128,1024]{3,2,1,0:T(8,128)(2,1)}, bf16[2,2,128,1024]{3,2,1,0:T(8,128)(2,1)S(1)}) custom-call(s32[8]{0:T(128)S(1)} %reshape.184.picked, bf16[32,256,1024]{2,1,0:T(8,128)(2,1)} %bitcast.102, bf16[32,256,1024]{2,1,0:T(8,128)(2,1)} %bitcast.103, ...), custom_call_target="tpu_custom_call" | custom-call | tf_op jit(solution)/shard_map/pallas_call | solution.py:421
  45.7 2.0 collective-permute-start.2
  47.7 11.6 %all-to-all-done.refs_0_ = bf16[8,4,256,128]{3,2,1,0:T(8,128)(2,1)S(1)} async-done(((bf16[8,4,256,128]{3,2,1,0:T(8,128)(2,1)}), bf16[8,4,256,128]{3,2,1,0:T(8,128)(2,1)S(1)}, u32[]{:S(2)}, u32[]{:S(2)}) %all-to-all-start) | async-done | bytes 2097184 | tf_op jit(solution)/shard_map/all_to_all | solution.py:542
  60.2 1.4 collective-permute-start.3
  62.6 4.6 collective-permute-start.4
  67.8 13.0 %collective-permute-done.2 = bf16[2,2,128,1024]{3,2,1,0:T(8,128)(2,1)} collective-permute-done((bf16[2,2,128,1024]{3,2,1,0:T(8,128)(2,1)}, bf16[2,2,128,1024]{3,2,1,0:T(8,128)(2,1)}, u32[]{:S(2)}, u32[]{:S(2)}) %collective-permute-start.2) | collective-permute-done | bytes 1048608 | tf_op jit(solution)/shard_map/ppermute | solution.py:442
  80.8 1.6 add_convert_fusion.2
  82.5 10.4 %collective-permute-done.1 = bf16[2,2,128,1024]{3,2,1,0:T(8,128)(2,1)S(1)} collective-permute-done((bf16[2,2,128,1024]{3,2,1,0:T(8,128)(2,1)S(1)}, bf16[2,2,128,1024]{3,2,1,0:T(8,128)(2,1)S(1)}, u32[]{:S(2)}, u32[]{:S(2)}) %collective-permute-start.1) | collective-permute-done | bytes 1048608 | tf_op jit(solution)/shard_map/ppermute | solution.py:442
  93.3 2.2 collective-permute-done.3.refs_1_
  95.5 2.1 collective-permute-done.4.refs_4_
  97.6 1.4 collective-permute-start.5
  99.1 2.6 collective-permute-start.6
  101.7 6.0 %collective-permute-done.5 = bf16[2,128,1024]{2,1,0:T(8,128)(2,1)S(1)} collective-permute-done((bf16[2,128,1024]{2,1,0:T(8,128)(2,1)S(1)}, bf16[2,128,1024]{2,1,0:T(8,128)(2,1)S(1)}, u32[]{:S(2)}, u32[]{:S(2)}) %collective-permute-start.5) | collective-permute-done | bytes 524320 | tf_op jit(solution)/shard_map/ppermute | solution.py:442
  107.9 4.4 collective-permute-done.6
  113.6 5.2 shard_map.203
  118.8 4.2 all-to-all-start.1
  123.2 6.2 %shard_map.205 = (bf16[2,2,128,1024]{3,2,1,0:T(8,128)(2,1)}, bf16[2,2,128,1024]{3,2,1,0:T(8,128)(2,1)S(1)}, bf16[2,2,128,1024]{3,2,1,0:T(8,128)(2,1)S(1)}, bf16[2,2,128,1024]{3,2,1,0:T(8,128)(2,1)S(1)}) custom-call(s32[8]{0:T(128)S(1)} %reshape.193.picked, bf16[32,256,1024]{2,1,0:T(8,128)(2,1)} %bitcast.106, bf16[32,256,1024]{2,1,0:T(8,128)(2,1)} %bitcast.107, ...), custom_call_target="tpu_custom_call" | custom-call | tf_op jit(solution)/shard_map/pallas_call | solution.py:421
  129.3 1.9 collective-permute-start.9
  131.3 1.5 collective-permute-start.8
  133.9 1.3 collective-permute-start.10
  136.3 5.7 %collective-permute-start.11 = (bf16[4,4,256,128]{3,2,1,0:T(8,128)(2,1)}, bf16[4,4,256,128]{3,2,1,0:T(8,128)(2,1)}, u32[]{:S(2)}, u32[]{:S(2)}) collective-permute-start(bf16[4,4,256,128]{3,2,1,0:T(8,128)(2,1)} %slice.162), channel_id=1, source_target_pairs={{0,8},{8,16},{16,24},{1,9},{9,17},{17,25},{2,10},{10,18},{18,26},{... | collective-permute-start | bytes 3145736 | tf_op jit(solution)/shard_map/ppermute | solution.py:321
  142.0 7.3 %shard_map.204 = bf16[32,256,128]{2,1,0:T(8,128)(2,1)S(1)} custom-call(s32[32]{0:T(128)S(1)} %select_reduce_fusion.order, bf16[32,256,128]{2,1,0:T(8,128)(2,1)S(1)} %copy-done.16), custom_call_target="tpu_custom_call" | custom-call | tf_op jit(solution)/shard_map/pallas_call | solution.py:72
  149.3 1.3 copy-done.7
  150.6 20.5 %collective-permute-done.9 = bf16[2,2,128,1024]{3,2,1,0:T(8,128)(2,1)S(1)} collective-permute-done((bf16[2,2,128,1024]{3,2,1,0:T(8,128)(2,1)S(1)}, bf16[2,2,128,1024]{3,2,1,0:T(8,128)(2,1)S(1)}, u32[]{:S(2)}, u32[]{:S(2)}) %collective-permute-start.9) | collective-permute-done | bytes 1048608 | tf_op jit(solution)/shard_map/ppermute | solution.py:442
  171.2 1.4 add_convert_fusion
  172.6 1.3 copy-done.26
  173.9 3.6 all-to-all-start.2
  177.5 2.0 add_convert_fusion.1
  179.6 28.4 %collective-permute-done.10.refs_2_ = bf16[4,4,256,128]{3,2,1,0:T(8,128)(2,1)S(1)} collective-permute-done((bf16[4,4,256,128]{3,2,1,0:T(8,128)(2,1)}, bf16[4,4,256,128]{3,2,1,0:T(8,128)(2,1)S(1)}, u32[]{:S(2)}, u32[]{:S(2)}) %collective-permute-start.10) | collective-permute-done | bytes 1048608 | tf_op jit(solution)/shard_map/ppermute | solution.py:321
  208.8 13.4 %collective-permute-done.12 = bf16[2,128,1024]{2,1,0:T(8,128)(2,1)S(1)} collective-permute-done((bf16[2,128,1024]{2,1,0:T(8,128)(2,1)S(1)}, bf16[2,128,1024]{2,1,0:T(8,128)(2,1)S(1)}, u32[]{:S(2)}, u32[]{:S(2)}) %collective-permute-start.12) | collective-permute-done | bytes 524320 | tf_op jit(solution)/shard_map/ppermute | solution.py:442
  223.6 3.4 bitcast_bitcast_fusion
  227.1 30.9 %all_to_all.35 = bf16[8,4,256,128]{3,2,1,0:T(8,128)(2,1)} all-to-all(bf16[8,4,256,128]{3,2,1,0:T(8,128)(2,1)} %bitcast_bitcast_fusion), channel_id=1, replica_groups=mesh['shard'=4,'tensor'=4,'section'=2] {'tensor','section'}, dimensions={0} | all-to-all | bytes 4194304 | tf_op jit(solution)/shard_map/all_to_all | solution.py:542
  258.0 2.2 copy-done.1
  260.2 12.0 %shard_map.206 = bf16[8,2,2,1024,128]{4,3,2,1,0:T(8,128)(2,1)} custom-call(s32[2]{0:T(128)S(1)} %iota.51.chosen, bf16[4,2,256,1024]{3,2,1,0:T(8,128)(2,1)S(1)} %bitcast.94), custom_call_target="tpu_custom_call" | custom-call | tf_op jit(solution)/shard_map/pallas_call | solution.py:177
  272.1 5.0 all-to-all-start.4
  278.6 1.4 collective-permute-start.14
  281.1 4.6 collective-permute-start.15
  285.9 20.5 %shard_map.207 = (f32[32,256,128]{2,1,0:T(8,128)}, f32[32,256,128]{2,1,0:T(8,128)}, f32[32,1,128]{2,1,0:T(1,128)S(1)}) custom-call(s32[32]{0:T(128)S(1)} %fusion.12.place, bf16[32,256,128]{2,1,0:T(8,128)(2,1)S(1)} %bitcast.97, f32[32,256,128]{2,1,0:T(8,128)} %moment.1, f32[32,256,128]{2,1,0:T(8,128)} %second.1), custom_call_target="tpu_custom_call" | custom-call | tf_op jit(solution)/shard_map/pallas_call | solution.py:125
  306.4 5.0 shard_map.208
  314.0 51.1 %all-gather.7.cloned.1.call-done = bf16[8,256,1024]{2,1,0:T(8,128)(2,1)} async-done(((bf16[2,256,1024]{2,1,0:T(8,128)(2,1)}), bf16[8,256,1024]{2,1,0:T(8,128)(2,1)}) %all-gather.7.cloned.1.call-update) | async-done | bytes 4194320 | tf_op jit(solution)/shard_map/all_gather | solution.py:572
  365.4 6.3 %shard_map.209 = bf16[8,1,2,1024,128]{4,3,2,1,0:T(8,128)(2,1)S(1)} custom-call(s32[1]{0:T(128)} %bitcast.25.chosen, bf16[4,2,256,1024]{3,2,1,0:T(8,128)(2,1)} %bitcast.110), custom_call_target="tpu_custom_call" | custom-call | tf_op jit(solution)/shard_map/pallas_call | solution.py:177
  371.7 2.1 copy-done.2
  373.8 5.0 shard_map.210
  380.2 16.1 %all_to_all.36 = f32[32,8,128]{2,1,0:T(8,128)S(1)} all-to-all(f32[32,8,128]{2,1,0:T(8,128)S(1)} %broadcast_in_dim.47), channel_id=1, replica_groups=mesh['shard'=4,'tensor'=4,'section'=2] {'shard','tensor','section'}, dimensions={0} | all-to-all | bytes 262144 | tf_op jit(solution)/shard_map/all_to_all | solution.py:610
  396.3 4.8 all-to-all-start.6
  403.7 1.8 collective-permute-start.17
  405.5 2.0 shard_map.211.refs_0_
  407.5 1.5 collective-permute-start.16
  409.5 19.4 %shard_map.213 = (f32[24,1024,128]{2,1,0:T(8,128)}, f32[24,1024,128]{2,1,0:T(8,128)}) custom-call(s32[1]{0:T(128)} %bitcast.33.base, s32[16]{0:T(128)S(1)} %get-tuple-element.160.source, s32[16]{0:T(128)S(1)} %get-tuple-element.159.entry, s32[16]{0:T(128)S(1)} %mul.136.filled, f32[24,1024,128]{2,1,0:T(8,128)} %left_stat.3, f32[24,1024,128]{2,1,0:T(8,128)} %right_stat.3, ...), custom_call_target="tpu_custom_call" | custom-call | tf_op jit(solution)/shard_map/pallas_call | solution.py:212
  429.3 42.7 %collective-permute-done.17.refs_5_ = bf16[2,256,1024]{2,1,0:T(8,128)(2,1)} collective-permute-done((bf16[2,256,1024]{2,1,0:T(8,128)(2,1)S(1)}, bf16[2,256,1024]{2,1,0:T(8,128)(2,1)}, u32[]{:S(2)}, u32[]{:S(2)}) %collective-permute-start.17) | collective-permute-done | bytes 1048608 | tf_op jit(solution)/shard_map/ppermute | solution.py:442
  472.5 21.6 %collective-permute-done.20.refs_3_ = bf16[2,256,1024]{2,1,0:T(8,128)(2,1)} collective-permute-done((bf16[2,256,1024]{2,1,0:T(8,128)(2,1)S(1)}, bf16[2,256,1024]{2,1,0:T(8,128)(2,1)}, u32[]{:S(2)}, u32[]{:S(2)}) %collective-permute-start.20) | collective-permute-done | bytes 1048608 | tf_op jit(solution)/shard_map/ppermute | solution.py:442
  494.7 1.5 collective-permute-start.18
  500.1 9.3 %shard_map.214.refs_4_ = bf16[32,256,1024]{2,1,0:T(8,128)(2,1)} custom-call(s32[24]{0:T(128)S(1)} %concatenate.23.target, bf16[2,256,1024]{2,1,0:T(8,128)(2,1)} %shard_map.211.refs_0_, bf16[2,256,1024]{2,1,0:T(8,128)(2,1)S(1)} %shard_map.212.refs_1_, bf16[2,256,1024]{2,1,0:T(8,128)(2,1)S(1)} %collective-permute-done.16.refs_2_, ...), custom_call_target="tpu_custom_call" | custom-call | tf_op jit(solution)/shard_map/pallas_call | solution.py:97
  509.5 10.3 %shard_map.215 = (f32[24,1024,128]{2,1,0:T(8,128)}, f32[24,1024,128]{2,1,0:T(8,128)}) custom-call(s32[1]{0:T(128)} %bitcast.46.base, s32[8]{0:T(128)S(1)} %and_select_fusion.source, s32[8]{0:T(128)S(1)} %broadcast.203.entry, s32[8]{0:T(128)S(1)} %compare_convert_fusion.filled, ...), custom_call_target="tpu_custom_call", output_to_operand_aliasing={{0}: (8, {}), {1}: (9, {})} | custom-call | tf_op jit(solution)/shard_map/pallas_call | solution.py:212
  520.2 2.5 collective-permute-done.19.refs_1_
  524.3 2.5 collective-permute-done.28.refs_2_
  527.1 3.8 shard_map.216
  (182 shorter events, 33.5 us)
Async XLA Ops:
  14.4 4.7 copy-start.14
  18.6 19.7 %collective-permute-start = (bf16[8,256,1024]{2,1,0:T(8,128)(2,1)}, bf16[8,256,1024]{2,1,0:T(8,128)(2,1)}, u32[]{:S(2)}, u32[]{:S(2)}) collective-permute-start(bf16[8,256,1024]{2,1,0:T(8,128)(2,1)} %shard_map.197), channel_id=1, source_target_pairs={{0,1},{1,0},{2,3},{3,2},{4,5},{5,4},{6,7},{7,6},{8,9},{9,8},{10,11... | collective-permute-start | bytes 12582920 | tf_op jit(solution)/shard_map/ppermute | solution.py:446
  26.4 1.3 copy-start.8
  27.7 31.6 %all-to-all-start = ((bf16[8,4,256,128]{3,2,1,0:T(8,128)(2,1)}), bf16[8,4,256,128]{3,2,1,0:T(8,128)(2,1)S(1)}, u32[]{:S(2)}, u32[]{:S(2)}) async-start(bf16[8,4,256,128]{3,2,1,0:T(8,128)(2,1)} %bitcast.96), calls=%async_computation | async-start | bytes 4194304 | tf_op jit(solution)/shard_map/all_to_all | solution.py:542
  32.5 225.5 %all-gather.5.cloned.1.call-start = ((), (), s32[]{:S(2)}) async-start(), calls=%async_computation.7 | async-start | bytes 5242880 | tf_op jit(solution)/shard_map/all_gather | solution.py:572
  45.7 35.1 %collective-permute-start.2 = (bf16[2,2,128,1024]{3,2,1,0:T(8,128)(2,1)}, bf16[2,2,128,1024]{3,2,1,0:T(8,128)(2,1)}, u32[]{:S(2)}, u32[]{:S(2)}) collective-permute-start(bf16[2,2,128,1024]{3,2,1,0:T(8,128)(2,1)} %get-tuple-element.64), channel_id=1, source_target_pairs={{0,4},{2,6},{4,0},{6,2},{1,5},{3,7},{5,1},{7,3},{8,12},{10,14},{12... | collective-permute-start | bytes 3145736 | tf_op jit(solution)/shard_map/ppermute | solution.py:442
  59.3 3.3 copy-start
  60.2 7.1 %copy-start.25 = (bf16[2,2,128,1024]{3,2,1,0:T(8,128)(2,1)S(1)}, bf16[2,2,128,1024]{3,2,1,0:T(8,128)(2,1)}, u32[]{:S(2)}) copy-start(bf16[2,2,128,1024]{3,2,1,0:T(8,128)(2,1)} %copy-done.24) | copy-start | bytes 3145732
  60.2 20.6 %copy-start.23 = (bf16[2,2,128,1024]{3,2,1,0:T(8,128)(2,1)S(1)}, bf16[2,2,128,1024]{3,2,1,0:T(8,128)(2,1)}, u32[]{:S(2)}) copy-start(bf16[2,2,128,1024]{3,2,1,0:T(8,128)(2,1)} %copy-done.22) | copy-start | bytes 3145732
  60.2 35.3 %collective-permute-start.3 = (bf16[6,4,256,128]{3,2,1,0:T(8,128)(2,1)S(1)}, bf16[6,4,256,128]{3,2,1,0:T(8,128)(2,1)S(1)}, u32[]{:S(2)}, u32[]{:S(2)}) collective-permute-start(bf16[6,4,256,128]{3,2,1,0:T(8,128)(2,1)S(1)} %bitcast.98), channel_id=1, source_target_pairs={{8,0},{16,8},{24,16},{9,1},{17,9},{25,17},{10,2},{18,10},{26,18},{... | collective-permute-start | bytes 4718600 | tf_op jit(solution)/shard_map/ppermute | solution.py:321
  62.6 35.0 %collective-permute-start.4 = (bf16[6,4,256,128]{3,2,1,0:T(8,128)(2,1)S(1)}, bf16[6,4,256,128]{3,2,1,0:T(8,128)(2,1)S(1)}, u32[]{:S(2)}, u32[]{:S(2)}) collective-permute-start(bf16[6,4,256,128]{3,2,1,0:T(8,128)(2,1)S(1)} %bitcast.99), channel_id=1, source_target_pairs={{0,8},{8,16},{16,24},{1,9},{9,17},{17,25},{2,10},{10,18},{18,26},{... | collective-permute-start | bytes 4718600 | tf_op jit(solution)/shard_map/ppermute | solution.py:321
  67.2 56.0 %collective-permute-start.7 = (bf16[8,256,1024]{2,1,0:T(8,128)(2,1)}, bf16[8,256,1024]{2,1,0:T(8,128)(2,1)}, u32[]{:S(2)}, u32[]{:S(2)}) collective-permute-start(bf16[8,256,1024]{2,1,0:T(8,128)(2,1)} %shard_map.200), channel_id=1, source_target_pairs={{0,1},{1,0},{2,3},{3,2},{4,5},{5,4},{6,7},{7,6},{8,9},{9,8},{10,11... | collective-permute-start | bytes 12582920 | tf_op jit(solution)/shard_map/ppermute | solution.py:446
  67.3 25.6 %collective-permute-start.1 = (bf16[2,2,128,1024]{3,2,1,0:T(8,128)(2,1)S(1)}, bf16[2,2,128,1024]{3,2,1,0:T(8,128)(2,1)S(1)}, u32[]{:S(2)}, u32[]{:S(2)}) collective-permute-start(bf16[2,2,128,1024]{3,2,1,0:T(8,128)(2,1)S(1)} %copy-done.25), channel_id=1, source_target_pairs={{0,2},{2,0},{4,6},{6,4},{1,3},{3,1},{5,7},{7,5},{8,10},{10,8},{12,... | collective-permute-start | bytes 3145736 | tf_op jit(solution)/shard_map/ppermute | solution.py:442
  95.5 17.0 %copy-start.3 = (bf16[6,4,256,128]{3,2,1,0:T(8,128)(2,1)}, bf16[6,4,256,128]{3,2,1,0:T(8,128)(2,1)S(1)}, u32[]{:S(2)}) copy-start(bf16[6,4,256,128]{3,2,1,0:T(8,128)(2,1)S(1)} %collective-permute-done.3.refs_1_) | copy-start | bytes 4718596
  97.6 14.9 %copy-start.27 = (bf16[6,4,256,128]{3,2,1,0:T(8,128)(2,1)}, bf16[6,4,256,128]{3,2,1,0:T(8,128)(2,1)S(1)}, u32[]{:S(2)}) copy-start(bf16[6,4,256,128]{3,2,1,0:T(8,128)(2,1)S(1)} %collective-permute-done.4.refs_4_) | copy-start | bytes 4718596
  97.6 10.1 %collective-permute-start.5 = (bf16[2,128,1024]{2,1,0:T(8,128)(2,1)S(1)}, bf16[2,128,1024]{2,1,0:T(8,128)(2,1)S(1)}, u32[]{:S(2)}, u32[]{:S(2)}) collective-permute-start(bf16[2,128,1024]{2,1,0:T(8,128)(2,1)S(1)} %slice_bitcast_fusion.3), channel_id=1, source_target_pairs={{0,4},{2,6},{4,0},{6,2},{1,5},{3,7},{5,1},{7,3},{8,12},{10,14},{12... | collective-permute-start | bytes 1572872 | tf_op jit(solution)/shard_map/ppermute | solution.py:442
  99.1 13.2 %collective-permute-start.6 = (bf16[2,128,1024]{2,1,0:T(8,128)(2,1)S(1)}, bf16[2,128,1024]{2,1,0:T(8,128)(2,1)S(1)}, u32[]{:S(2)}, u32[]{:S(2)}) collective-permute-start(bf16[2,128,1024]{2,1,0:T(8,128)(2,1)S(1)} %slice_bitcast_fusion.2), channel_id=1, source_target_pairs={{0,2},{2,0},{4,6},{6,4},{1,3},{3,1},{5,7},{7,5},{8,10},{10,8},{12,... | collective-permute-start | bytes 1572872 | tf_op jit(solution)/shard_map/ppermute | solution.py:442
  107.9 5.7 %copy-start.15 = (bf16[32,256,128]{2,1,0:T(8,128)(2,1)S(1)}, bf16[32,256,128]{2,1,0:T(8,128)(2,1)}, u32[]{:S(2)}) copy-start(bf16[32,256,128]{2,1,0:T(8,128)(2,1)} %blocks.4) | copy-start | bytes 6291460
  118.8 53.8 %all-to-all-start.1 = ((bf16[8,4,256,128]{3,2,1,0:T(8,128)(2,1)}), bf16[8,4,256,128]{3,2,1,0:T(8,128)(2,1)S(1)}, u32[]{:S(2)}, u32[]{:S(2)}) async-start(bf16[8,4,256,128]{3,2,1,0:T(8,128)(2,1)} %bitcast.17), calls=%async_computation.1 | async-start | bytes 4194304 | tf_op jit(solution)/shard_map/all_to_all | solution.py:542
  123.2 9.5 %copy-start.4 = (bf16[6,4,256,128]{3,2,1,0:T(8,128)(2,1)S(1)}, bf16[6,4,256,128]{3,2,1,0:T(8,128)(2,1)}, u32[]{:S(2)}) copy-start(bf16[6,4,256,128]{3,2,1,0:T(8,128)(2,1)} %copy-done.3) | copy-start | bytes 4718596
  129.3 6.9 %copy-start.21 = (bf16[2,2,128,1024]{3,2,1,0:T(8,128)(2,1)}, bf16[2,2,128,1024]{3,2,1,0:T(8,128)(2,1)S(1)}, u32[]{:S(2)}) copy-start(bf16[2,2,128,1024]{3,2,1,0:T(8,128)(2,1)S(1)} %get-tuple-element.69) | copy-start | bytes 3145732
  129.3 5.8 %copy-start.28 = (bf16[6,4,256,128]{3,2,1,0:T(8,128)(2,1)S(1)}, bf16[6,4,256,128]{3,2,1,0:T(8,128)(2,1)}, u32[]{:S(2)}) copy-start(bf16[6,4,256,128]{3,2,1,0:T(8,128)(2,1)} %copy-done.27) | copy-start | bytes 4718596
  129.3 41.8 %collective-permute-start.9 = (bf16[2,2,128,1024]{3,2,1,0:T(8,128)(2,1)S(1)}, bf16[2,2,128,1024]{3,2,1,0:T(8,128)(2,1)S(1)}, u32[]{:S(2)}, u32[]{:S(2)}) collective-permute-start(bf16[2,2,128,1024]{3,2,1,0:T(8,128)(2,1)S(1)} %get-tuple-element.72), channel_id=1, source_target_pairs={{0,4},{2,6},{4,0},{6,2},{1,5},{3,7},{5,1},{7,3},{8,12},{10,14},{12... | collective-permute-start | bytes 3145736 | tf_op jit(solution)/shard_map/ppermute | solution.py:442
  131.3 10.8 %copy-start.16 = (bf16[32,256,128]{2,1,0:T(8,128)(2,1)S(1)}, bf16[32,256,128]{2,1,0:T(8,128)(2,1)}, u32[]{:S(2)}) copy-start(bf16[32,256,128]{2,1,0:T(8,128)(2,1)} %blocks.5) | copy-start | bytes 6291460
  131.3 46.2 %collective-permute-start.8 = (bf16[2,2,128,1024]{3,2,1,0:T(8,128)(2,1)}, bf16[2,2,128,1024]{3,2,1,0:T(8,128)(2,1)}, u32[]{:S(2)}, u32[]{:S(2)}) collective-permute-start(bf16[2,2,128,1024]{3,2,1,0:T(8,128)(2,1)} %get-tuple-element.70), channel_id=1, source_target_pairs={{0,2},{2,0},{4,6},{6,4},{1,3},{3,1},{5,7},{7,5},{8,10},{10,8},{12,... | collective-permute-start | bytes 3145736 | tf_op jit(solution)/shard_map/ppermute | solution.py:442
  133.9 74.1 %collective-permute-start.10 = (bf16[4,4,256,128]{3,2,1,0:T(8,128)(2,1)}, bf16[4,4,256,128]{3,2,1,0:T(8,128)(2,1)S(1)}, u32[]{:S(2)}, u32[]{:S(2)}) collective-permute-start(bf16[4,4,256,128]{3,2,1,0:T(8,128)(2,1)} %slice.161), channel_id=1, source_target_pairs={{8,0},{16,8},{24,16},{9,1},{17,9},{25,17},{10,2},{18,10},{26,18},{... | collective-permute-start | bytes 3145736 | tf_op jit(solution)/shard_map/ppermute | solution.py:321
  136.3 71.7 %collective-permute-start.11 = (bf16[4,4,256,128]{3,2,1,0:T(8,128)(2,1)}, bf16[4,4,256,128]{3,2,1,0:T(8,128)(2,1)}, u32[]{:S(2)}, u32[]{:S(2)}) collective-permute-start(bf16[4,4,256,128]{3,2,1,0:T(8,128)(2,1)} %slice.162), channel_id=1, source_target_pairs={{0,8},{8,16},{16,24},{1,9},{9,17},{17,25},{2,10},{10,18},{18,26},{... | collective-permute-start | bytes 3145736 | tf_op jit(solution)/shard_map/ppermute | solution.py:321
  173.9 53.2 %all-to-all-start.2 = ((bf16[8,4,256,128]{3,2,1,0:T(8,128)(2,1)}), bf16[8,4,256,128]{3,2,1,0:T(8,128)(2,1)S(1)}, u32[]{:S(2)}, u32[]{:S(2)}) async-start(bf16[8,4,256,128]{3,2,1,0:T(8,128)(2,1)} %bitcast.95), calls=%async_computation.2 | async-start | bytes 4194304 | tf_op jit(solution)/shard_map/all_to_all | solution.py:542
  177.5 31.1 %copy-start.29 = (bf16[2,2,128,1024]{3,2,1,0:T(8,128)(2,1)S(1)}, bf16[2,2,128,1024]{3,2,1,0:T(8,128)(2,1)}, u32[]{:S(2)}) copy-start(bf16[2,2,128,1024]{3,2,1,0:T(8,128)(2,1)} %add_convert_fusion) | copy-start | bytes 3145732
  208.0 14.1 %collective-permute-start.12 = (bf16[2,128,1024]{2,1,0:T(8,128)(2,1)S(1)}, bf16[2,128,1024]{2,1,0:T(8,128)(2,1)S(1)}, u32[]{:S(2)}, u32[]{:S(2)}) collective-permute-start(bf16[2,128,1024]{2,1,0:T(8,128)(2,1)S(1)} %slice_bitcast_fusion.1), channel_id=1, source_target_pairs={{0,4},{2,6},{4,0},{6,2},{1,5},{3,7},{5,1},{7,3},{8,12},{10,14},{12... | collective-permute-start | bytes 1572872 | tf_op jit(solution)/shard_map/ppermute | solution.py:442
  208.7 13.7 %collective-permute-start.13 = (bf16[2,128,1024]{2,1,0:T(8,128)(2,1)S(1)}, bf16[2,128,1024]{2,1,0:T(8,128)(2,1)S(1)}, u32[]{:S(2)}, u32[]{:S(2)}) collective-permute-start(bf16[2,128,1024]{2,1,0:T(8,128)(2,1)S(1)} %slice_bitcast_fusion), channel_id=1, source_target_pairs={{0,2},{2,0},{4,6},{6,4},{1,3},{3,1},{5,7},{7,5},{8,10},{10,8},{12,... | collective-permute-start | bytes 1572872 | tf_op jit(solution)/shard_map/ppermute | solution.py:442
  258.0 2.2 copy-start.1
  272.1 108.0 %all-to-all-start.4 = ((bf16[8,2,2,1024,128]{4,3,2,1,0:T(8,128)(2,1)}), bf16[8,2,2,1024,128]{4,3,2,1,0:T(8,128)(2,1)}, u32[]{:S(2)}, u32[]{:S(2)}) async-start(bf16[8,2,2,1024,128]{4,3,2,1,0:T(8,128)(2,1)} %shard_map.206), calls=%async_computation.4 | async-start | bytes 16777216 | tf_op jit(solution)/shard_map/all_to_all | solution.py:584
  277.1 8.7 %copy-start.36 = (s32[32]{0:T(128)S(1)}, s32[32]{0:T(128)}, u32[]{:S(2)}) copy-start(s32[32]{0:T(128)} %param.25) | copy-start | bytes 388
  277.2 87.9 %all-gather.7.cloned.1.call-start = ((), (), s32[]{:S(2)}) async-start(), calls=%async_computation.8 | async-start | bytes 5242880 | tf_op jit(solution)/shard_map/all_gather | solution.py:572
  278.6 7.3 %copy-start.9 = (bf16[8,4,256,128]{3,2,1,0:T(8,128)(2,1)S(1)}, bf16[8,4,256,128]{3,2,1,0:T(8,128)(2,1)}, u32[]{:S(2)}) copy-start(bf16[8,4,256,128]{3,2,1,0:T(8,128)(2,1)} %all_to_all.35) | copy-start | bytes 6291460
  278.6 27.7 %collective-permute-start.14 = (bf16[2,4,256,128]{3,2,1,0:T(8,128)(2,1)S(1)}, bf16[2,4,256,128]{3,2,1,0:T(8,128)(2,1)S(1)}, u32[]{:S(2)}, u32[]{:S(2)}) collective-permute-start(bf16[2,4,256,128]{3,2,1,0:T(8,128)(2,1)S(1)} %slice.167), channel_id=1, source_target_pairs={{8,0},{16,8},{24,16},{9,1},{17,9},{25,17},{10,2},{18,10},{26,18},{... | collective-permute-start | bytes 1572872 | tf_op jit(solution)/shard_map/ppermute | solution.py:321
  281.1 25.2 %collective-permute-start.15 = (bf16[2,4,256,128]{3,2,1,0:T(8,128)(2,1)S(1)}, bf16[2,4,256,128]{3,2,1,0:T(8,128)(2,1)S(1)}, u32[]{:S(2)}, u32[]{:S(2)}) collective-permute-start(bf16[2,4,256,128]{3,2,1,0:T(8,128)(2,1)S(1)} %slice.168), channel_id=1, source_target_pairs={{0,8},{8,16},{16,24},{1,9},{9,17},{17,25},{2,10},{10,18},{18,26},{... | collective-permute-start | bytes 1572872 | tf_op jit(solution)/shard_map/ppermute | solution.py:321
  285.9 20.5 %copy-start.5 = (bf16[6,4,256,128]{3,2,1,0:T(8,128)(2,1)S(1)}, bf16[6,4,256,128]{3,2,1,0:T(8,128)(2,1)}, u32[]{:S(2)}) copy-start(bf16[6,4,256,128]{3,2,1,0:T(8,128)(2,1)} %copy-done.3) | copy-start | bytes 4718596
  365.4 8.4 %copy-start.6 = (bf16[6,4,256,128]{3,2,1,0:T(8,128)(2,1)S(1)}, bf16[6,4,256,128]{3,2,1,0:T(8,128)(2,1)}, u32[]{:S(2)}) copy-start(bf16[6,4,256,128]{3,2,1,0:T(8,128)(2,1)} %copy-done.3) | copy-start | bytes 4718596
  365.4 8.4 %copy-start.11 = (bf16[2,4,256,128]{3,2,1,0:T(8,128)(2,1)S(1)}, bf16[2,4,256,128]{3,2,1,0:T(8,128)(2,1)}, u32[]{:S(2)}) copy-start(bf16[2,4,256,128]{3,2,1,0:T(8,128)(2,1)} %copy-done.10) | copy-start | bytes 1572868
  365.4 8.4 %copy-start.13 = (bf16[2,4,256,128]{3,2,1,0:T(8,128)(2,1)S(1)}, bf16[2,4,256,128]{3,2,1,0:T(8,128)(2,1)}, u32[]{:S(2)}) copy-start(bf16[2,4,256,128]{3,2,1,0:T(8,128)(2,1)} %copy-done.12) | copy-start | bytes 1572868
  371.7 2.1 copy-start.2
  396.3 113.1 %all-to-all-start.6 = ((bf16[8,1,2,1024,128]{4,3,2,1,0:T(8,128)(2,1)}), bf16[8,1,2,1024,128]{4,3,2,1,0:T(8,128)(2,1)}, u32[]{:S(2)}, u32[]{:S(2)}) async-start(bf16[8,1,2,1024,128]{4,3,2,1,0:T(8,128)(2,1)} %copy-done.2), calls=%async_computation.6 | async-start | bytes 8388608 | tf_op jit(solution)/shard_map/all_to_all | solution.py:618
  402.5 3.0 copy-start.18
  403.7 68.2 %collective-permute-start.17 = (bf16[2,256,1024]{2,1,0:T(8,128)(2,1)S(1)}, bf16[2,256,1024]{2,1,0:T(8,128)(2,1)}, u32[]{:S(2)}, u32[]{:S(2)}) collective-permute-start(bf16[2,256,1024]{2,1,0:T(8,128)(2,1)S(1)} %shard_map.212.refs_1_), channel_id=1, source_target_pairs={{0,4},{2,6},{4,0},{6,2},{1,5},{3,7},{5,1},{7,3},{8,12},{10,14},{12... | collective-permute-start | bytes 3145736 | tf_op jit(solution)/shard_map/ppermute | solution.py:442
  407.5 64.5 %collective-permute-start.16 = (bf16[2,256,1024]{2,1,0:T(8,128)(2,1)}, bf16[2,256,1024]{2,1,0:T(8,128)(2,1)S(1)}, u32[]{:S(2)}, u32[]{:S(2)}) collective-permute-start(bf16[2,256,1024]{2,1,0:T(8,128)(2,1)} %shard_map.211.refs_0_), channel_id=1, source_target_pairs={{0,2},{2,0},{4,6},{6,4},{1,3},{3,1},{5,7},{7,5},{8,10},{10,8},{12,... | collective-permute-start | bytes 3145736 | tf_op jit(solution)/shard_map/ppermute | solution.py:442
  409.0 85.1 %collective-permute-start.20 = (bf16[2,256,1024]{2,1,0:T(8,128)(2,1)S(1)}, bf16[2,256,1024]{2,1,0:T(8,128)(2,1)}, u32[]{:S(2)}, u32[]{:S(2)}) collective-permute-start(bf16[2,256,1024]{2,1,0:T(8,128)(2,1)S(1)} %shard_map.212.refs_1_), channel_id=1, source_target_pairs={{0,2},{2,0},{4,6},{6,4},{1,3},{3,1},{5,7},{7,5},{8,10},{10,8},{12,... | collective-permute-start | bytes 3145736 | tf_op jit(solution)/shard_map/ppermute | solution.py:442
  409.5 84.5 %collective-permute-start.23 = (bf16[2,256,1024]{2,1,0:T(8,128)(2,1)S(1)}, bf16[2,256,1024]{2,1,0:T(8,128)(2,1)S(1)}, u32[]{:S(2)}, u32[]{:S(2)}) collective-permute-start(bf16[2,256,1024]{2,1,0:T(8,128)(2,1)S(1)} %shard_map.212.refs_1_), channel_id=1, source_target_pairs={{0,1},{1,0},{2,3},{3,2},{4,5},{5,4},{6,7},{7,6},{8,9},{9,8},{10,11... | collective-permute-start | bytes 3145736 | tf_op jit(solution)/shard_map/ppermute | solution.py:446
  429.0 65.6 %collective-permute-start.21 = (bf16[2,256,1024]{2,1,0:T(8,128)(2,1)}, bf16[2,256,1024]{2,1,0:T(8,128)(2,1)}, u32[]{:S(2)}, u32[]{:S(2)}) collective-permute-start(bf16[2,256,1024]{2,1,0:T(8,128)(2,1)} %shard_map.211.refs_0_), channel_id=1, source_target_pairs={{0,4},{2,6},{4,0},{6,2},{1,5},{3,7},{5,1},{7,3},{8,12},{10,14},{12... | collective-permute-start | bytes 3145736 | tf_op jit(solution)/shard_map/ppermute | solution.py:442
  472.0 22.7 %collective-permute-start.22 = (bf16[2,256,1024]{2,1,0:T(8,128)(2,1)}, bf16[2,256,1024]{2,1,0:T(8,128)(2,1)}, u32[]{:S(2)}, u32[]{:S(2)}) collective-permute-start(bf16[2,256,1024]{2,1,0:T(8,128)(2,1)} %shard_map.211.refs_0_), channel_id=1, source_target_pairs={{0,1},{1,0},{2,3},{3,2},{4,5},{5,4},{6,7},{7,6},{8,9},{9,8},{10,11... | collective-permute-start | bytes 3145736 | tf_op jit(solution)/shard_map/ppermute | solution.py:446
  472.0 24.2 %collective-permute-start.24 = (bf16[2,256,1024]{2,1,0:T(8,128)(2,1)S(1)}, bf16[2,256,1024]{2,1,0:T(8,128)(2,1)S(1)}, u32[]{:S(2)}, u32[]{:S(2)}) collective-permute-start(bf16[2,256,1024]{2,1,0:T(8,128)(2,1)S(1)} %collective-permute-done.16.refs_2_), channel_id=1, source_target_pairs={{0,1},{1,0},{2,3},{3,2},{4,5},{5,4},{6,7},{7,6},{8,9},{9,8},{10,11... | collective-permute-start | bytes 3145736 | tf_op jit(solution)/shard_map/ppermute | solution.py:446
  494.1 5.2 collective-permute-start.27
  494.1 2.1 copy-start.30
  494.1 5.2 collective-permute-start.25
  494.6 5.5 %collective-permute-start.26 = (bf16[2,256,1024]{2,1,0:T(8,128)(2,1)}, bf16[2,256,1024]{2,1,0:T(8,128)(2,1)}, u32[]{:S(2)}, u32[]{:S(2)}) collective-permute-start(bf16[2,256,1024]{2,1,0:T(8,128)(2,1)} %collective-permute-done.21.refs_4_), channel_id=1, source_target_pairs={{0,1},{1,0},{2,3},{3,2},{4,5},{5,4},{6,7},{7,6},{8,9},{9,8},{10,11... | collective-permute-start | bytes 3145736 | tf_op jit(solution)/shard_map/ppermute | solution.py:446
  494.7 25.5 %collective-permute-start.18 = (bf16[2,256,1024]{2,1,0:T(8,128)(2,1)S(1)}, bf16[2,256,1024]{2,1,0:T(8,128)(2,1)S(1)}, u32[]{:S(2)}, u32[]{:S(2)}) collective-permute-start(bf16[2,256,1024]{2,1,0:T(8,128)(2,1)S(1)} %collective-permute-done.16.refs_2_), channel_id=1, source_target_pairs={{0,4},{2,6},{4,0},{6,2},{1,5},{3,7},{5,1},{7,3},{8,12},{10,14},{12... | collective-permute-start | bytes 3145736 | tf_op jit(solution)/shard_map/ppermute | solution.py:442
  497.2 25.5 %collective-permute-start.19 = (bf16[2,256,1024]{2,1,0:T(8,128)(2,1)}, bf16[2,256,1024]{2,1,0:T(8,128)(2,1)}, u32[]{:S(2)}, u32[]{:S(2)}) collective-permute-start(bf16[2,256,1024]{2,1,0:T(8,128)(2,1)} %collective-permute-done.17.refs_5_), channel_id=1, source_target_pairs={{0,2},{2,0},{4,6},{6,4},{1,3},{3,1},{5,7},{7,5},{8,10},{10,8},{12,... | collective-permute-start | bytes 3145736 | tf_op jit(solution)/shard_map/ppermute | solution.py:442
  509.4 14.0 %copy-start.32 = (f32[208,256]{1,0:T(8,128)S(1)}, f32[208,256]{1,0:T(8,128)}, u32[]{:S(2)}) copy-start(f32[208,256]{1,0:T(8,128)} %param.26) | copy-start | bytes 638980
  509.4 14.0 %copy-start.33 = (f32[208,256]{1,0:T(8,128)S(1)}, f32[208,256]{1,0:T(8,128)}, u32[]{:S(2)}) copy-start(f32[208,256]{1,0:T(8,128)} %param.28) | copy-start | bytes 638980
  509.5 13.9 %copy-start.34 = (f32[208,256]{1,0:T(8,128)S(1)}, f32[208,256]{1,0:T(8,128)}, u32[]{:S(2)}) copy-start(f32[208,256]{1,0:T(8,128)} %param.29) | copy-start | bytes 638980
  509.5 13.9 %copy-start.35 = (bf16[208,256]{1,0:T(8,128)(2,1)S(1)}, bf16[208,256]{1,0:T(8,128)(2,1)}, u32[]{:S(2)}) copy-start(bf16[208,256]{1,0:T(8,128)(2,1)} %param.27) | copy-start | bytes 319492
  522.7 4.1 collective-permute-start.28
  522.7 4.4 collective-permute-start.29
  (10 other events, 10.4 us)
Sparse Core Ops, SparseCore 0:
  113.7 105.5 all-gather.4
  279.6 85.4 all-gather.6
where the time goes:
time: 540 us; the launch traced here: 538 us
  waiting for transfers between devices  235 us (44%)
  Pallas kernels  136 us (25%)
  starting transfers between devices  60.5 us (11%)
  blocking collectives  47 us (9%)
  local copies, waits for them, and re-layouts  23.2 us (4%)
  other arithmetic  20.2 us (4%)
  between operations  16 us (3%)
    ppermute x14, waiting for transfers between devices, swap(): return lax.ppermute(array, 'tensor', [(t, t ^ bit) for t in range(devices)])  135 us
    all_gather x2, waiting for transfers between devices, shards(): grad_blocks = [lax.all_gather(part, 'shard', axis=0) for part in gradient]  51.1 us
    all_to_all x1, blocking collectives, deal(): lax.all_to_all(tiles.reshape(group, per, rows, cols), GROUP, split_axis=0...  30.9 us
    ppermute x3, waiting for transfers between devices, hop(): lax.ppermute(moved[0], 'shard', down)  30.7 us
    pallas_call x7, Pallas kernels, reorder(): pl.pallas_call(reorder_kernel, grid_spec=pltpu.PrefetchScalarGridSpec(num...  29.8 us
    pallas_call x2, Pallas kernels, refresh(): pl.pallas_call(stat_kernel, grid_spec=pltpu.PrefetchScalarGridSpec(num_sc...  29.7 us
    pallas_call x1, Pallas kernels, adam(): pl.pallas_call(adam_kernel, grid_spec=pltpu.PrefetchScalarGridSpec(num_sc...  20.5 us
    pallas_call x2, Pallas kernels, grams(): pl.pallas_call(gram_kernel, grid_spec=pltpu.PrefetchScalarGridSpec(num_sc...  18.2 us
  transfers between devices with their start and end apart: 37, of which 18 were waited for; matrix products, arithmetic and copies ran while one was open for 4% of the time, Pallas kernels for 22%

commit v1 on v0

--- a/solution.py
+++ b/solution.py
@@ -454,9 +454,11 @@
     return mine, other
 
 
-def first_sums(partials, sent, mine):
-    received = swap_core(sent)
-    send_a, keep_a, send_b, keep_b = add_pair(partials, received, mine)
+def pair_sums(partials, sent, mine):
+    return add_pair(partials, swap_core(sent), mine)
+
+
+def first_sums(send_a, keep_a, send_b, keep_b):
     return add(keep_a, swap(send_a, 1)), add(keep_b, swap(send_b, 2))
 
 
@@ -553,11 +555,12 @@
     if early and owner_count == 4 and rows * owner_count == size:
         spread = group // owner_count
         near = first_hop(right_dealt)
-        sums = first_sums(partials, sent[0], orders[0][0])
-        sums, near = lax.optimization_barrier((sums, near))
+        sums = first_sums(*pair_sums(partials, sent[0], orders[0][0]))
+        pairs = pair_sums(partials, sent[1], orders[1][0])
+        sums, near, pairs = lax.optimization_barrier((sums, near, pairs))
         gradient = [last_sums(*sums)]
         middle = next_hop(near, spread)
-        sums = first_sums(partials, sent[1], orders[1][0])
+        sums = first_sums(*pairs)
         sums, middle = lax.optimization_barrier((sums, middle))
         gradient.append(last_sums(*sums))
         far = next_hop(middle, spread)
@@ -565,7 +568,8 @@
         rights = [right_dealt, *downs, *ups]
     else:
         gradient = [
-            last_sums(*first_sums(partials, part, mine)) for part, (mine, _) in zip(sent, orders)
+            last_sums(*first_sums(*pair_sums(partials, part, mine)))
+            for part, (mine, _) in zip(sent, orders)
         ]
         rights = [lax.all_gather(right_dealt, "shard", axis=0)]
     gradient = [lax.optimization_barrier(part) for part in gradient]
@@ -573,17 +577,27 @@
     left_dealt = deal(reorder(left_root, order))
     weights_dealt = deal(reorder(weights, order))
     tiles = jnp.concatenate(gradient, axis=0).reshape(per, rows, group, cols)
-    tiles = deal(jnp.transpose(tiles, (2, 0, 1, 3)))
+    tiles = jnp.transpose(tiles, (2, 0, 1, 3)).reshape(group, per * rows, cols)
+    partners = jnp.arange(group, dtype=jnp.int32) ^ group_index
+    tiles = reorder(tiles, partners)
+    tiles = jnp.concatenate(
+        [tiles[:1]]
+        + [
+            lax.ppermute(tiles[k : k + 1], GROUP, [(g, g ^ k) for g in range(group)])
+            for k in range(1, group)
+        ]
+    )
+    tile_place = ((place // per) ^ group_index) * per + place % per
 
     if early:
-        grad_blocks[0], left_dealt, weights_dealt, tiles = lax.optimization_barrier(
-            (grad_blocks[0], left_dealt, weights_dealt, tiles)
+        grad_blocks[0], left_dealt, weights_dealt = lax.optimization_barrier(
+            (grad_blocks[0], left_dealt, weights_dealt)
         )
         slabs = grams(grad_blocks[0], jnp.arange(early, dtype=jnp.int32))
-        slabs, left_dealt, tiles = lax.optimization_barrier((slabs, left_dealt, tiles))
+        slabs, left_dealt, tile_place = lax.optimization_barrier((slabs, left_dealt, tile_place))
         received = lax.all_to_all(slabs, GROUP, split_axis=0, concat_axis=0, tiled=True)
     adam_m_new, adam_v_new, adam_total = adam(
-        tiles.reshape(blocks, rows, cols), place, adam_m, adam_v
+        tiles.reshape(blocks, rows, cols), tile_place, adam_m, adam_v
     )
     pieces = [precondition(left_dealt, 0, grad_blocks[0], rights)]
     if early:

time: 540 us -> 566 us (1.048)
  waiting for transfers between devices: 235 us -> 278 us
  blocking collectives: 47 us -> 11.7 us
  local copies, waits for them, and re-layouts: 23.2 us -> 31.1 us
  starting transfers between devices: 60.5 us -> 67.3 us
    ppermute x0 -> x7, waiting for transfers between devices: none -> 91.7 us  [shards(): lax.ppermute(tiles[k:k + 1], GROUP, [(g, g ^ k) for g in range(group)])]
    all_gather x2, waiting for transfers between devices: 51.1 us -> 0.01 us  [shards(): grad_blocks = [lax.all_gather(part, 'shard', axis=0) for part in gradient]]
    all_to_all x1 -> x0, blocking collectives: 30.9 us -> none  [deal(): lax.all_to_all(tiles.reshape(group, per, rows, cols), GROUP, split_axis=0...]
    ppermute x14, waiting for transfers between devices: 135 us -> 110 us  [swap(): return lax.ppermute(array, 'tensor', [(t, t ^ bit) for t in range(devices)])]
    all_to_all x3, waiting for transfers between devices: 11.6 us -> 30.5 us  [deal(): lax.all_to_all(tiles.reshape(group, per, rows, cols), GROUP, split_axis=0...]
    ppermute x3, waiting for transfers between devices: 30.7 us -> 40.3 us  [hop(): lax.ppermute(moved[0], 'shard', down)]
    ppermute x0 -> x7, starting transfers between devices: none -> 6.85 us  [shards(): lax.ppermute(tiles[k:k + 1], GROUP, [(g, g ^ k) for g in range(group)])]
    unnamed x74 -> x82, local copies, waits for them, and re-layouts: 16.1 us -> 20.5 us
  transfers between devices with their start and end apart: 37 -> 44, of which waited for: 18 -> 21; matrix products, arithmetic and copies ran while one was open for 4% -> 5% of each run, Pallas kernels for 22% -> 22%
where the time goes in v1:
time: 566 us; the launch traced here: 564 us
  waiting for transfers between devices  278 us (49%)
  Pallas kernels  137 us (24%)
  starting transfers between devices  67.3 us (12%)
  local copies, waits for them, and re-layouts  31.1 us (5%)
  other arithmetic  22.9 us (4%)
  between operations  16.1 us (3%)
  blocking collectives  11.7 us (2%)
    ppermute x14, waiting for transfers between devices, swap(): return lax.ppermute(array, 'tensor', [(t, t ^ bit) for t in range(devices)])  110 us
    ppermute x7, waiting for transfers between devices, shards(): lax.ppermute(tiles[k:k + 1], GROUP, [(g, g ^ k) for g in range(group)])  91.7 us
    ppermute x3, waiting for transfers between devices, hop(): lax.ppermute(moved[0], 'shard', down)  40.3 us
    pallas_call x8, Pallas kernels, reorder(): pl.pallas_call(reorder_kernel, grid_spec=pltpu.PrefetchScalarGridSpec(num...  31.5 us
    all_to_all x3, waiting for transfers between devices, deal(): lax.all_to_all(tiles.reshape(group, per, rows, cols), GROUP, split_axis=0...  30.5 us
    pallas_call x2, Pallas kernels, refresh(): pl.pallas_call(stat_kernel, grid_spec=pltpu.PrefetchScalarGridSpec(num_sc...  29.7 us
    unnamed x82, local copies, waits for them, and re-layouts  20.5 us
    pallas_call x1, Pallas kernels, adam(): pl.pallas_call(adam_kernel, grid_spec=pltpu.PrefetchScalarGridSpec(num_sc...  20.3 us
  transfers between devices with their start and end apart: 44, of which 21 were waited for; matrix products, arithmetic and copies ran while one was open for 5% of the time, Pallas kernels for 22%

profile of v1, /device:TPU:0, one launch (start us, length us, event | category | flops | bytes accessed | tf_op | source)
XLA Modules:
  0.0 564.0 jit_solution(3883574190467960546)
XLA Ops:
  10.5 1.9 fusion.19
  12.8 1.6 copy-done.14
  14.4 7.3 %shard_map.199 = bf16[32,256,128]{2,1,0:T(8,128)(2,1)S(1)} custom-call(s32[32]{0:T(128)S(1)} %select_reduce_fusion.order, bf16[32,256,128]{2,1,0:T(8,128)(2,1)S(1)} %copy-done.14), custom_call_target="tpu_custom_call" | custom-call | tf_op jit(solution)/shard_map/pallas_call | solution.py:72
  23.0 5.2 all-to-all-start
  29.8 4.1 shard_map.197
  34.6 2.9 shard_map.200
  37.5 2.0 copy-done.8
  39.5 15.3 %all-to-all-done.refs_0_ = bf16[8,4,256,128]{3,2,1,0:T(8,128)(2,1)S(1)} async-done(((bf16[8,4,256,128]{3,2,1,0:T(8,128)(2,1)}), bf16[8,4,256,128]{3,2,1,0:T(8,128)(2,1)S(1)}, u32[]{:S(2)}, u32[]{:S(2)}) %all-to-all-start) | async-done | bytes 2097184 | tf_op jit(solution)/shard_map/all_to_all | solution.py:544
  56.2 5.5 shard_map.198
  63.3 1.9 shard_map.201
  66.5 1.9 shard_map.202
  68.4 4.6 collective-permute-start.4
  73.9 14.7 %collective-permute-done.2 = bf16[2,2,128,1024]{3,2,1,0:T(8,128)(2,1)} collective-permute-done((bf16[2,2,128,1024]{3,2,1,0:T(8,128)(2,1)}, bf16[2,2,128,1024]{3,2,1,0:T(8,128)(2,1)}, u32[]{:S(2)}, u32[]{:S(2)}) %collective-permute-start.2) | collective-permute-done | bytes 1048608 | tf_op jit(solution)/shard_map/ppermute | solution.py:442
  88.6 2.0 add_convert_fusion.2
  90.6 7.6 %collective-permute-done.1 = bf16[2,2,128,1024]{3,2,1,0:T(8,128)(2,1)} collective-permute-done((bf16[2,2,128,1024]{3,2,1,0:T(8,128)(2,1)}, bf16[2,2,128,1024]{3,2,1,0:T(8,128)(2,1)}, u32[]{:S(2)}, u32[]{:S(2)}) %collective-permute-start.1) | collective-permute-done | bytes 1048608 | tf_op jit(solution)/shard_map/ppermute | solution.py:442
  98.2 1.6 add_convert_fusion.3
  99.8 5.5 shard_map.203
  105.4 1.7 collective-permute-done.4.refs_4_
  107.1 1.5 collective-permute-start.6
  109.2 10.8 %collective-permute-done.6 = bf16[2,128,1024]{2,1,0:T(8,128)(2,1)S(1)} collective-permute-done((bf16[2,128,1024]{2,1,0:T(8,128)(2,1)S(1)}, bf16[2,128,1024]{2,1,0:T(8,128)(2,1)S(1)}, u32[]{:S(2)}, u32[]{:S(2)}) %collective-permute-start.6) | collective-permute-done | bytes 524320 | tf_op jit(solution)/shard_map/ppermute | solution.py:442
  122.7 5.2 shard_map.204
  127.9 4.5 all-to-all-start.1
  132.4 1.9 collective-permute-start.9
  134.3 1.5 collective-permute-start.8
  135.8 7.3 %shard_map.205 = bf16[32,256,128]{2,1,0:T(8,128)(2,1)S(1)} custom-call(s32[32]{0:T(128)S(1)} %select_reduce_fusion.order, bf16[32,256,128]{2,1,0:T(8,128)(2,1)S(1)} %copy-done.16), custom_call_target="tpu_custom_call" | custom-call | tf_op jit(solution)/shard_map/pallas_call | solution.py:72
  144.4 15.2 %all-to-all-done.1.left = bf16[8,4,256,128]{3,2,1,0:T(8,128)(2,1)} async-done(((bf16[8,4,256,128]{3,2,1,0:T(8,128)(2,1)}), bf16[8,4,256,128]{3,2,1,0:T(8,128)(2,1)}, u32[]{:S(2)}, u32[]{:S(2)}) %all-to-all-start.1) | async-done | bytes 2097184 | tf_op jit(solution)/shard_map/all_to_all | solution.py:544
  159.6 3.6 all-to-all-start.2
  167.2 5.3 collective-permute-start.11
  172.5 8.5 %collective-permute-done.9 = bf16[2,2,128,1024]{3,2,1,0:T(8,128)(2,1)} collective-permute-done((bf16[2,2,128,1024]{3,2,1,0:T(8,128)(2,1)}, bf16[2,2,128,1024]{3,2,1,0:T(8,128)(2,1)}, u32[]{:S(2)}, u32[]{:S(2)}) %collective-permute-start.9) | collective-permute-done | bytes 1048608 | tf_op jit(solution)/shard_map/ppermute | solution.py:442
  181.0 1.6 add_convert_fusion
  182.7 2.0 add_convert_fusion.1
  184.7 40.3 %collective-permute-done.10.refs_2_ = bf16[4,4,256,128]{3,2,1,0:T(8,128)(2,1)S(1)} collective-permute-done((bf16[4,4,256,128]{3,2,1,0:T(8,128)(2,1)S(1)}, bf16[4,4,256,128]{3,2,1,0:T(8,128)(2,1)S(1)}, u32[]{:S(2)}, u32[]{:S(2)}) %collective-permute-start.10) | collective-permute-done | bytes 1048608 | tf_op jit(solution)/shard_map/ppermute | solution.py:321
  225.9 1.5 collective-permute-start.12
  229.8 2.2 copy-done.1
  231.9 12.0 %shard_map.206 = bf16[8,2,2,1024,128]{4,3,2,1,0:T(8,128)(2,1)} custom-call(s32[2]{0:T(128)S(1)} %iota.54.chosen, bf16[4,2,256,1024]{3,2,1,0:T(8,128)(2,1)S(1)} %bitcast.95), custom_call_target="tpu_custom_call" | custom-call | tf_op jit(solution)/shard_map/pallas_call | solution.py:177
  243.9 5.0 all-to-all-start.3
  252.9 2.1 copy_bitcast_fusion
  257.7 1.7 collective-permute-start.15
  260.2 1.6 collective-permute-start.21
  262.8 5.2 collective-permute-start.22
  268.0 1.8 collective-permute-start.17
  270.8 77.4 %collective-permute-done.15 = bf16[1,1024,128]{2,1,0:T(8,128)(2,1)} collective-permute-done((bf16[1,1024,128]{2,1,0:T(8,128)(2,1)}, bf16[1,1024,128]{2,1,0:T(8,128)(2,1)}, u32[]{:S(2)}, u32[]{:S(2)}) %collective-permute-start.15) | collective-permute-done | bytes 262176 | tf_op jit(solution)/shard_map/ppermute | solution.py:586
  349.4 3.4 collective-permute-done.16
  356.8 6.1 %collective-permute-done.19 = bf16[1,1024,128]{2,1,0:T(8,128)(2,1)S(1)} collective-permute-done((bf16[1,1024,128]{2,1,0:T(8,128)(2,1)S(1)}, bf16[1,1024,128]{2,1,0:T(8,128)(2,1)S(1)}, u32[]{:S(2)}, u32[]{:S(2)}) %collective-permute-start.19) | collective-permute-done | bytes 262176 | tf_op jit(solution)/shard_map/ppermute | solution.py:586
  362.9 4.8 collective-permute-done.20
  367.7 20.3 %shard_map.208 = (f32[32,256,128]{2,1,0:T(8,128)}, f32[32,256,128]{2,1,0:T(8,128)}, f32[32,1,128]{2,1,0:T(1,128)S(1)}) custom-call(s32[32]{0:T(128)S(1)} %get-tuple-element.87.place, bf16[32,256,128]{2,1,0:T(8,128)(2,1)S(1)} %bitcast.99, f32[32,256,128]{2,1,0:T(8,128)} %moment.1, f32[32,256,128]{2,1,0:T(8,128)} %second.1), custom_call_target="tpu_custom_call" | custom-call | tf_op jit(solution)/shard_map/pallas_call | solution.py:125
  388.0 5.1 shard_map.209
  396.1 6.3 %shard_map.210 = bf16[8,1,2,1024,128]{4,3,2,1,0:T(8,128)(2,1)S(1)} custom-call(s32[1]{0:T(128)} %bitcast.20.chosen, bf16[4,2,256,1024]{3,2,1,0:T(8,128)(2,1)} %bitcast.110), custom_call_target="tpu_custom_call" | custom-call | tf_op jit(solution)/shard_map/pallas_call | solution.py:177
  402.4 2.0 copy-done.2
  404.5 5.1 shard_map.211
  410.9 11.7 %all_to_all.30 = f32[32,8,128]{2,1,0:T(8,128)S(1)} all-to-all(f32[32,8,128]{2,1,0:T(8,128)S(1)} %broadcast_in_dim.47), channel_id=1, replica_groups=mesh['shard'=4,'tensor'=4,'section'=2] {'shard','tensor','section'}, dimensions={0} | all-to-all | bytes 262144 | tf_op jit(solution)/shard_map/all_to_all | solution.py:624
  422.6 4.8 all-to-all-start.5
  430.1 1.7 collective-permute-start.24
  431.8 2.0 shard_map.212.refs_0_
  433.8 1.5 collective-permute-start.23
  435.8 19.4 %shard_map.214 = (f32[24,1024,128]{2,1,0:T(8,128)}, f32[24,1024,128]{2,1,0:T(8,128)}) custom-call(s32[1]{0:T(128)} %bitcast.34.base, s32[16]{0:T(128)S(1)} %get-tuple-element.176.source, s32[16]{0:T(128)S(1)} %get-tuple-element.175.entry, s32[16]{0:T(128)S(1)} %mul.139.filled, f32[24,1024,128]{2,1,0:T(8,128)} %left_stat.3, f32[24,1024,128]{2,1,0:T(8,128)} %right_stat.3, ...), custom_call_target="tpu_custom_call" | custom-call | tf_op jit(solution)/shard_map/pallas_call | solution.py:212
  455.6 42.7 %collective-permute-done.24.refs_5_ = bf16[2,256,1024]{2,1,0:T(8,128)(2,1)} collective-permute-done((bf16[2,256,1024]{2,1,0:T(8,128)(2,1)S(1)}, bf16[2,256,1024]{2,1,0:T(8,128)(2,1)}, u32[]{:S(2)}, u32[]{:S(2)}) %collective-permute-start.24) | collective-permute-done | bytes 1048608 | tf_op jit(solution)/shard_map/ppermute | solution.py:442
  498.8 21.6 %collective-permute-done.27.refs_3_ = bf16[2,256,1024]{2,1,0:T(8,128)(2,1)} collective-permute-done((bf16[2,256,1024]{2,1,0:T(8,128)(2,1)S(1)}, bf16[2,256,1024]{2,1,0:T(8,128)(2,1)}, u32[]{:S(2)}, u32[]{:S(2)}) %collective-permute-start.27) | collective-permute-done | bytes 1048608 | tf_op jit(solution)/shard_map/ppermute | solution.py:442
  520.9 1.5 collective-permute-start.25
  526.3 9.3 %shard_map.215.refs_4_ = bf16[32,256,1024]{2,1,0:T(8,128)(2,1)} custom-call(s32[24]{0:T(128)S(1)} %concatenate.27.target, bf16[2,256,1024]{2,1,0:T(8,128)(2,1)} %shard_map.212.refs_0_, bf16[2,256,1024]{2,1,0:T(8,128)(2,1)S(1)} %shard_map.213.refs_1_, bf16[2,256,1024]{2,1,0:T(8,128)(2,1)S(1)} %collective-permute-done.23.refs_2_, ...), custom_call_target="tpu_custom_call" | custom-call | tf_op jit(solution)/shard_map/pallas_call | solution.py:97
  535.8 10.3 %shard_map.216 = (f32[24,1024,128]{2,1,0:T(8,128)}, f32[24,1024,128]{2,1,0:T(8,128)}) custom-call(s32[1]{0:T(128)} %bitcast.47.base, s32[8]{0:T(128)S(1)} %and_select_fusion.source, s32[8]{0:T(128)S(1)} %broadcast.212.entry, s32[8]{0:T(128)S(1)} %compare_convert_fusion.filled, ...), custom_call_target="tpu_custom_call", output_to_operand_aliasing={{0}: (8, {}), {1}: (9, {})} | custom-call | tf_op jit(solution)/shard_map/pallas_call | solution.py:212
  546.5 2.5 collective-permute-done.26.refs_1_
  550.6 2.5 collective-permute-done.35.refs_2_
  553.4 3.8 shard_map.217
  (207 shorter events, 52.7 us)
Async XLA Ops:
  23.0 31.8 %all-to-all-start = ((bf16[8,4,256,128]{3,2,1,0:T(8,128)(2,1)}), bf16[8,4,256,128]{3,2,1,0:T(8,128)(2,1)S(1)}, u32[]{:S(2)}, u32[]{:S(2)}) async-start(bf16[8,4,256,128]{3,2,1,0:T(8,128)(2,1)} %bitcast.97), calls=%async_computation | async-start | bytes 4194304 | tf_op jit(solution)/shard_map/all_to_all | solution.py:544
  28.2 201.6 %all-gather.5.cloned.1.call-start = ((), (), s32[]{:S(2)}) async-start(), calls=%async_computation.6 | async-start | bytes 5242880 | tf_op jit(solution)/shard_map/all_gather | solution.py:576
  33.9 22.3 %collective-permute-start = (bf16[8,256,1024]{2,1,0:T(8,128)(2,1)}, bf16[8,256,1024]{2,1,0:T(8,128)(2,1)}, u32[]{:S(2)}, u32[]{:S(2)}) collective-permute-start(bf16[8,256,1024]{2,1,0:T(8,128)(2,1)} %shard_map.197), channel_id=1, source_target_pairs={{0,1},{1,0},{2,3},{3,2},{4,5},{5,4},{6,7},{7,6},{8,9},{9,8},{10,11... | collective-permute-start | bytes 12582920 | tf_op jit(solution)/shard_map/ppermute | solution.py:446
  54.8 11.7 %copy-start = (bf16[8,4,256,128]{3,2,1,0:T(8,128)(2,1)}, bf16[8,4,256,128]{3,2,1,0:T(8,128)(2,1)S(1)}, u32[]{:S(2)}) copy-start(bf16[8,4,256,128]{3,2,1,0:T(8,128)(2,1)S(1)} %all-to-all-done.refs_0_) | copy-start | bytes 6291460
  54.8 45.0 %collective-permute-start.5 = (bf16[8,256,1024]{2,1,0:T(8,128)(2,1)}, bf16[8,256,1024]{2,1,0:T(8,128)(2,1)}, u32[]{:S(2)}, u32[]{:S(2)}) collective-permute-start(bf16[8,256,1024]{2,1,0:T(8,128)(2,1)} %copy-done.8), channel_id=1, source_target_pairs={{0,1},{1,0},{2,3},{3,2},{4,5},{5,4},{6,7},{7,6},{8,9},{9,8},{10,11... | collective-permute-start | bytes 12582920 | tf_op jit(solution)/shard_map/ppermute | solution.py:446
  62.7 25.9 %collective-permute-start.2 = (bf16[2,2,128,1024]{3,2,1,0:T(8,128)(2,1)}, bf16[2,2,128,1024]{3,2,1,0:T(8,128)(2,1)}, u32[]{:S(2)}, u32[]{:S(2)}) collective-permute-start(bf16[2,2,128,1024]{3,2,1,0:T(8,128)(2,1)} %get-tuple-element.67), channel_id=1, source_target_pairs={{0,4},{2,6},{4,0},{6,2},{1,5},{3,7},{5,1},{7,3},{8,12},{10,14},{12... | collective-permute-start | bytes 3145736 | tf_op jit(solution)/shard_map/ppermute | solution.py:442
  65.2 40.2 %collective-permute-start.3 = (bf16[6,4,256,128]{3,2,1,0:T(8,128)(2,1)}, bf16[6,4,256,128]{3,2,1,0:T(8,128)(2,1)}, u32[]{:S(2)}, u32[]{:S(2)}) collective-permute-start(bf16[6,4,256,128]{3,2,1,0:T(8,128)(2,1)} %bitcast.10), channel_id=1, source_target_pairs={{8,0},{16,8},{24,16},{9,1},{17,9},{25,17},{10,2},{18,10},{26,18},{... | collective-permute-start | bytes 4718600 | tf_op jit(solution)/shard_map/ppermute | solution.py:321
  68.4 38.6 %collective-permute-start.4 = (bf16[6,4,256,128]{3,2,1,0:T(8,128)(2,1)}, bf16[6,4,256,128]{3,2,1,0:T(8,128)(2,1)S(1)}, u32[]{:S(2)}, u32[]{:S(2)}) collective-permute-start(bf16[6,4,256,128]{3,2,1,0:T(8,128)(2,1)} %bitcast.11), channel_id=1, source_target_pairs={{0,8},{8,16},{16,24},{1,9},{9,17},{17,25},{2,10},{10,18},{18,26},{... | collective-permute-start | bytes 4718600 | tf_op jit(solution)/shard_map/ppermute | solution.py:321
  73.1 25.1 %collective-permute-start.1 = (bf16[2,2,128,1024]{3,2,1,0:T(8,128)(2,1)}, bf16[2,2,128,1024]{3,2,1,0:T(8,128)(2,1)}, u32[]{:S(2)}, u32[]{:S(2)}) collective-permute-start(bf16[2,2,128,1024]{3,2,1,0:T(8,128)(2,1)} %get-tuple-element.65), channel_id=1, source_target_pairs={{0,2},{2,0},{4,6},{6,4},{1,3},{3,1},{5,7},{7,5},{8,10},{10,8},{12,... | collective-permute-start | bytes 3145736 | tf_op jit(solution)/shard_map/ppermute | solution.py:442
  105.4 16.2 %copy-start.17 = (bf16[2,2,128,1024]{3,2,1,0:T(8,128)(2,1)}, bf16[2,2,128,1024]{3,2,1,0:T(8,128)(2,1)S(1)}, u32[]{:S(2)}) copy-start(bf16[2,2,128,1024]{3,2,1,0:T(8,128)(2,1)S(1)} %get-tuple-element.79) | copy-start | bytes 3145732
  105.4 16.2 %copy-start.19 = (bf16[2,2,128,1024]{3,2,1,0:T(8,128)(2,1)}, bf16[2,2,128,1024]{3,2,1,0:T(8,128)(2,1)S(1)}, u32[]{:S(2)}) copy-start(bf16[2,2,128,1024]{3,2,1,0:T(8,128)(2,1)S(1)} %get-tuple-element.81) | copy-start | bytes 3145732
  107.0 13.0 %copy-start.26 = (bf16[6,4,256,128]{3,2,1,0:T(8,128)(2,1)}, bf16[6,4,256,128]{3,2,1,0:T(8,128)(2,1)S(1)}, u32[]{:S(2)}) copy-start(bf16[6,4,256,128]{3,2,1,0:T(8,128)(2,1)S(1)} %collective-permute-done.4.refs_4_) | copy-start | bytes 4718596
  107.1 13.0 %collective-permute-start.6 = (bf16[2,128,1024]{2,1,0:T(8,128)(2,1)S(1)}, bf16[2,128,1024]{2,1,0:T(8,128)(2,1)S(1)}, u32[]{:S(2)}, u32[]{:S(2)}) collective-permute-start(bf16[2,128,1024]{2,1,0:T(8,128)(2,1)S(1)} %slice_bitcast_fusion.3), channel_id=1, source_target_pairs={{0,4},{2,6},{4,0},{6,2},{1,5},{3,7},{5,1},{7,3},{8,12},{10,14},{12... | collective-permute-start | bytes 1572872 | tf_op jit(solution)/shard_map/ppermute | solution.py:442
  108.7 12.7 %collective-permute-start.7 = (bf16[2,128,1024]{2,1,0:T(8,128)(2,1)S(1)}, bf16[2,128,1024]{2,1,0:T(8,128)(2,1)S(1)}, u32[]{:S(2)}, u32[]{:S(2)}) collective-permute-start(bf16[2,128,1024]{2,1,0:T(8,128)(2,1)S(1)} %slice_bitcast_fusion.2), channel_id=1, source_target_pairs={{0,2},{2,0},{4,6},{6,4},{1,3},{3,1},{5,7},{7,5},{8,10},{10,8},{12,... | collective-permute-start | bytes 1572872 | tf_op jit(solution)/shard_map/ppermute | solution.py:442
  127.9 7.9 %copy-start.16 = (bf16[32,256,128]{2,1,0:T(8,128)(2,1)S(1)}, bf16[32,256,128]{2,1,0:T(8,128)(2,1)}, u32[]{:S(2)}) copy-start(bf16[32,256,128]{2,1,0:T(8,128)(2,1)} %blocks.5) | copy-start | bytes 6291460
  127.9 31.7 %all-to-all-start.1 = ((bf16[8,4,256,128]{3,2,1,0:T(8,128)(2,1)}), bf16[8,4,256,128]{3,2,1,0:T(8,128)(2,1)}, u32[]{:S(2)}, u32[]{:S(2)}) async-start(bf16[8,4,256,128]{3,2,1,0:T(8,128)(2,1)} %bitcast.18), calls=%async_computation.1 | async-start | bytes 4194304 | tf_op jit(solution)/shard_map/all_to_all | solution.py:544
  132.4 48.6 %collective-permute-start.9 = (bf16[2,2,128,1024]{3,2,1,0:T(8,128)(2,1)}, bf16[2,2,128,1024]{3,2,1,0:T(8,128)(2,1)}, u32[]{:S(2)}, u32[]{:S(2)}) collective-permute-start(bf16[2,2,128,1024]{3,2,1,0:T(8,128)(2,1)} %get-tuple-element.82), channel_id=1, source_target_pairs={{0,4},{2,6},{4,0},{6,2},{1,5},{3,7},{5,1},{7,3},{8,12},{10,14},{12... | collective-permute-start | bytes 3145736 | tf_op jit(solution)/shard_map/ppermute | solution.py:442
  134.3 48.4 %collective-permute-start.8 = (bf16[2,2,128,1024]{3,2,1,0:T(8,128)(2,1)}, bf16[2,2,128,1024]{3,2,1,0:T(8,128)(2,1)}, u32[]{:S(2)}, u32[]{:S(2)}) collective-permute-start(bf16[2,2,128,1024]{3,2,1,0:T(8,128)(2,1)} %get-tuple-element.80), channel_id=1, source_target_pairs={{0,2},{2,0},{4,6},{6,4},{1,3},{3,1},{5,7},{7,5},{8,10},{10,8},{12,... | collective-permute-start | bytes 3145736 | tf_op jit(solution)/shard_map/ppermute | solution.py:442
  159.6 70.2 %all-to-all-start.2 = ((bf16[8,4,256,128]{3,2,1,0:T(8,128)(2,1)}), bf16[8,4,256,128]{3,2,1,0:T(8,128)(2,1)S(1)}, u32[]{:S(2)}, u32[]{:S(2)}) async-start(bf16[8,4,256,128]{3,2,1,0:T(8,128)(2,1)} %bitcast.96), calls=%async_computation.2 | async-start | bytes 4194304 | tf_op jit(solution)/shard_map/all_to_all | solution.py:544
  163.2 17.9 %copy-start.20 = (bf16[2,2,128,1024]{3,2,1,0:T(8,128)(2,1)S(1)}, bf16[2,2,128,1024]{3,2,1,0:T(8,128)(2,1)}, u32[]{:S(2)}) copy-start(bf16[2,2,128,1024]{3,2,1,0:T(8,128)(2,1)} %copy-done.19) | copy-start | bytes 3145732
  164.6 60.4 %collective-permute-start.10 = (bf16[4,4,256,128]{3,2,1,0:T(8,128)(2,1)S(1)}, bf16[4,4,256,128]{3,2,1,0:T(8,128)(2,1)S(1)}, u32[]{:S(2)}, u32[]{:S(2)}) collective-permute-start(bf16[4,4,256,128]{3,2,1,0:T(8,128)(2,1)S(1)} %slice.185), channel_id=1, source_target_pairs={{8,0},{16,8},{24,16},{9,1},{17,9},{25,17},{10,2},{18,10},{26,18},{... | collective-permute-start | bytes 3145736 | tf_op jit(solution)/shard_map/ppermute | solution.py:321
  167.2 15.5 %copy-start.18 = (bf16[2,2,128,1024]{3,2,1,0:T(8,128)(2,1)S(1)}, bf16[2,2,128,1024]{3,2,1,0:T(8,128)(2,1)}, u32[]{:S(2)}) copy-start(bf16[2,2,128,1024]{3,2,1,0:T(8,128)(2,1)} %copy-done.17) | copy-start | bytes 3145732
  167.2 57.8 %collective-permute-start.11 = (bf16[4,4,256,128]{3,2,1,0:T(8,128)(2,1)S(1)}, bf16[4,4,256,128]{3,2,1,0:T(8,128)(2,1)S(1)}, u32[]{:S(2)}, u32[]{:S(2)}) collective-permute-start(bf16[4,4,256,128]{3,2,1,0:T(8,128)(2,1)S(1)} %slice.186), channel_id=1, source_target_pairs={{0,8},{8,16},{16,24},{1,9},{9,17},{17,25},{2,10},{10,18},{18,26},{... | collective-permute-start | bytes 3145736 | tf_op jit(solution)/shard_map/ppermute | solution.py:321
  182.7 44.8 %copy-start.27 = (bf16[2,2,128,1024]{3,2,1,0:T(8,128)(2,1)}, bf16[2,2,128,1024]{3,2,1,0:T(8,128)(2,1)S(1)}, u32[]{:S(2)}) copy-start(bf16[2,2,128,1024]{3,2,1,0:T(8,128)(2,1)S(1)} %add_convert_fusion) | copy-start | bytes 3145732
  184.7 43.6 %copy-start.28 = (bf16[2,2,128,1024]{3,2,1,0:T(8,128)(2,1)}, bf16[2,2,128,1024]{3,2,1,0:T(8,128)(2,1)S(1)}, u32[]{:S(2)}) copy-start(bf16[2,2,128,1024]{3,2,1,0:T(8,128)(2,1)S(1)} %add_convert_fusion.1) | copy-start | bytes 3145732
  225.9 23.0 %collective-permute-start.12 = (bf16[2,128,1024]{2,1,0:T(8,128)(2,1)}, bf16[2,128,1024]{2,1,0:T(8,128)(2,1)}, u32[]{:S(2)}, u32[]{:S(2)}) collective-permute-start(bf16[2,128,1024]{2,1,0:T(8,128)(2,1)} %slice_bitcast_fusion.1), channel_id=1, source_target_pairs={{0,4},{2,6},{4,0},{6,2},{1,5},{3,7},{5,1},{7,3},{8,12},{10,14},{12... | collective-permute-start | bytes 1572872 | tf_op jit(solution)/shard_map/ppermute | solution.py:442
  228.3 22.1 %collective-permute-start.13 = (bf16[2,128,1024]{2,1,0:T(8,128)(2,1)}, bf16[2,128,1024]{2,1,0:T(8,128)(2,1)}, u32[]{:S(2)}, u32[]{:S(2)}) collective-permute-start(bf16[2,128,1024]{2,1,0:T(8,128)(2,1)} %slice_bitcast_fusion), channel_id=1, source_target_pairs={{0,2},{2,0},{4,6},{6,4},{1,3},{3,1},{5,7},{7,5},{8,10},{10,8},{12,... | collective-permute-start | bytes 1572872 | tf_op jit(solution)/shard_map/ppermute | solution.py:442
  243.9 167.0 %all-to-all-start.3 = ((bf16[8,2,2,1024,128]{4,3,2,1,0:T(8,128)(2,1)}), bf16[8,2,2,1024,128]{4,3,2,1,0:T(8,128)(2,1)}, u32[]{:S(2)}, u32[]{:S(2)}) async-start(bf16[8,2,2,1024,128]{4,3,2,1,0:T(8,128)(2,1)} %shard_map.206), calls=%async_computation.3 | async-start | bytes 16777216 | tf_op jit(solution)/shard_map/all_to_all | solution.py:598
  248.9 146.9 %all-gather.7.cloned.1.call-start = ((), (), s32[]{:S(2)}) async-start(), calls=%async_computation.7 | async-start | bytes 5242880 | tf_op jit(solution)/shard_map/all_gather | solution.py:576
  257.3 10.7 %collective-permute-start.14 = (bf16[1,1024,128]{2,1,0:T(8,128)(2,1)}, bf16[1,1024,128]{2,1,0:T(8,128)(2,1)}, u32[]{:S(2)}, u32[]{:S(2)}) collective-permute-start(bf16[1,1024,128]{2,1,0:T(8,128)(2,1)} %get-tuple-element.139), channel_id=1, source_target_pairs={{0,1},{1,0},{2,3},{3,2},{4,5},{5,4},{6,7},{7,6},{8,9},{9,8},{10,11... | collective-permute-start | bytes 786440 | tf_op jit(solution)/shard_map/ppermute | solution.py:586
  257.7 90.5 %collective-permute-start.15 = (bf16[1,1024,128]{2,1,0:T(8,128)(2,1)}, bf16[1,1024,128]{2,1,0:T(8,128)(2,1)}, u32[]{:S(2)}, u32[]{:S(2)}) collective-permute-start(bf16[1,1024,128]{2,1,0:T(8,128)(2,1)} %get-tuple-element.138), channel_id=1, source_target_pairs={{0,2},{1,3},{2,0},{3,1},{4,6},{5,7},{6,4},{7,5},{8,10},{9,11},{10,... | collective-permute-start | bytes 786440 | tf_op jit(solution)/shard_map/ppermute | solution.py:586
  259.4 93.4 %collective-permute-start.16 = (bf16[1,1024,128]{2,1,0:T(8,128)(2,1)}, bf16[1,1024,128]{2,1,0:T(8,128)(2,1)}, u32[]{:S(2)}, u32[]{:S(2)}) collective-permute-start(bf16[1,1024,128]{2,1,0:T(8,128)(2,1)} %get-tuple-element.137), channel_id=1, source_target_pairs={{0,3},{1,2},{2,1},{3,0},{4,7},{5,6},{6,5},{7,4},{8,11},{9,10},{10,... | collective-permute-start | bytes 786440 | tf_op jit(solution)/shard_map/ppermute | solution.py:586
  260.1 9.7 %copy-start.9 = (bf16[8,1024,128]{2,1,0:T(8,128)(2,1)S(1)}, bf16[8,1024,128]{2,1,0:T(8,128)(2,1)}, u32[]{:S(2)}) copy-start(bf16[8,1024,128]{2,1,0:T(8,128)(2,1)} %get-tuple-element.140) | copy-start | bytes 6291460
  260.1 88.1 %copy-start.32 = (bf16[1,1024,128]{2,1,0:T(8,128)(2,1)S(1)}, bf16[1,1024,128]{2,1,0:T(8,128)(2,1)}, u32[]{:S(2)}) copy-start(bf16[1,1024,128]{2,1,0:T(8,128)(2,1)} %get-tuple-element.135) | copy-start | bytes 786436
  260.1 92.7 %copy-start.31 = (bf16[1,1024,128]{2,1,0:T(8,128)(2,1)S(1)}, bf16[1,1024,128]{2,1,0:T(8,128)(2,1)}, u32[]{:S(2)}) copy-start(bf16[1,1024,128]{2,1,0:T(8,128)(2,1)} %get-tuple-element.134) | copy-start | bytes 786436
  260.2 127.8 %collective-permute-start.21 = (bf16[2,4,256,128]{3,2,1,0:T(8,128)(2,1)S(1)}, bf16[2,4,256,128]{3,2,1,0:T(8,128)(2,1)S(1)}, u32[]{:S(2)}, u32[]{:S(2)}) collective-permute-start(bf16[2,4,256,128]{3,2,1,0:T(8,128)(2,1)S(1)} %slice.199), channel_id=1, source_target_pairs={{8,0},{16,8},{24,16},{9,1},{17,9},{25,17},{10,2},{18,10},{26,18},{... | collective-permute-start | bytes 1572872 | tf_op jit(solution)/shard_map/ppermute | solution.py:321
  262.8 125.2 %collective-permute-start.22 = (bf16[2,4,256,128]{3,2,1,0:T(8,128)(2,1)S(1)}, bf16[2,4,256,128]{3,2,1,0:T(8,128)(2,1)S(1)}, u32[]{:S(2)}, u32[]{:S(2)}) collective-permute-start(bf16[2,4,256,128]{3,2,1,0:T(8,128)(2,1)S(1)} %slice.200), channel_id=1, source_target_pairs={{0,8},{8,16},{16,24},{1,9},{9,17},{17,25},{2,10},{10,18},{18,26},{... | collective-permute-start | bytes 1572872 | tf_op jit(solution)/shard_map/ppermute | solution.py:321
  268.0 87.3 %collective-permute-start.17 = (bf16[1,1024,128]{2,1,0:T(8,128)(2,1)}, bf16[1,1024,128]{2,1,0:T(8,128)(2,1)S(1)}, u32[]{:S(2)}, u32[]{:S(2)}) collective-permute-start(bf16[1,1024,128]{2,1,0:T(8,128)(2,1)} %get-tuple-element.136), channel_id=1, source_target_pairs={{0,4},{1,5},{2,6},{3,7},{4,0},{5,1},{6,2},{7,3},{8,12},{9,13},{10,... | collective-permute-start | bytes 786440 | tf_op jit(solution)/shard_map/ppermute | solution.py:586
  348.2 8.6 %collective-permute-start.18 = (bf16[1,1024,128]{2,1,0:T(8,128)(2,1)S(1)}, bf16[1,1024,128]{2,1,0:T(8,128)(2,1)S(1)}, u32[]{:S(2)}, u32[]{:S(2)}) collective-permute-start(bf16[1,1024,128]{2,1,0:T(8,128)(2,1)S(1)} %copy-done.32), channel_id=1, source_target_pairs={{0,5},{1,4},{2,7},{3,6},{4,1},{5,0},{6,3},{7,2},{8,13},{9,12},{10,... | collective-permute-start | bytes 786440 | tf_op jit(solution)/shard_map/ppermute | solution.py:586
  352.9 10.0 %collective-permute-start.19 = (bf16[1,1024,128]{2,1,0:T(8,128)(2,1)S(1)}, bf16[1,1024,128]{2,1,0:T(8,128)(2,1)S(1)}, u32[]{:S(2)}, u32[]{:S(2)}) collective-permute-start(bf16[1,1024,128]{2,1,0:T(8,128)(2,1)S(1)} %copy-done.31), channel_id=1, source_target_pairs={{0,6},{1,7},{2,4},{3,5},{4,2},{5,3},{6,0},{7,1},{8,14},{9,15},{10,... | collective-permute-start | bytes 786440 | tf_op jit(solution)/shard_map/ppermute | solution.py:586
  355.3 12.3 %collective-permute-start.20 = (bf16[1,1024,128]{2,1,0:T(8,128)(2,1)S(1)}, bf16[1,1024,128]{2,1,0:T(8,128)(2,1)S(1)}, u32[]{:S(2)}, u32[]{:S(2)}) collective-permute-start(bf16[1,1024,128]{2,1,0:T(8,128)(2,1)S(1)} %get-tuple-element.133), channel_id=1, source_target_pairs={{0,7},{1,6},{2,5},{3,4},{4,3},{5,2},{6,1},{7,0},{8,15},{9,14},{10,... | collective-permute-start | bytes 786440 | tf_op jit(solution)/shard_map/ppermute | solution.py:586
  367.7 20.3 %copy-start.6 = (bf16[4,4,256,128]{3,2,1,0:T(8,128)(2,1)S(1)}, bf16[4,4,256,128]{3,2,1,0:T(8,128)(2,1)}, u32[]{:S(2)}) copy-start(bf16[4,4,256,128]{3,2,1,0:T(8,128)(2,1)} %copy-done.5) | copy-start | bytes 3145732
  396.1 8.4 %copy-start.7 = (bf16[4,4,256,128]{3,2,1,0:T(8,128)(2,1)S(1)}, bf16[4,4,256,128]{3,2,1,0:T(8,128)(2,1)}, u32[]{:S(2)}) copy-start(bf16[4,4,256,128]{3,2,1,0:T(8,128)(2,1)} %copy-done.5) | copy-start | bytes 3145732
  396.1 8.4 %copy-start.11 = (bf16[2,4,256,128]{3,2,1,0:T(8,128)(2,1)S(1)}, bf16[2,4,256,128]{3,2,1,0:T(8,128)(2,1)}, u32[]{:S(2)}) copy-start(bf16[2,4,256,128]{3,2,1,0:T(8,128)(2,1)} %copy-done.10) | copy-start | bytes 1572868
  396.1 8.4 %copy-start.13 = (bf16[2,4,256,128]{3,2,1,0:T(8,128)(2,1)S(1)}, bf16[2,4,256,128]{3,2,1,0:T(8,128)(2,1)}, u32[]{:S(2)}) copy-start(bf16[2,4,256,128]{3,2,1,0:T(8,128)(2,1)} %copy-done.12) | copy-start | bytes 1572868
  422.6 113.1 %all-to-all-start.5 = ((bf16[8,1,2,1024,128]{4,3,2,1,0:T(8,128)(2,1)}), bf16[8,1,2,1024,128]{4,3,2,1,0:T(8,128)(2,1)}, u32[]{:S(2)}, u32[]{:S(2)}) async-start(bf16[8,1,2,1024,128]{4,3,2,1,0:T(8,128)(2,1)} %copy-done.2), calls=%async_computation.5 | async-start | bytes 8388608 | tf_op jit(solution)/shard_map/all_to_all | solution.py:632
  430.1 68.2 %collective-permute-start.24 = (bf16[2,256,1024]{2,1,0:T(8,128)(2,1)S(1)}, bf16[2,256,1024]{2,1,0:T(8,128)(2,1)}, u32[]{:S(2)}, u32[]{:S(2)}) collective-permute-start(bf16[2,256,1024]{2,1,0:T(8,128)(2,1)S(1)} %shard_map.213.refs_1_), channel_id=1, source_target_pairs={{0,4},{2,6},{4,0},{6,2},{1,5},{3,7},{5,1},{7,3},{8,12},{10,14},{12... | collective-permute-start | bytes 3145736 | tf_op jit(solution)/shard_map/ppermute | solution.py:442
  433.8 64.5 %collective-permute-start.23 = (bf16[2,256,1024]{2,1,0:T(8,128)(2,1)}, bf16[2,256,1024]{2,1,0:T(8,128)(2,1)S(1)}, u32[]{:S(2)}, u32[]{:S(2)}) collective-permute-start(bf16[2,256,1024]{2,1,0:T(8,128)(2,1)} %shard_map.212.refs_0_), channel_id=1, source_target_pairs={{0,2},{2,0},{4,6},{6,4},{1,3},{3,1},{5,7},{7,5},{8,10},{10,8},{12,... | collective-permute-start | bytes 3145736 | tf_op jit(solution)/shard_map/ppermute | solution.py:442
  435.3 85.1 %collective-permute-start.27 = (bf16[2,256,1024]{2,1,0:T(8,128)(2,1)S(1)}, bf16[2,256,1024]{2,1,0:T(8,128)(2,1)}, u32[]{:S(2)}, u32[]{:S(2)}) collective-permute-start(bf16[2,256,1024]{2,1,0:T(8,128)(2,1)S(1)} %shard_map.213.refs_1_), channel_id=1, source_target_pairs={{0,2},{2,0},{4,6},{6,4},{1,3},{3,1},{5,7},{7,5},{8,10},{10,8},{12,... | collective-permute-start | bytes 3145736 | tf_op jit(solution)/shard_map/ppermute | solution.py:442
  435.8 84.5 %collective-permute-start.30 = (bf16[2,256,1024]{2,1,0:T(8,128)(2,1)S(1)}, bf16[2,256,1024]{2,1,0:T(8,128)(2,1)S(1)}, u32[]{:S(2)}, u32[]{:S(2)}) collective-permute-start(bf16[2,256,1024]{2,1,0:T(8,128)(2,1)S(1)} %shard_map.213.refs_1_), channel_id=1, source_target_pairs={{0,1},{1,0},{2,3},{3,2},{4,5},{5,4},{6,7},{7,6},{8,9},{9,8},{10,11... | collective-permute-start | bytes 3145736 | tf_op jit(solution)/shard_map/ppermute | solution.py:446
  455.2 65.6 %collective-permute-start.28 = (bf16[2,256,1024]{2,1,0:T(8,128)(2,1)}, bf16[2,256,1024]{2,1,0:T(8,128)(2,1)}, u32[]{:S(2)}, u32[]{:S(2)}) collective-permute-start(bf16[2,256,1024]{2,1,0:T(8,128)(2,1)} %shard_map.212.refs_0_), channel_id=1, source_target_pairs={{0,4},{2,6},{4,0},{6,2},{1,5},{3,7},{5,1},{7,3},{8,12},{10,14},{12... | collective-permute-start | bytes 3145736 | tf_op jit(solution)/shard_map/ppermute | solution.py:442
  498.3 22.7 %collective-permute-start.29 = (bf16[2,256,1024]{2,1,0:T(8,128)(2,1)}, bf16[2,256,1024]{2,1,0:T(8,128)(2,1)}, u32[]{:S(2)}, u32[]{:S(2)}) collective-permute-start(bf16[2,256,1024]{2,1,0:T(8,128)(2,1)} %shard_map.212.refs_0_), channel_id=1, source_target_pairs={{0,1},{1,0},{2,3},{3,2},{4,5},{5,4},{6,7},{7,6},{8,9},{9,8},{10,11... | collective-permute-start | bytes 3145736 | tf_op jit(solution)/shard_map/ppermute | solution.py:446
  498.3 24.2 %collective-permute-start.31 = (bf16[2,256,1024]{2,1,0:T(8,128)(2,1)S(1)}, bf16[2,256,1024]{2,1,0:T(8,128)(2,1)S(1)}, u32[]{:S(2)}, u32[]{:S(2)}) collective-permute-start(bf16[2,256,1024]{2,1,0:T(8,128)(2,1)S(1)} %collective-permute-done.23.refs_2_), channel_id=1, source_target_pairs={{0,1},{1,0},{2,3},{3,2},{4,5},{5,4},{6,7},{7,6},{8,9},{9,8},{10,11... | collective-permute-start | bytes 3145736 | tf_op jit(solution)/shard_map/ppermute | solution.py:446
  520.3 5.2 collective-permute-start.34
  520.4 5.2 collective-permute-start.32
  520.9 5.5 collective-permute-start.33
  520.9 25.5 %collective-permute-start.25 = (bf16[2,256,1024]{2,1,0:T(8,128)(2,1)S(1)}, bf16[2,256,1024]{2,1,0:T(8,128)(2,1)S(1)}, u32[]{:S(2)}, u32[]{:S(2)}) collective-permute-start(bf16[2,256,1024]{2,1,0:T(8,128)(2,1)S(1)} %collective-permute-done.23.refs_2_), channel_id=1, source_target_pairs={{0,4},{2,6},{4,0},{6,2},{1,5},{3,7},{5,1},{7,3},{8,12},{10,14},{12... | collective-permute-start | bytes 3145736 | tf_op jit(solution)/shard_map/ppermute | solution.py:442
  523.4 25.5 %collective-permute-start.26 = (bf16[2,256,1024]{2,1,0:T(8,128)(2,1)}, bf16[2,256,1024]{2,1,0:T(8,128)(2,1)}, u32[]{:S(2)}, u32[]{:S(2)}) collective-permute-start(bf16[2,256,1024]{2,1,0:T(8,128)(2,1)} %collective-permute-done.24.refs_5_), channel_id=1, source_target_pairs={{0,2},{2,0},{4,6},{6,4},{1,3},{3,1},{5,7},{7,5},{8,10},{10,8},{12,... | collective-permute-start | bytes 3145736 | tf_op jit(solution)/shard_map/ppermute | solution.py:442
  535.7 13.9 %copy-start.33 = (f32[208,256]{1,0:T(8,128)S(1)}, f32[208,256]{1,0:T(8,128)}, u32[]{:S(2)}) copy-start(f32[208,256]{1,0:T(8,128)} %param.26) | copy-start | bytes 638980
  535.7 13.9 %copy-start.34 = (f32[208,256]{1,0:T(8,128)S(1)}, f32[208,256]{1,0:T(8,128)}, u32[]{:S(2)}) copy-start(f32[208,256]{1,0:T(8,128)} %param.28) | copy-start | bytes 638980
  535.7 13.9 %copy-start.35 = (f32[208,256]{1,0:T(8,128)S(1)}, f32[208,256]{1,0:T(8,128)}, u32[]{:S(2)}) copy-start(f32[208,256]{1,0:T(8,128)} %param.29) | copy-start | bytes 638980
  535.7 13.9 %copy-start.36 = (bf16[208,256]{1,0:T(8,128)(2,1)S(1)}, bf16[208,256]{1,0:T(8,128)(2,1)}, u32[]{:S(2)}) copy-start(bf16[208,256]{1,0:T(8,128)(2,1)} %param.27) | copy-start | bytes 319492
  549.0 4.1 collective-permute-start.35
  549.0 4.4 collective-permute-start.36
  (18 other events, 30.6 us)
Sparse Core Ops, SparseCore 0:
  122.8 100.4 all-gather.4
  253.0 92.1 all-gather.6

commit v2 on v0

--- a/solution.py
+++ b/solution.py
@@ -547,8 +547,9 @@
     partials = grad_parts[0]
     cuts = [(0, early), (early, per)] if early else [(0, per)]
     orders = [pick(by_entry[:, a:b]) for a, b in cuts]
+    sent = [reorder(partials, other) for _, other in orders]
+    sent[0], right_root = lax.optimization_barrier((sent[0], right_root))
     right_dealt = deal(reorder(right_root, order))
-    sent = [reorder(partials, other) for _, other in orders]
     right_dealt, sent[-1] = lax.optimization_barrier((right_dealt, sent[-1]))
     if early and owner_count == 4 and rows * owner_count == size:
         spread = group // owner_count
@@ -557,12 +558,8 @@
         sums, near = lax.optimization_barrier((sums, near))
         gradient = [last_sums(*sums)]
         middle = next_hop(near, spread)
-        sums = first_sums(partials, sent[1], orders[1][0])
-        sums, middle = lax.optimization_barrier((sums, middle))
-        gradient.append(last_sums(*sums))
-        far = next_hop(middle, spread)
-        downs, ups = zip(near, middle, far)
-        rights = [right_dealt, *downs, *ups]
+        gradient.append(last_sums(*first_sums(partials, sent[1], orders[1][0])))
+        rights = [near, middle]
     else:
         gradient = [
             last_sums(*first_sums(partials, part, mine)) for part, (mine, _) in zip(sent, orders)
@@ -576,9 +573,12 @@
     tiles = deal(jnp.transpose(tiles, (2, 0, 1, 3)))
 
     if early:
-        grad_blocks[0], left_dealt, weights_dealt, tiles = lax.optimization_barrier(
-            (grad_blocks[0], left_dealt, weights_dealt, tiles)
+        grad_blocks[0], left_dealt, weights_dealt, tiles, rights = lax.optimization_barrier(
+            (grad_blocks[0], left_dealt, weights_dealt, tiles, rights)
         )
+        if len(rights) == 2:
+            downs, ups = zip(*rights, next_hop(rights[1], group // owner_count))
+            rights = [right_dealt, *downs, *ups]
         slabs = grams(grad_blocks[0], jnp.arange(early, dtype=jnp.int32))
         slabs, left_dealt, tiles = lax.optimization_barrier((slabs, left_dealt, tiles))
         received = lax.all_to_all(slabs, GROUP, split_axis=0, concat_axis=0, tiled=True)

time: 540 us -> 535 us (level)
  blocking collectives: 47 us -> 15.1 us
  waiting for transfers between devices: 235 us -> 255 us
  starting transfers between devices: 60.5 us -> 68.5 us
    all_to_all x1 -> x0, blocking collectives: 30.9 us -> none  [deal(): lax.all_to_all(tiles.reshape(group, per, rows, cols), GROUP, split_axis=0...]
    ppermute x14, waiting for transfers between devices: 135 us -> 161 us  [swap(): return lax.ppermute(array, 'tensor', [(t, t ^ bit) for t in range(devices)])]
    ppermute x3, waiting for transfers between devices: 30.7 us -> 22.8 us  [hop(): lax.ppermute(moved[0], 'shard', down)]
    all_to_all x3 -> x4, starting transfers between devices: 12.6 us -> 17 us  [deal(): lax.all_to_all(tiles.reshape(group, per, rows, cols), GROUP, split_axis=0...]
    unnamed x74 -> x70, local copies, waits for them, and re-layouts: 16.1 us -> 16.1 us
    all_to_all x3 -> x4, waiting for transfers between devices: 11.6 us -> 11.6 us  [deal(): lax.all_to_all(tiles.reshape(group, per, rows, cols), GROUP, split_axis=0...]
  transfers between devices with their start and end apart: 37 -> 38, of which waited for: 18 -> 19; matrix products, arithmetic and copies ran while one was open for 4% -> 4% of each run, Pallas kernels for 22% -> 22%
where the time goes in v2:
time: 535 us; the launch traced here: 533 us
  waiting for transfers between devices  255 us (48%)
  Pallas kernels  136 us (25%)
  starting transfers between devices  68.5 us (13%)
  local copies, waits for them, and re-layouts  23.5 us (4%)
  other arithmetic  18.9 us (4%)
  between operations  16 us (3%)
  blocking collectives  15.1 us (3%)
    ppermute x14, waiting for transfers between devices, swap(): return lax.ppermute(array, 'tensor', [(t, t ^ bit) for t in range(devices)])  161 us
    all_gather x2, waiting for transfers between devices, shards(): grad_blocks = [lax.all_gather(part, 'shard', axis=0) for part in gradient]  51.2 us
    pallas_call x7, Pallas kernels, reorder(): pl.pallas_call(reorder_kernel, grid_spec=pltpu.PrefetchScalarGridSpec(num...  29.8 us
    pallas_call x2, Pallas kernels, refresh(): pl.pallas_call(stat_kernel, grid_spec=pltpu.PrefetchScalarGridSpec(num_sc...  29.7 us
    ppermute x3, waiting for transfers between devices, hop(): lax.ppermute(moved[0], 'shard', down)  22.8 us
    pallas_call x1, Pallas kernels, adam(): pl.pallas_call(adam_kernel, grid_spec=pltpu.PrefetchScalarGridSpec(num_sc...  20.6 us
    ppermute x14, starting transfers between devices, swap(): return lax.ppermute(array, 'tensor', [(t, t ^ bit) for t in range(devices)])  19.7 us
    pallas_call x2, Pallas kernels, grams(): pl.pallas_call(gram_kernel, grid_spec=pltpu.PrefetchScalarGridSpec(num_sc...  18.2 us
  transfers between devices with their start and end apart: 38, of which 19 were waited for; matrix products, arithmetic and copies ran while one was open for 4% of the time, Pallas kernels for 22%

profile of v2, /device:TPU:0, one launch (start us, length us, event | category | flops | bytes accessed | tf_op | source)
XLA Modules:
  0.0 533.1 jit_solution(11167957571445840133)
XLA Ops:
  10.5 2.0 fusion.18
  14.4 4.2 shard_map.197
  19.1 7.3 %shard_map.199 = bf16[32,256,128]{2,1,0:T(8,128)(2,1)S(1)} custom-call(s32[32]{0:T(128)S(1)} %select_reduce_fusion.order, bf16[32,256,128]{2,1,0:T(8,128)(2,1)S(1)} %copy-done.12), custom_call_target="tpu_custom_call" | custom-call | tf_op jit(solution)/shard_map/pallas_call | solution.py:72
  26.4 1.3 copy-done.7
  27.7 4.8 all-to-all-start
  34.2 4.1 shard_map.200
  38.3 5.4 %shard_map.198 = (bf16[2,2,128,1024]{3,2,1,0:T(8,128)(2,1)S(1)}, bf16[2,2,128,1024]{3,2,1,0:T(8,128)(2,1)S(1)}, bf16[2,2,128,1024]{3,2,1,0:T(8,128)(2,1)}, bf16[2,2,128,1024]{3,2,1,0:T(8,128)(2,1)S(1)}) custom-call(s32[8]{0:T(128)S(1)} %reshape.184.picked, bf16[32,256,1024]{2,1,0:T(8,128)(2,1)} %bitcast.105, bf16[32,256,1024]{2,1,0:T(8,128)(2,1)} %bitcast.106, ...), custom_call_target="tpu_custom_call" | custom-call | tf_op jit(solution)/shard_map/pallas_call | solution.py:421
  45.7 2.0 collective-permute-start.2
  47.7 11.6 %all-to-all-done.refs_0_ = bf16[8,4,256,128]{3,2,1,0:T(8,128)(2,1)S(1)} async-done(((bf16[8,4,256,128]{3,2,1,0:T(8,128)(2,1)}), bf16[8,4,256,128]{3,2,1,0:T(8,128)(2,1)S(1)}, u32[]{:S(2)}, u32[]{:S(2)}) %all-to-all-start) | async-done | bytes 2097184 | tf_op jit(solution)/shard_map/all_to_all | solution.py:542
  60.2 1.4 collective-permute-start.3
  62.6 4.6 collective-permute-start.4
  67.8 13.0 %collective-permute-done.2 = bf16[2,2,128,1024]{3,2,1,0:T(8,128)(2,1)} collective-permute-done((bf16[2,2,128,1024]{3,2,1,0:T(8,128)(2,1)}, bf16[2,2,128,1024]{3,2,1,0:T(8,128)(2,1)}, u32[]{:S(2)}, u32[]{:S(2)}) %collective-permute-start.2) | collective-permute-done | bytes 1048608 | tf_op jit(solution)/shard_map/ppermute | solution.py:442
  80.8 1.6 add_convert_fusion.2
  82.5 10.4 %collective-permute-done.1 = bf16[2,2,128,1024]{3,2,1,0:T(8,128)(2,1)S(1)} collective-permute-done((bf16[2,2,128,1024]{3,2,1,0:T(8,128)(2,1)S(1)}, bf16[2,2,128,1024]{3,2,1,0:T(8,128)(2,1)S(1)}, u32[]{:S(2)}, u32[]{:S(2)}) %collective-permute-start.1) | collective-permute-done | bytes 1048608 | tf_op jit(solution)/shard_map/ppermute | solution.py:442
  93.3 2.2 collective-permute-done.3.refs_1_
  95.5 2.1 collective-permute-done.4.refs_4_
  97.6 1.4 collective-permute-start.5
  99.1 2.6 collective-permute-start.6
  101.7 6.0 %collective-permute-done.5 = bf16[2,128,1024]{2,1,0:T(8,128)(2,1)S(1)} collective-permute-done((bf16[2,128,1024]{2,1,0:T(8,128)(2,1)S(1)}, bf16[2,128,1024]{2,1,0:T(8,128)(2,1)S(1)}, u32[]{:S(2)}, u32[]{:S(2)}) %collective-permute-start.5) | collective-permute-done | bytes 524320 | tf_op jit(solution)/shard_map/ppermute | solution.py:442
  107.9 4.4 collective-permute-done.6
  113.6 5.2 shard_map.203
  118.8 4.2 all-to-all-start.1
  123.2 6.2 %shard_map.205 = (bf16[2,2,128,1024]{3,2,1,0:T(8,128)(2,1)S(1)}, bf16[2,2,128,1024]{3,2,1,0:T(8,128)(2,1)S(1)}, bf16[2,2,128,1024]{3,2,1,0:T(8,128)(2,1)}, bf16[2,2,128,1024]{3,2,1,0:T(8,128)(2,1)S(1)}) custom-call(s32[8]{0:T(128)S(1)} %reshape.193.picked, bf16[32,256,1024]{2,1,0:T(8,128)(2,1)} %bitcast.109, bf16[32,256,1024]{2,1,0:T(8,128)(2,1)} %bitcast.110, ...), custom_call_target="tpu_custom_call" | custom-call | tf_op jit(solution)/shard_map/pallas_call | solution.py:421
  129.4 2.0 collective-permute-start.8
  131.4 1.5 collective-permute-start.10
  132.8 7.3 %shard_map.204 = bf16[32,256,128]{2,1,0:T(8,128)(2,1)S(1)} custom-call(s32[32]{0:T(128)S(1)} %select_reduce_fusion.order, bf16[32,256,128]{2,1,0:T(8,128)(2,1)S(1)} %copy-done.14), custom_call_target="tpu_custom_call" | custom-call | tf_op jit(solution)/shard_map/pallas_call | solution.py:72
  140.1 1.3 copy-done.6
  141.4 29.8 %collective-permute-done.8 = bf16[2,2,128,1024]{3,2,1,0:T(8,128)(2,1)S(1)} collective-permute-done((bf16[2,2,128,1024]{3,2,1,0:T(8,128)(2,1)S(1)}, bf16[2,2,128,1024]{3,2,1,0:T(8,128)(2,1)S(1)}, u32[]{:S(2)}, u32[]{:S(2)}) %collective-permute-start.8) | collective-permute-done | bytes 1048608 | tf_op jit(solution)/shard_map/ppermute | solution.py:442
  171.3 1.4 add_convert_fusion.1
  172.6 1.3 copy-done.23
  174.0 3.6 all-to-all-start.2
  178.7 2.0 collective-permute-start.9
  180.7 1.7 add_convert_fusion
  182.4 1.5 collective-permute-start.11
  184.0 30.5 %collective-permute-done.9 = bf16[2,128,1024]{2,1,0:T(8,128)(2,1)S(1)} collective-permute-done((bf16[2,128,1024]{2,1,0:T(8,128)(2,1)S(1)}, bf16[2,128,1024]{2,1,0:T(8,128)(2,1)S(1)}, u32[]{:S(2)}, u32[]{:S(2)}) %collective-permute-start.9) | collective-permute-done | bytes 524320 | tf_op jit(solution)/shard_map/ppermute | solution.py:442
  214.9 3.5 bitcast_bitcast_fusion
  218.4 4.4 all-to-all-start.3
  222.8 1.4 slice.165
  225.7 6.0 %collective-permute-start.13 = (bf16[4,4,256,128]{3,2,1,0:T(8,128)(2,1)S(1)}, bf16[4,4,256,128]{3,2,1,0:T(8,128)(2,1)}, u32[]{:S(2)}, u32[]{:S(2)}) collective-permute-start(bf16[4,4,256,128]{3,2,1,0:T(8,128)(2,1)S(1)} %slice.166), channel_id=1, source_target_pairs={{0,8},{8,16},{16,24},{1,9},{9,17},{17,25},{2,10},{10,18},{18,26},{... | collective-permute-start | bytes 3145736 | tf_op jit(solution)/shard_map/ppermute | solution.py:321
  231.7 20.6 %collective-permute-done.12.refs_2_ = bf16[4,4,256,128]{3,2,1,0:T(8,128)(2,1)S(1)} collective-permute-done((bf16[4,4,256,128]{3,2,1,0:T(8,128)(2,1)S(1)}, bf16[4,4,256,128]{3,2,1,0:T(8,128)(2,1)S(1)}, u32[]{:S(2)}, u32[]{:S(2)}) %collective-permute-start.12) | collective-permute-done | bytes 1048608 | tf_op jit(solution)/shard_map/ppermute | solution.py:321
  253.6 2.2 copy-done.1
  255.8 12.0 %shard_map.206 = bf16[8,2,2,1024,128]{4,3,2,1,0:T(8,128)(2,1)} custom-call(s32[2]{0:T(128)S(1)} %iota.51.chosen, bf16[4,2,256,1024]{3,2,1,0:T(8,128)(2,1)S(1)} %bitcast.98), custom_call_target="tpu_custom_call" | custom-call | tf_op jit(solution)/shard_map/pallas_call | solution.py:177
  267.8 5.0 all-to-all-start.4
  276.6 5.2 collective-permute-start.15
  281.9 20.6 %shard_map.207 = (f32[32,256,128]{2,1,0:T(8,128)}, f32[32,256,128]{2,1,0:T(8,128)}, f32[32,1,128]{2,1,0:T(1,128)S(1)}) custom-call(s32[32]{0:T(128)S(1)} %fusion.12.place, bf16[32,256,128]{2,1,0:T(8,128)(2,1)} %bitcast.27.grad, f32[32,256,128]{2,1,0:T(8,128)} %moment.1, f32[32,256,128]{2,1,0:T(8,128)} %second.1), custom_call_target="tpu_custom_call" | custom-call | tf_op jit(solution)/shard_map/pallas_call | solution.py:125
  302.5 5.0 shard_map.208
  310.1 51.2 %all-gather.7.cloned.1.call-done = bf16[8,256,1024]{2,1,0:T(8,128)(2,1)} async-done(((bf16[2,256,1024]{2,1,0:T(8,128)(2,1)}), bf16[8,256,1024]{2,1,0:T(8,128)(2,1)}) %all-gather.7.cloned.1.call-update) | async-done | bytes 4194320 | tf_op jit(solution)/shard_map/all_gather | solution.py:569
  361.7 6.3 %shard_map.209 = bf16[8,1,2,1024,128]{4,3,2,1,0:T(8,128)(2,1)S(1)} custom-call(s32[1]{0:T(128)} %bitcast.25.chosen, bf16[4,2,256,1024]{3,2,1,0:T(8,128)(2,1)} %bitcast.113), custom_call_target="tpu_custom_call" | custom-call | tf_op jit(solution)/shard_map/pallas_call | solution.py:177
  368.0 2.1 copy-done.2
  370.1 5.0 shard_map.210
  376.5 15.1 %all_to_all.35 = f32[32,8,128]{2,1,0:T(8,128)S(1)} all-to-all(f32[32,8,128]{2,1,0:T(8,128)S(1)} %broadcast_in_dim.47), channel_id=1, replica_groups=mesh['shard'=4,'tensor'=4,'section'=2] {'shard','tensor','section'}, dimensions={0} | all-to-all | bytes 262144 | tf_op jit(solution)/shard_map/all_to_all | solution.py:610
  391.6 4.8 all-to-all-start.6
  399.0 1.8 collective-permute-start.17
  400.8 2.0 shard_map.211.refs_0_
  402.8 1.5 collective-permute-start.16
  404.8 19.4 %shard_map.213 = (f32[24,1024,128]{2,1,0:T(8,128)}, f32[24,1024,128]{2,1,0:T(8,128)}) custom-call(s32[1]{0:T(128)} %bitcast.33.base, s32[16]{0:T(128)S(1)} %get-tuple-element.164.source, s32[16]{0:T(128)S(1)} %get-tuple-element.163.entry, s32[16]{0:T(128)S(1)} %mul.136.filled, f32[24,1024,128]{2,1,0:T(8,128)} %left_stat.3, f32[24,1024,128]{2,1,0:T(8,128)} %right_stat.3, ...), custom_call_target="tpu_custom_call" | custom-call | tf_op jit(solution)/shard_map/pallas_call | solution.py:212
  424.6 42.7 %collective-permute-done.17.refs_5_ = bf16[2,256,1024]{2,1,0:T(8,128)(2,1)} collective-permute-done((bf16[2,256,1024]{2,1,0:T(8,128)(2,1)S(1)}, bf16[2,256,1024]{2,1,0:T(8,128)(2,1)}, u32[]{:S(2)}, u32[]{:S(2)}) %collective-permute-start.17) | collective-permute-done | bytes 1048608 | tf_op jit(solution)/shard_map/ppermute | solution.py:442
  467.8 21.6 %collective-permute-done.20.refs_3_ = bf16[2,256,1024]{2,1,0:T(8,128)(2,1)} collective-permute-done((bf16[2,256,1024]{2,1,0:T(8,128)(2,1)S(1)}, bf16[2,256,1024]{2,1,0:T(8,128)(2,1)}, u32[]{:S(2)}, u32[]{:S(2)}) %collective-permute-start.20) | collective-permute-done | bytes 1048608 | tf_op jit(solution)/shard_map/ppermute | solution.py:442
  490.0 1.5 collective-permute-start.18
  495.4 9.3 %shard_map.214.refs_4_ = bf16[32,256,1024]{2,1,0:T(8,128)(2,1)} custom-call(s32[24]{0:T(128)S(1)} %concatenate.23.target, bf16[2,256,1024]{2,1,0:T(8,128)(2,1)} %shard_map.211.refs_0_, bf16[2,256,1024]{2,1,0:T(8,128)(2,1)S(1)} %shard_map.212.refs_1_, bf16[2,256,1024]{2,1,0:T(8,128)(2,1)S(1)} %collective-permute-done.16.refs_2_, ...), custom_call_target="tpu_custom_call" | custom-call | tf_op jit(solution)/shard_map/pallas_call | solution.py:97
  504.8 10.3 %shard_map.215 = (f32[24,1024,128]{2,1,0:T(8,128)}, f32[24,1024,128]{2,1,0:T(8,128)}) custom-call(s32[1]{0:T(128)} %bitcast.46.base, s32[8]{0:T(128)S(1)} %and_select_fusion.source, s32[8]{0:T(128)S(1)} %broadcast.203.entry, s32[8]{0:T(128)S(1)} %compare_convert_fusion.filled, ...), custom_call_target="tpu_custom_call", output_to_operand_aliasing={{0}: (8, {}), {1}: (9, {})} | custom-call | tf_op jit(solution)/shard_map/pallas_call | solution.py:212
  515.5 2.5 collective-permute-done.19.refs_1_
  519.6 2.5 collective-permute-done.28.refs_2_
  522.4 3.8 shard_map.216
  (179 shorter events, 35.9 us)
Async XLA Ops:
  14.4 4.7 copy-start.12
  18.6 19.7 %collective-permute-start = (bf16[8,256,1024]{2,1,0:T(8,128)(2,1)}, bf16[8,256,1024]{2,1,0:T(8,128)(2,1)}, u32[]{:S(2)}, u32[]{:S(2)}) collective-permute-start(bf16[8,256,1024]{2,1,0:T(8,128)(2,1)} %shard_map.197), channel_id=1, source_target_pairs={{0,1},{1,0},{2,3},{3,2},{4,5},{5,4},{6,7},{7,6},{8,9},{9,8},{10,11... | collective-permute-start | bytes 12582920 | tf_op jit(solution)/shard_map/ppermute | solution.py:446
  26.4 1.3 copy-start.7
  27.7 31.6 %all-to-all-start = ((bf16[8,4,256,128]{3,2,1,0:T(8,128)(2,1)}), bf16[8,4,256,128]{3,2,1,0:T(8,128)(2,1)S(1)}, u32[]{:S(2)}, u32[]{:S(2)}) async-start(bf16[8,4,256,128]{3,2,1,0:T(8,128)(2,1)} %bitcast.100), calls=%async_computation | async-start | bytes 4194304 | tf_op jit(solution)/shard_map/all_to_all | solution.py:542
  32.5 221.1 %all-gather.5.cloned.1.call-start = ((), (), s32[]{:S(2)}) async-start(), calls=%async_computation.7 | async-start | bytes 5242880 | tf_op jit(solution)/shard_map/all_gather | solution.py:569
  45.7 35.1 %collective-permute-start.2 = (bf16[2,2,128,1024]{3,2,1,0:T(8,128)(2,1)}, bf16[2,2,128,1024]{3,2,1,0:T(8,128)(2,1)}, u32[]{:S(2)}, u32[]{:S(2)}) collective-permute-start(bf16[2,2,128,1024]{3,2,1,0:T(8,128)(2,1)} %get-tuple-element.67), channel_id=1, source_target_pairs={{0,4},{2,6},{4,0},{6,2},{1,5},{3,7},{5,1},{7,3},{8,12},{10,14},{12... | collective-permute-start | bytes 3145736 | tf_op jit(solution)/shard_map/ppermute | solution.py:442
  59.3 3.3 copy-start
  60.2 7.1 %copy-start.22 = (bf16[2,2,128,1024]{3,2,1,0:T(8,128)(2,1)S(1)}, bf16[2,2,128,1024]{3,2,1,0:T(8,128)(2,1)}, u32[]{:S(2)}) copy-start(bf16[2,2,128,1024]{3,2,1,0:T(8,128)(2,1)} %copy-done.21) | copy-start | bytes 3145732
  60.2 20.6 %copy-start.20 = (bf16[2,2,128,1024]{3,2,1,0:T(8,128)(2,1)S(1)}, bf16[2,2,128,1024]{3,2,1,0:T(8,128)(2,1)}, u32[]{:S(2)}) copy-start(bf16[2,2,128,1024]{3,2,1,0:T(8,128)(2,1)} %copy-done.19) | copy-start | bytes 3145732
  60.2 35.3 %collective-permute-start.3 = (bf16[6,4,256,128]{3,2,1,0:T(8,128)(2,1)S(1)}, bf16[6,4,256,128]{3,2,1,0:T(8,128)(2,1)S(1)}, u32[]{:S(2)}, u32[]{:S(2)}) collective-permute-start(bf16[6,4,256,128]{3,2,1,0:T(8,128)(2,1)S(1)} %bitcast.101), channel_id=1, source_target_pairs={{8,0},{16,8},{24,16},{9,1},{17,9},{25,17},{10,2},{18,10},{26,18},{... | collective-permute-start | bytes 4718600 | tf_op jit(solution)/shard_map/ppermute | solution.py:321
  62.6 35.0 %collective-permute-start.4 = (bf16[6,4,256,128]{3,2,1,0:T(8,128)(2,1)S(1)}, bf16[6,4,256,128]{3,2,1,0:T(8,128)(2,1)S(1)}, u32[]{:S(2)}, u32[]{:S(2)}) collective-permute-start(bf16[6,4,256,128]{3,2,1,0:T(8,128)(2,1)S(1)} %bitcast.102), channel_id=1, source_target_pairs={{0,8},{8,16},{16,24},{1,9},{9,17},{17,25},{2,10},{10,18},{18,26},{... | collective-permute-start | bytes 4718600 | tf_op jit(solution)/shard_map/ppermute | solution.py:321
  67.2 56.0 %collective-permute-start.7 = (bf16[8,256,1024]{2,1,0:T(8,128)(2,1)}, bf16[8,256,1024]{2,1,0:T(8,128)(2,1)}, u32[]{:S(2)}, u32[]{:S(2)}) collective-permute-start(bf16[8,256,1024]{2,1,0:T(8,128)(2,1)} %shard_map.200), channel_id=1, source_target_pairs={{0,1},{1,0},{2,3},{3,2},{4,5},{5,4},{6,7},{7,6},{8,9},{9,8},{10,11... | collective-permute-start | bytes 12582920 | tf_op jit(solution)/shard_map/ppermute | solution.py:446
  67.3 25.6 %collective-permute-start.1 = (bf16[2,2,128,1024]{3,2,1,0:T(8,128)(2,1)S(1)}, bf16[2,2,128,1024]{3,2,1,0:T(8,128)(2,1)S(1)}, u32[]{:S(2)}, u32[]{:S(2)}) collective-permute-start(bf16[2,2,128,1024]{3,2,1,0:T(8,128)(2,1)S(1)} %copy-done.22), channel_id=1, source_target_pairs={{0,2},{2,0},{4,6},{6,4},{1,3},{3,1},{5,7},{7,5},{8,10},{10,8},{12,... | collective-permute-start | bytes 3145736 | tf_op jit(solution)/shard_map/ppermute | solution.py:442
  95.5 17.0 %copy-start.3 = (bf16[6,4,256,128]{3,2,1,0:T(8,128)(2,1)}, bf16[6,4,256,128]{3,2,1,0:T(8,128)(2,1)S(1)}, u32[]{:S(2)}) copy-start(bf16[6,4,256,128]{3,2,1,0:T(8,128)(2,1)S(1)} %collective-permute-done.3.refs_1_) | copy-start | bytes 4718596
  97.6 14.9 %copy-start.24 = (bf16[6,4,256,128]{3,2,1,0:T(8,128)(2,1)}, bf16[6,4,256,128]{3,2,1,0:T(8,128)(2,1)S(1)}, u32[]{:S(2)}) copy-start(bf16[6,4,256,128]{3,2,1,0:T(8,128)(2,1)S(1)} %collective-permute-done.4.refs_4_) | copy-start | bytes 4718596
  97.6 10.1 %collective-permute-start.5 = (bf16[2,128,1024]{2,1,0:T(8,128)(2,1)S(1)}, bf16[2,128,1024]{2,1,0:T(8,128)(2,1)S(1)}, u32[]{:S(2)}, u32[]{:S(2)}) collective-permute-start(bf16[2,128,1024]{2,1,0:T(8,128)(2,1)S(1)} %slice_bitcast_fusion.5), channel_id=1, source_target_pairs={{0,4},{2,6},{4,0},{6,2},{1,5},{3,7},{5,1},{7,3},{8,12},{10,14},{12... | collective-permute-start | bytes 1572872 | tf_op jit(solution)/shard_map/ppermute | solution.py:442
  99.1 13.2 %collective-permute-start.6 = (bf16[2,128,1024]{2,1,0:T(8,128)(2,1)S(1)}, bf16[2,128,1024]{2,1,0:T(8,128)(2,1)S(1)}, u32[]{:S(2)}, u32[]{:S(2)}) collective-permute-start(bf16[2,128,1024]{2,1,0:T(8,128)(2,1)S(1)} %slice_bitcast_fusion.4), channel_id=1, source_target_pairs={{0,2},{2,0},{4,6},{6,4},{1,3},{3,1},{5,7},{7,5},{8,10},{10,8},{12,... | collective-permute-start | bytes 1572872 | tf_op jit(solution)/shard_map/ppermute | solution.py:442
  107.9 5.7 %copy-start.13 = (bf16[32,256,128]{2,1,0:T(8,128)(2,1)S(1)}, bf16[32,256,128]{2,1,0:T(8,128)(2,1)}, u32[]{:S(2)}) copy-start(bf16[32,256,128]{2,1,0:T(8,128)(2,1)} %blocks.3) | copy-start | bytes 6291460
  118.8 53.8 %all-to-all-start.1 = ((bf16[8,4,256,128]{3,2,1,0:T(8,128)(2,1)}), bf16[8,4,256,128]{3,2,1,0:T(8,128)(2,1)S(1)}, u32[]{:S(2)}, u32[]{:S(2)}) async-start(bf16[8,4,256,128]{3,2,1,0:T(8,128)(2,1)} %bitcast.17), calls=%async_computation.1 | async-start | bytes 4194304 | tf_op jit(solution)/shard_map/all_to_all | solution.py:542
  123.2 9.6 %copy-start.14 = (bf16[32,256,128]{2,1,0:T(8,128)(2,1)S(1)}, bf16[32,256,128]{2,1,0:T(8,128)(2,1)}, u32[]{:S(2)}) copy-start(bf16[32,256,128]{2,1,0:T(8,128)(2,1)} %blocks.4) | copy-start | bytes 6291460
  129.4 41.9 %collective-permute-start.8 = (bf16[2,2,128,1024]{3,2,1,0:T(8,128)(2,1)S(1)}, bf16[2,2,128,1024]{3,2,1,0:T(8,128)(2,1)S(1)}, u32[]{:S(2)}, u32[]{:S(2)}) collective-permute-start(bf16[2,2,128,1024]{3,2,1,0:T(8,128)(2,1)S(1)} %get-tuple-element.74), channel_id=1, source_target_pairs={{0,2},{2,0},{4,6},{6,4},{1,3},{3,1},{5,7},{7,5},{8,10},{10,8},{12,... | collective-permute-start | bytes 3145736 | tf_op jit(solution)/shard_map/ppermute | solution.py:442
  131.4 49.3 %collective-permute-start.10 = (bf16[2,2,128,1024]{3,2,1,0:T(8,128)(2,1)}, bf16[2,2,128,1024]{3,2,1,0:T(8,128)(2,1)}, u32[]{:S(2)}, u32[]{:S(2)}) collective-permute-start(bf16[2,2,128,1024]{3,2,1,0:T(8,128)(2,1)} %get-tuple-element.76), channel_id=1, source_target_pairs={{0,4},{2,6},{4,0},{6,2},{1,5},{3,7},{5,1},{7,3},{8,12},{10,14},{12... | collective-permute-start | bytes 3145736 | tf_op jit(solution)/shard_map/ppermute | solution.py:442
  140.1 1.3 copy-start.6
  174.0 44.5 %all-to-all-start.2 = ((bf16[8,4,256,128]{3,2,1,0:T(8,128)(2,1)}), bf16[8,4,256,128]{3,2,1,0:T(8,128)(2,1)S(1)}, u32[]{:S(2)}, u32[]{:S(2)}) async-start(bf16[8,4,256,128]{3,2,1,0:T(8,128)(2,1)} %bitcast.99), calls=%async_computation.2 | async-start | bytes 4194304 | tf_op jit(solution)/shard_map/all_to_all | solution.py:542
  178.7 35.8 %collective-permute-start.9 = (bf16[2,128,1024]{2,1,0:T(8,128)(2,1)S(1)}, bf16[2,128,1024]{2,1,0:T(8,128)(2,1)S(1)}, u32[]{:S(2)}, u32[]{:S(2)}) collective-permute-start(bf16[2,128,1024]{2,1,0:T(8,128)(2,1)S(1)} %slice_bitcast_fusion.2), channel_id=1, source_target_pairs={{0,4},{2,6},{4,0},{6,2},{1,5},{3,7},{5,1},{7,3},{8,12},{10,14},{12... | collective-permute-start | bytes 1572872 | tf_op jit(solution)/shard_map/ppermute | solution.py:442
  180.7 33.8 %copy-start.27 = (bf16[2,2,128,1024]{3,2,1,0:T(8,128)(2,1)S(1)}, bf16[2,2,128,1024]{3,2,1,0:T(8,128)(2,1)}, u32[]{:S(2)}) copy-start(bf16[2,2,128,1024]{3,2,1,0:T(8,128)(2,1)} %add_convert_fusion.1) | copy-start | bytes 3145732
  182.4 32.2 %collective-permute-start.11 = (bf16[2,128,1024]{2,1,0:T(8,128)(2,1)S(1)}, bf16[2,128,1024]{2,1,0:T(8,128)(2,1)S(1)}, u32[]{:S(2)}, u32[]{:S(2)}) collective-permute-start(bf16[2,128,1024]{2,1,0:T(8,128)(2,1)S(1)} %slice_bitcast_fusion), channel_id=1, source_target_pairs={{0,2},{2,0},{4,6},{6,4},{1,3},{3,1},{5,7},{7,5},{8,10},{10,8},{12,... | collective-permute-start | bytes 1572872 | tf_op jit(solution)/shard_map/ppermute | solution.py:442
  214.9 3.5 copy-start.26
  218.4 35.2 %all-to-all-start.3 = ((bf16[8,4,256,128]{3,2,1,0:T(8,128)(2,1)}), bf16[8,4,256,128]{3,2,1,0:T(8,128)(2,1)}, u32[]{:S(2)}, u32[]{:S(2)}) async-start(bf16[8,4,256,128]{3,2,1,0:T(8,128)(2,1)} %bitcast_bitcast_fusion), calls=%async_computation.3 | async-start | bytes 4194304 | tf_op jit(solution)/shard_map/all_to_all | solution.py:542
  222.8 2.7 copy-start.25
  224.2 28.1 %collective-permute-start.12 = (bf16[4,4,256,128]{3,2,1,0:T(8,128)(2,1)S(1)}, bf16[4,4,256,128]{3,2,1,0:T(8,128)(2,1)S(1)}, u32[]{:S(2)}, u32[]{:S(2)}) collective-permute-start(bf16[4,4,256,128]{3,2,1,0:T(8,128)(2,1)S(1)} %slice.165), channel_id=1, source_target_pairs={{8,0},{16,8},{24,16},{9,1},{17,9},{25,17},{10,2},{18,10},{26,18},{... | collective-permute-start | bytes 3145736 | tf_op jit(solution)/shard_map/ppermute | solution.py:321
  225.7 28.0 %collective-permute-start.13 = (bf16[4,4,256,128]{3,2,1,0:T(8,128)(2,1)S(1)}, bf16[4,4,256,128]{3,2,1,0:T(8,128)(2,1)}, u32[]{:S(2)}, u32[]{:S(2)}) collective-permute-start(bf16[4,4,256,128]{3,2,1,0:T(8,128)(2,1)S(1)} %slice.166), channel_id=1, source_target_pairs={{0,8},{8,16},{16,24},{1,9},{9,17},{17,25},{2,10},{10,18},{18,26},{... | collective-permute-start | bytes 3145736 | tf_op jit(solution)/shard_map/ppermute | solution.py:321
  253.6 2.2 copy-start.1
  267.8 108.7 %all-to-all-start.4 = ((bf16[8,2,2,1024,128]{4,3,2,1,0:T(8,128)(2,1)}), bf16[8,2,2,1024,128]{4,3,2,1,0:T(8,128)(2,1)}, u32[]{:S(2)}, u32[]{:S(2)}) async-start(bf16[8,2,2,1024,128]{4,3,2,1,0:T(8,128)(2,1)} %shard_map.206), calls=%async_computation.4 | async-start | bytes 16777216 | tf_op jit(solution)/shard_map/all_to_all | solution.py:584
  272.7 9.1 %copy-start.34 = (s32[32]{0:T(128)S(1)}, s32[32]{0:T(128)}, u32[]{:S(2)}) copy-start(s32[32]{0:T(128)} %param.25) | copy-start | bytes 388
  272.8 88.6 %all-gather.7.cloned.1.call-start = ((), (), s32[]{:S(2)}) async-start(), calls=%async_computation.8 | async-start | bytes 5242880 | tf_op jit(solution)/shard_map/all_gather | solution.py:569
  274.2 28.3 %collective-permute-start.14 = (bf16[2,4,256,128]{3,2,1,0:T(8,128)(2,1)S(1)}, bf16[2,4,256,128]{3,2,1,0:T(8,128)(2,1)S(1)}, u32[]{:S(2)}, u32[]{:S(2)}) collective-permute-start(bf16[2,4,256,128]{3,2,1,0:T(8,128)(2,1)S(1)} %slice.167), channel_id=1, source_target_pairs={{8,0},{16,8},{24,16},{9,1},{17,9},{25,17},{10,2},{18,10},{26,18},{... | collective-permute-start | bytes 1572872 | tf_op jit(solution)/shard_map/ppermute | solution.py:321
  276.6 25.9 %collective-permute-start.15 = (bf16[2,4,256,128]{3,2,1,0:T(8,128)(2,1)S(1)}, bf16[2,4,256,128]{3,2,1,0:T(8,128)(2,1)S(1)}, u32[]{:S(2)}, u32[]{:S(2)}) collective-permute-start(bf16[2,4,256,128]{3,2,1,0:T(8,128)(2,1)S(1)} %slice.168), channel_id=1, source_target_pairs={{0,8},{8,16},{16,24},{1,9},{9,17},{17,25},{2,10},{10,18},{18,26},{... | collective-permute-start | bytes 1572872 | tf_op jit(solution)/shard_map/ppermute | solution.py:321
  281.9 20.6 %copy-start.4 = (bf16[6,4,256,128]{3,2,1,0:T(8,128)(2,1)S(1)}, bf16[6,4,256,128]{3,2,1,0:T(8,128)(2,1)}, u32[]{:S(2)}) copy-start(bf16[6,4,256,128]{3,2,1,0:T(8,128)(2,1)} %copy-done.3) | copy-start | bytes 4718596
  361.7 8.4 %copy-start.5 = (bf16[6,4,256,128]{3,2,1,0:T(8,128)(2,1)S(1)}, bf16[6,4,256,128]{3,2,1,0:T(8,128)(2,1)}, u32[]{:S(2)}) copy-start(bf16[6,4,256,128]{3,2,1,0:T(8,128)(2,1)} %copy-done.3) | copy-start | bytes 4718596
  361.7 8.4 %copy-start.9 = (bf16[2,4,256,128]{3,2,1,0:T(8,128)(2,1)S(1)}, bf16[2,4,256,128]{3,2,1,0:T(8,128)(2,1)}, u32[]{:S(2)}) copy-start(bf16[2,4,256,128]{3,2,1,0:T(8,128)(2,1)} %copy-done.8) | copy-start | bytes 1572868
  361.7 8.4 %copy-start.11 = (bf16[2,4,256,128]{3,2,1,0:T(8,128)(2,1)S(1)}, bf16[2,4,256,128]{3,2,1,0:T(8,128)(2,1)}, u32[]{:S(2)}) copy-start(bf16[2,4,256,128]{3,2,1,0:T(8,128)(2,1)} %copy-done.10) | copy-start | bytes 1572868
  368.0 2.1 copy-start.2
  391.6 113.1 %all-to-all-start.6 = ((bf16[8,1,2,1024,128]{4,3,2,1,0:T(8,128)(2,1)}), bf16[8,1,2,1024,128]{4,3,2,1,0:T(8,128)(2,1)}, u32[]{:S(2)}, u32[]{:S(2)}) async-start(bf16[8,1,2,1024,128]{4,3,2,1,0:T(8,128)(2,1)} %copy-done.2), calls=%async_computation.6 | async-start | bytes 8388608 | tf_op jit(solution)/shard_map/all_to_all | solution.py:618
  397.9 3.0 copy-start.16
  399.0 68.2 %collective-permute-start.17 = (bf16[2,256,1024]{2,1,0:T(8,128)(2,1)S(1)}, bf16[2,256,1024]{2,1,0:T(8,128)(2,1)}, u32[]{:S(2)}, u32[]{:S(2)}) collective-permute-start(bf16[2,256,1024]{2,1,0:T(8,128)(2,1)S(1)} %shard_map.212.refs_1_), channel_id=1, source_target_pairs={{0,4},{2,6},{4,0},{6,2},{1,5},{3,7},{5,1},{7,3},{8,12},{10,14},{12... | collective-permute-start | bytes 3145736 | tf_op jit(solution)/shard_map/ppermute | solution.py:442
  402.8 64.5 %collective-permute-start.16 = (bf16[2,256,1024]{2,1,0:T(8,128)(2,1)}, bf16[2,256,1024]{2,1,0:T(8,128)(2,1)S(1)}, u32[]{:S(2)}, u32[]{:S(2)}) collective-permute-start(bf16[2,256,1024]{2,1,0:T(8,128)(2,1)} %shard_map.211.refs_0_), channel_id=1, source_target_pairs={{0,2},{2,0},{4,6},{6,4},{1,3},{3,1},{5,7},{7,5},{8,10},{10,8},{12,... | collective-permute-start | bytes 3145736 | tf_op jit(solution)/shard_map/ppermute | solution.py:442
  404.3 85.1 %collective-permute-start.20 = (bf16[2,256,1024]{2,1,0:T(8,128)(2,1)S(1)}, bf16[2,256,1024]{2,1,0:T(8,128)(2,1)}, u32[]{:S(2)}, u32[]{:S(2)}) collective-permute-start(bf16[2,256,1024]{2,1,0:T(8,128)(2,1)S(1)} %shard_map.212.refs_1_), channel_id=1, source_target_pairs={{0,2},{2,0},{4,6},{6,4},{1,3},{3,1},{5,7},{7,5},{8,10},{10,8},{12,... | collective-permute-start | bytes 3145736 | tf_op jit(solution)/shard_map/ppermute | solution.py:442
  404.8 84.5 %collective-permute-start.23 = (bf16[2,256,1024]{2,1,0:T(8,128)(2,1)S(1)}, bf16[2,256,1024]{2,1,0:T(8,128)(2,1)S(1)}, u32[]{:S(2)}, u32[]{:S(2)}) collective-permute-start(bf16[2,256,1024]{2,1,0:T(8,128)(2,1)S(1)} %shard_map.212.refs_1_), channel_id=1, source_target_pairs={{0,1},{1,0},{2,3},{3,2},{4,5},{5,4},{6,7},{7,6},{8,9},{9,8},{10,11... | collective-permute-start | bytes 3145736 | tf_op jit(solution)/shard_map/ppermute | solution.py:446
  424.3 65.6 %collective-permute-start.21 = (bf16[2,256,1024]{2,1,0:T(8,128)(2,1)}, bf16[2,256,1024]{2,1,0:T(8,128)(2,1)}, u32[]{:S(2)}, u32[]{:S(2)}) collective-permute-start(bf16[2,256,1024]{2,1,0:T(8,128)(2,1)} %shard_map.211.refs_0_), channel_id=1, source_target_pairs={{0,4},{2,6},{4,0},{6,2},{1,5},{3,7},{5,1},{7,3},{8,12},{10,14},{12... | collective-permute-start | bytes 3145736 | tf_op jit(solution)/shard_map/ppermute | solution.py:442
  467.3 22.7 %collective-permute-start.22 = (bf16[2,256,1024]{2,1,0:T(8,128)(2,1)}, bf16[2,256,1024]{2,1,0:T(8,128)(2,1)}, u32[]{:S(2)}, u32[]{:S(2)}) collective-permute-start(bf16[2,256,1024]{2,1,0:T(8,128)(2,1)} %shard_map.211.refs_0_), channel_id=1, source_target_pairs={{0,1},{1,0},{2,3},{3,2},{4,5},{5,4},{6,7},{7,6},{8,9},{9,8},{10,11... | collective-permute-start | bytes 3145736 | tf_op jit(solution)/shard_map/ppermute | solution.py:446
  467.3 24.2 %collective-permute-start.24 = (bf16[2,256,1024]{2,1,0:T(8,128)(2,1)S(1)}, bf16[2,256,1024]{2,1,0:T(8,128)(2,1)S(1)}, u32[]{:S(2)}, u32[]{:S(2)}) collective-permute-start(bf16[2,256,1024]{2,1,0:T(8,128)(2,1)S(1)} %collective-permute-done.16.refs_2_), channel_id=1, source_target_pairs={{0,1},{1,0},{2,3},{3,2},{4,5},{5,4},{6,7},{7,6},{8,9},{9,8},{10,11... | collective-permute-start | bytes 3145736 | tf_op jit(solution)/shard_map/ppermute | solution.py:446
  489.4 5.2 collective-permute-start.27
  489.4 2.1 copy-start.28
  489.4 5.2 collective-permute-start.25
  489.9 5.5 %collective-permute-start.26 = (bf16[2,256,1024]{2,1,0:T(8,128)(2,1)}, bf16[2,256,1024]{2,1,0:T(8,128)(2,1)}, u32[]{:S(2)}, u32[]{:S(2)}) collective-permute-start(bf16[2,256,1024]{2,1,0:T(8,128)(2,1)} %collective-permute-done.21.refs_4_), channel_id=1, source_target_pairs={{0,1},{1,0},{2,3},{3,2},{4,5},{5,4},{6,7},{7,6},{8,9},{9,8},{10,11... | collective-permute-start | bytes 3145736 | tf_op jit(solution)/shard_map/ppermute | solution.py:446
  490.0 25.5 %collective-permute-start.18 = (bf16[2,256,1024]{2,1,0:T(8,128)(2,1)S(1)}, bf16[2,256,1024]{2,1,0:T(8,128)(2,1)S(1)}, u32[]{:S(2)}, u32[]{:S(2)}) collective-permute-start(bf16[2,256,1024]{2,1,0:T(8,128)(2,1)S(1)} %collective-permute-done.16.refs_2_), channel_id=1, source_target_pairs={{0,4},{2,6},{4,0},{6,2},{1,5},{3,7},{5,1},{7,3},{8,12},{10,14},{12... | collective-permute-start | bytes 3145736 | tf_op jit(solution)/shard_map/ppermute | solution.py:442
  492.5 25.5 %collective-permute-start.19 = (bf16[2,256,1024]{2,1,0:T(8,128)(2,1)}, bf16[2,256,1024]{2,1,0:T(8,128)(2,1)}, u32[]{:S(2)}, u32[]{:S(2)}) collective-permute-start(bf16[2,256,1024]{2,1,0:T(8,128)(2,1)} %collective-permute-done.17.refs_5_), channel_id=1, source_target_pairs={{0,2},{2,0},{4,6},{6,4},{1,3},{3,1},{5,7},{7,5},{8,10},{10,8},{12,... | collective-permute-start | bytes 3145736 | tf_op jit(solution)/shard_map/ppermute | solution.py:442
  504.7 14.0 %copy-start.30 = (f32[208,256]{1,0:T(8,128)S(1)}, f32[208,256]{1,0:T(8,128)}, u32[]{:S(2)}) copy-start(f32[208,256]{1,0:T(8,128)} %param.26) | copy-start | bytes 638980
  504.7 14.0 %copy-start.31 = (f32[208,256]{1,0:T(8,128)S(1)}, f32[208,256]{1,0:T(8,128)}, u32[]{:S(2)}) copy-start(f32[208,256]{1,0:T(8,128)} %param.28) | copy-start | bytes 638980
  504.8 13.9 %copy-start.32 = (f32[208,256]{1,0:T(8,128)S(1)}, f32[208,256]{1,0:T(8,128)}, u32[]{:S(2)}) copy-start(f32[208,256]{1,0:T(8,128)} %param.29) | copy-start | bytes 638980
  504.8 13.9 %copy-start.33 = (bf16[208,256]{1,0:T(8,128)(2,1)S(1)}, bf16[208,256]{1,0:T(8,128)(2,1)}, u32[]{:S(2)}) copy-start(bf16[208,256]{1,0:T(8,128)(2,1)} %param.27) | copy-start | bytes 319492
  518.0 4.1 collective-permute-start.28
  518.0 4.4 collective-permute-start.29
  (9 other events, 9.1 us)
Sparse Core Ops, SparseCore 0:
  113.7 83.4 all-gather.4
  275.2 86.1 all-gather.6

commit v3 on v2

--- a/solution.py
+++ b/solution.py
@@ -364,34 +364,35 @@
     )(lax.axis_index("shard").reshape(1), left, grad_blocks, *rights)
 
 
-def update_kernel(scale, weights, precond, out):
-    slabs = weights.shape[0]
+def update_kernel(me, scale, precond, *refs):
+    weights, out = refs[:-1], refs[-1]
     factor = scale[pl.program_id(0)]
-    old = jnp.concatenate([weights[s, 0] for s in range(slabs)], axis=1).astype(jnp.float32)
-    step = factor * precond[0].astype(jnp.float32) + DECAY_RATE * old
-    out[0] = (old - LEARNING * step).astype(jnp.bfloat16)
-
-
-def update(weights, start, precond, scale):
-    slabs, _, rows, cols = weights.shape
-    count = precond.shape[0]
-    width = slabs * cols
-    own = pl.BlockSpec((1, rows, width), lambda m, scale: (m, 0, 0))
+    cols = weights[0].shape[2]
+    for k, slab in enumerate(weights):
+        here = pl.ds(pl.multiple_of((me[0] ^ k) * cols, cols), cols)
+        old = slab[0].astype(jnp.float32)
+        step = factor * precond[0, :, here].astype(jnp.float32) + DECAY_RATE * old
+        out[0, :, here] = (old - LEARNING * step).astype(jnp.bfloat16)
+
+
+def update(weights, start, precond, scale, me):
+    count, rows, width = precond.shape
+    cols = weights[0].shape[2]
+    own = pl.BlockSpec((1, rows, width), lambda m, me, scale: (m, 0, 0))
     return pl.pallas_call(
         update_kernel,
         grid_spec=pltpu.PrefetchScalarGridSpec(
-            num_scalar_prefetch=1,
+            num_scalar_prefetch=2,
             grid=(count,),
-            in_specs=[
-                pl.BlockSpec((slabs, 1, rows, cols), lambda m, scale: (0, start + m, 0, 0)),
-                own,
-            ],
+            in_specs=[own]
+            + [pl.BlockSpec((1, rows, cols), lambda m, me, scale: (0, start + m, 0))]
+            * len(weights),
             out_specs=own,
         ),
         out_shape=jax.ShapeDtypeStruct((count, rows, width), jnp.bfloat16),
         compiler_params=params(),
         cost_estimate=SMALL,
-    )(scale, weights, precond)
+    )(me.reshape(1), scale, precond, *weights)
 
 
 def pair_kernel(picked, first, second, third, fourth, received, send_a, keep_a, send_b, keep_b):
@@ -568,28 +569,37 @@
     gradient = [lax.optimization_barrier(part) for part in gradient]
     grad_blocks = [lax.all_gather(part, "shard", axis=0) for part in gradient]
     left_dealt = deal(reorder(left_root, order))
-    weights_dealt = deal(reorder(weights, order))
+    partners = jnp.arange(group, dtype=jnp.int32) ^ group_index
+    weights_sent = reorder(weights, by_entry[partners].reshape(-1))
     tiles = jnp.concatenate(gradient, axis=0).reshape(per, rows, group, cols)
     tiles = deal(jnp.transpose(tiles, (2, 0, 1, 3)))
 
     if early:
-        grad_blocks[0], left_dealt, weights_dealt, tiles, rights = lax.optimization_barrier(
-            (grad_blocks[0], left_dealt, weights_dealt, tiles, rights)
+        grad_blocks[0], left_dealt, weights_sent, tiles, rights = lax.optimization_barrier(
+            (grad_blocks[0], left_dealt, weights_sent, tiles, rights)
         )
         if len(rights) == 2:
             downs, ups = zip(*rights, next_hop(rights[1], group // owner_count))
             rights = [right_dealt, *downs, *ups]
         slabs = grams(grad_blocks[0], jnp.arange(early, dtype=jnp.int32))
-        slabs, left_dealt, tiles = lax.optimization_barrier((slabs, left_dealt, tiles))
+        slabs, left_dealt, tiles, weights_sent = lax.optimization_barrier(
+            (slabs, left_dealt, tiles, weights_sent)
+        )
         received = lax.all_to_all(slabs, GROUP, split_axis=0, concat_axis=0, tiled=True)
     adam_m_new, adam_v_new, adam_total = adam(
         tiles.reshape(blocks, rows, cols), place, adam_m, adam_v
     )
+    away = weights_sent.reshape(group, per * rows, cols)
+    away = [away[:1]] + [
+        lax.ppermute(away[k : k + 1], GROUP, [(g, g ^ k) for g in range(group)])
+        for k in range(1, group)
+    ]
     pieces = [precondition(left_dealt, 0, grad_blocks[0], rights)]
     if early:
-        grad_blocks[1], adam_total, pieces[0] = lax.optimization_barrier(
-            (grad_blocks[1], adam_total, pieces[0])
+        grad_blocks[1], adam_total, pieces[0], away = lax.optimization_barrier(
+            (grad_blocks[1], adam_total, pieces[0], away)
         )
+    if early:
         pieces.append(precondition(left_dealt, early, grad_blocks[1], rights))
     entry = jnp.where(is_heavy, early, own_entry) - early
     last_slabs = grams(grad_blocks[-1], jnp.clip(entry, 0, per - 1 - early).reshape(1))
@@ -617,7 +627,7 @@
 
     last = lax.all_to_all(last_slabs, GROUP, split_axis=0, concat_axis=0, tiled=True)
     updated = [
-        update(weights_dealt, a, piece, block_scale[a:b])
+        update(away, a, piece, block_scale[a:b], group_index)
         for (a, b), (piece, _) in zip(cuts, pieces)
     ]
     if len(updated) == 1:

time: 535 us -> 541 us (1.011)
  local copies, waits for them, and re-layouts: 23.5 us -> 31.3 us
  starting transfers between devices: 68.5 us -> 75.7 us
  waiting for transfers between devices: 255 us -> 249 us
    ppermute x0 -> x7, waiting for transfers between devices: none -> 80.9 us  [shards(): lax.ppermute(away[k:k + 1], GROUP, [(g, g ^ k) for g in range(group)])]
    all_gather x2, waiting for transfers between devices: 51.2 us -> 0.01 us  [shards(): grad_blocks = [lax.all_gather(part, 'shard', axis=0) for part in gradient]]
    ppermute x14, waiting for transfers between devices: 161 us -> 136 us  [swap(): return lax.ppermute(array, 'tensor', [(t, t ^ bit) for t in range(devices)])]
    ppermute x3, waiting for transfers between devices: 22.8 us -> 13.9 us  [hop(): lax.ppermute(moved[0], 'shard', down)]
    ppermute x0 -> x7, starting transfers between devices: none -> 7.65 us  [shards(): lax.ppermute(away[k:k + 1], GROUP, [(g, g ^ k) for g in range(group)])]
    all_to_all x4 -> x3, starting transfers between devices: 17 us -> 13.7 us  [deal(): lax.all_to_all(tiles.reshape(group, per, rows, cols), GROUP, split_axis=0...]
    unnamed x70 -> x80, local copies, waits for them, and re-layouts: 16.1 us -> 19 us
    all_to_all x4 -> x3, waiting for transfers between devices: 11.6 us -> 11.6 us  [deal(): lax.all_to_all(tiles.reshape(group, per, rows, cols), GROUP, split_axis=0...]
  transfers between devices with their start and end apart: 38 -> 44, of which waited for: 19 -> 18; matrix products, arithmetic and copies ran while one was open for 4% -> 4% of each run, Pallas kernels for 22% -> 22%
where the time goes in v3:
time: 541 us; the launch traced here: 539 us
  waiting for transfers between devices  249 us (46%)
  Pallas kernels  137 us (25%)
  starting transfers between devices  75.7 us (14%)
  local copies, waits for them, and re-layouts  31.3 us (6%)
  other arithmetic  17.6 us (3%)
  between operations  16.1 us (3%)
  blocking collectives  12.7 us (2%)
    ppermute x14, waiting for transfers between devices, swap(): return lax.ppermute(array, 'tensor', [(t, t ^ bit) for t in range(devices)])  136 us
    ppermute x7, waiting for transfers between devices, shards(): lax.ppermute(away[k:k + 1], GROUP, [(g, g ^ k) for g in range(group)])  80.9 us
    pallas_call x7, Pallas kernels, reorder(): pl.pallas_call(reorder_kernel, grid_spec=pltpu.PrefetchScalarGridSpec(num...  29.8 us
    pallas_call x2, Pallas kernels, refresh(): pl.pallas_call(stat_kernel, grid_spec=pltpu.PrefetchScalarGridSpec(num_sc...  29.7 us
    ppermute x14, starting transfers between devices, swap(): return lax.ppermute(array, 'tensor', [(t, t ^ bit) for t in range(devices)])  21.5 us
    pallas_call x1, Pallas kernels, adam(): pl.pallas_call(adam_kernel, grid_spec=pltpu.PrefetchScalarGridSpec(num_sc...  20.4 us
    unnamed x80, local copies, waits for them, and re-layouts  19 us
    pallas_call x2, Pallas kernels, grams(): pl.pallas_call(gram_kernel, grid_spec=pltpu.PrefetchScalarGridSpec(num_sc...  18.1 us
  transfers between devices with their start and end apart: 44, of which 18 were waited for; matrix products, arithmetic and copies ran while one was open for 4% of the time, Pallas kernels for 22%

profile of v3, /device:TPU:0, one launch (start us, length us, event | category | flops | bytes accessed | tf_op | source)
XLA Modules:
  0.0 539.1 jit_solution(11597973476721735187)
XLA Ops:
  10.5 2.0 fusion.18
  14.4 4.2 shard_map.197
  19.1 7.3 %shard_map.199 = bf16[32,256,128]{2,1,0:T(8,128)(2,1)S(1)} custom-call(s32[32]{0:T(128)S(1)} %select_reduce_fusion.order, bf16[32,256,128]{2,1,0:T(8,128)(2,1)S(1)} %copy-done.7), custom_call_target="tpu_custom_call" | custom-call | tf_op jit(solution)/shard_map/pallas_call | solution.py:72
  27.7 4.8 all-to-all-start
  34.2 4.1 shard_map.200
  38.3 5.4 %shard_map.198 = (bf16[2,2,128,1024]{3,2,1,0:T(8,128)(2,1)S(1)}, bf16[2,2,128,1024]{3,2,1,0:T(8,128)(2,1)S(1)}, bf16[2,2,128,1024]{3,2,1,0:T(8,128)(2,1)}, bf16[2,2,128,1024]{3,2,1,0:T(8,128)(2,1)S(1)}) custom-call(s32[8]{0:T(128)S(1)} %reshape.214.picked, bf16[32,256,1024]{2,1,0:T(8,128)(2,1)} %bitcast.116, bf16[32,256,1024]{2,1,0:T(8,128)(2,1)} %bitcast.117, ...), custom_call_target="tpu_custom_call" | custom-call | tf_op jit(solution)/shard_map/pallas_call | solution.py:422
  45.7 2.0 collective-permute-start.2
  47.7 11.6 %all-to-all-done.refs_0_ = bf16[8,4,256,128]{3,2,1,0:T(8,128)(2,1)S(1)} async-done(((bf16[8,4,256,128]{3,2,1,0:T(8,128)(2,1)}), bf16[8,4,256,128]{3,2,1,0:T(8,128)(2,1)S(1)}, u32[]{:S(2)}, u32[]{:S(2)}) %all-to-all-start) | async-done | bytes 2097184 | tf_op jit(solution)/shard_map/all_to_all | solution.py:543
  62.6 4.6 collective-permute-start.4
  67.8 13.0 %collective-permute-done.2 = bf16[2,2,128,1024]{3,2,1,0:T(8,128)(2,1)} collective-permute-done((bf16[2,2,128,1024]{3,2,1,0:T(8,128)(2,1)}, bf16[2,2,128,1024]{3,2,1,0:T(8,128)(2,1)}, u32[]{:S(2)}, u32[]{:S(2)}) %collective-permute-start.2) | collective-permute-done | bytes 1048608 | tf_op jit(solution)/shard_map/ppermute | solution.py:443
  80.8 1.6 add_convert_fusion.2
  82.5 10.4 %collective-permute-done.1 = bf16[2,2,128,1024]{3,2,1,0:T(8,128)(2,1)S(1)} collective-permute-done((bf16[2,2,128,1024]{3,2,1,0:T(8,128)(2,1)S(1)}, bf16[2,2,128,1024]{3,2,1,0:T(8,128)(2,1)S(1)}, u32[]{:S(2)}, u32[]{:S(2)}) %collective-permute-start.1) | collective-permute-done | bytes 1048608 | tf_op jit(solution)/shard_map/ppermute | solution.py:443
  93.3 2.2 collective-permute-done.3.refs_1_
  95.5 2.1 collective-permute-done.4.refs_4_
  99.1 2.6 collective-permute-start.6
  101.7 6.0 %collective-permute-done.5 = bf16[2,128,1024]{2,1,0:T(8,128)(2,1)S(1)} collective-permute-done((bf16[2,128,1024]{2,1,0:T(8,128)(2,1)S(1)}, bf16[2,128,1024]{2,1,0:T(8,128)(2,1)S(1)}, u32[]{:S(2)}, u32[]{:S(2)}) %collective-permute-start.5) | collective-permute-done | bytes 524320 | tf_op jit(solution)/shard_map/ppermute | solution.py:443
  107.9 4.4 collective-permute-done.6
  113.8 5.4 %shard_map.205 = (bf16[2,2,128,1024]{3,2,1,0:T(8,128)(2,1)}, bf16[2,2,128,1024]{3,2,1,0:T(8,128)(2,1)S(1)}, bf16[2,2,128,1024]{3,2,1,0:T(8,128)(2,1)S(1)}, bf16[2,2,128,1024]{3,2,1,0:T(8,128)(2,1)S(1)}) custom-call(s32[8]{0:T(128)S(1)} %reshape.223.picked, bf16[32,256,1024]{2,1,0:T(8,128)(2,1)} %bitcast.120, bf16[32,256,1024]{2,1,0:T(8,128)(2,1)} %bitcast.121, ...), custom_call_target="tpu_custom_call" | custom-call | tf_op jit(solution)/shard_map/pallas_call | solution.py:422
  119.2 1.8 collective-permute-start.8
  121.0 1.6 collective-permute-start.10
  122.7 5.2 shard_map.203
  127.9 4.4 all-to-all-start.1
  132.2 13.4 %collective-permute-done.8 = bf16[2,2,128,1024]{3,2,1,0:T(8,128)(2,1)} collective-permute-done((bf16[2,2,128,1024]{3,2,1,0:T(8,128)(2,1)}, bf16[2,2,128,1024]{3,2,1,0:T(8,128)(2,1)}, u32[]{:S(2)}, u32[]{:S(2)}) %collective-permute-start.8) | collective-permute-done | bytes 1048608 | tf_op jit(solution)/shard_map/ppermute | solution.py:443
  145.6 1.6 add_convert_fusion.1
  147.3 1.8 collective-permute-start.9
  149.1 1.6 add_convert_fusion
  150.8 3.5 collective-permute-start.11
  154.3 23.2 %collective-permute-done.9 = bf16[2,128,1024]{2,1,0:T(8,128)(2,1)S(1)} collective-permute-done((bf16[2,128,1024]{2,1,0:T(8,128)(2,1)S(1)}, bf16[2,128,1024]{2,1,0:T(8,128)(2,1)S(1)}, u32[]{:S(2)}, u32[]{:S(2)}) %collective-permute-start.9) | collective-permute-done | bytes 524320 | tf_op jit(solution)/shard_map/ppermute | solution.py:443
  179.0 1.9 bitcast_bitcast_fusion
  180.9 4.5 all-to-all-start.2
  188.8 6.0 %collective-permute-start.13 = (bf16[4,4,256,128]{3,2,1,0:T(8,128)(2,1)}, bf16[4,4,256,128]{3,2,1,0:T(8,128)(2,1)}, u32[]{:S(2)}, u32[]{:S(2)}) collective-permute-start(bf16[4,4,256,128]{3,2,1,0:T(8,128)(2,1)} %slice.214), channel_id=1, source_target_pairs={{0,8},{8,16},{16,24},{1,9},{9,17},{17,25},{2,10},{10,18},{18,26},{... | collective-permute-start | bytes 3145736 | tf_op jit(solution)/shard_map/ppermute | solution.py:321
  195.5 1.6 copy-done.9
  197.1 7.3 %shard_map.204 = bf16[32,256,128]{2,1,0:T(8,128)(2,1)S(1)} custom-call(s32[32]{0:T(128)S(1)} %reshape.222.order, bf16[32,256,128]{2,1,0:T(8,128)(2,1)S(1)} %copy-done.9), custom_call_target="tpu_custom_call" | custom-call | tf_op jit(solution)/shard_map/pallas_call | solution.py:72
  205.7 11.7 %collective-permute-done.12.refs_2_ = bf16[4,4,256,128]{3,2,1,0:T(8,128)(2,1)S(1)} collective-permute-done((bf16[4,4,256,128]{3,2,1,0:T(8,128)(2,1)}, bf16[4,4,256,128]{3,2,1,0:T(8,128)(2,1)S(1)}, u32[]{:S(2)}, u32[]{:S(2)}) %collective-permute-start.12) | collective-permute-done | bytes 1048608 | tf_op jit(solution)/shard_map/ppermute | solution.py:321
  217.4 2.2 copy-done.1
  219.6 12.0 %shard_map.206 = bf16[8,2,2,1024,128]{4,3,2,1,0:T(8,128)(2,1)} custom-call(s32[2]{0:T(128)S(1)} %iota.55.chosen, bf16[4,2,256,1024]{3,2,1,0:T(8,128)(2,1)S(1)} %bitcast.108), custom_call_target="tpu_custom_call" | custom-call | tf_op jit(solution)/shard_map/pallas_call | solution.py:177
  231.5 5.0 all-to-all-start.3
  239.4 1.9 slice.216
  241.3 6.0 %collective-permute-start.15 = (bf16[2,4,256,128]{3,2,1,0:T(8,128)(2,1)}, bf16[2,4,256,128]{3,2,1,0:T(8,128)(2,1)}, u32[]{:S(2)}, u32[]{:S(2)}) collective-permute-start(bf16[2,4,256,128]{3,2,1,0:T(8,128)(2,1)} %slice.216), channel_id=1, source_target_pairs={{0,8},{8,16},{16,24},{1,9},{9,17},{17,25},{2,10},{10,18},{18,26},{... | collective-permute-start | bytes 1572872 | tf_op jit(solution)/shard_map/ppermute | solution.py:321
  247.4 3.0 fusion.27
  250.5 1.8 collective-permute-start.17
  253.2 1.8 collective-permute-start.19
  254.9 80.9 %collective-permute-done.17.refs_2_ = bf16[1,1024,128]{2,1,0:T(8,128)(2,1)} collective-permute-done((bf16[1,1024,128]{2,1,0:T(8,128)(2,1)}, bf16[1,1024,128]{2,1,0:T(8,128)(2,1)}, u32[]{:S(2)}, u32[]{:S(2)}) %collective-permute-start.17) | collective-permute-done | bytes 262176 | tf_op jit(solution)/shard_map/ppermute | solution.py:594
  337.3 2.4 collective-permute-start.22
  339.9 20.4 %shard_map.207 = (f32[32,256,128]{2,1,0:T(8,128)}, f32[32,256,128]{2,1,0:T(8,128)}, f32[32,1,128]{2,1,0:T(1,128)S(1)}) custom-call(s32[32]{0:T(128)S(1)} %fusion.12.place, bf16[32,256,128]{2,1,0:T(8,128)(2,1)} %bitcast.28.grad, f32[32,256,128]{2,1,0:T(8,128)} %moment.1, f32[32,256,128]{2,1,0:T(8,128)} %second.1), custom_call_target="tpu_custom_call" | custom-call | tf_op jit(solution)/shard_map/pallas_call | solution.py:125
  360.2 5.0 shard_map.208
  370.2 6.1 %shard_map.209 = bf16[8,1,2,1024,128]{4,3,2,1,0:T(8,128)(2,1)S(1)} custom-call(s32[1]{0:T(128)} %bitcast.26.chosen, bf16[4,2,256,1024]{3,2,1,0:T(8,128)(2,1)} %bitcast.124), custom_call_target="tpu_custom_call" | custom-call | tf_op jit(solution)/shard_map/pallas_call | solution.py:177
  376.3 2.1 copy-done.2
  378.4 5.0 shard_map.210
  384.8 12.7 %all_to_all.30 = f32[32,8,128]{2,1,0:T(8,128)S(1)} all-to-all(f32[32,8,128]{2,1,0:T(8,128)S(1)} %broadcast_in_dim.47), channel_id=1, replica_groups=mesh['shard'=4,'tensor'=4,'section'=2] {'shard','tensor','section'}, dimensions={0} | all-to-all | bytes 262144 | tf_op jit(solution)/shard_map/all_to_all | solution.py:620
  397.6 4.9 all-to-all-start.5
  403.7 2.3 shard_map.212.refs_1_
  406.0 1.8 collective-permute-start.24
  407.8 2.3 shard_map.211.refs_0_
  410.1 1.5 collective-permute-start.23
  412.2 19.4 %shard_map.213 = (f32[24,1024,128]{2,1,0:T(8,128)}, f32[24,1024,128]{2,1,0:T(8,128)}) custom-call(s32[1]{0:T(128)} %bitcast.42.base, s32[16]{0:T(128)S(1)} %get-tuple-element.190.source, s32[16]{0:T(128)S(1)} %get-tuple-element.189.entry, s32[16]{0:T(128)S(1)} %mul.136.filled, f32[24,1024,128]{2,1,0:T(8,128)} %left_stat.3, f32[24,1024,128]{2,1,0:T(8,128)} %right_stat.3, ...), custom_call_target="tpu_custom_call" | custom-call | tf_op jit(solution)/shard_map/pallas_call | solution.py:212
  431.9 41.5 %collective-permute-done.24.refs_5_ = bf16[2,256,1024]{2,1,0:T(8,128)(2,1)} collective-permute-done((bf16[2,256,1024]{2,1,0:T(8,128)(2,1)S(1)}, bf16[2,256,1024]{2,1,0:T(8,128)(2,1)}, u32[]{:S(2)}, u32[]{:S(2)}) %collective-permute-start.24) | collective-permute-done | bytes 1048608 | tf_op jit(solution)/shard_map/ppermute | solution.py:443
  473.9 21.6 %collective-permute-done.27.refs_3_ = bf16[2,256,1024]{2,1,0:T(8,128)(2,1)} collective-permute-done((bf16[2,256,1024]{2,1,0:T(8,128)(2,1)S(1)}, bf16[2,256,1024]{2,1,0:T(8,128)(2,1)}, u32[]{:S(2)}, u32[]{:S(2)}) %collective-permute-start.27) | collective-permute-done | bytes 1048608 | tf_op jit(solution)/shard_map/ppermute | solution.py:443
  496.1 1.5 collective-permute-start.25
  501.5 9.4 %shard_map.214.refs_4_ = bf16[32,256,1024]{2,1,0:T(8,128)(2,1)} custom-call(s32[24]{0:T(128)S(1)} %concatenate.23.target, bf16[2,256,1024]{2,1,0:T(8,128)(2,1)S(1)} %shard_map.211.refs_0_, bf16[2,256,1024]{2,1,0:T(8,128)(2,1)S(1)} %shard_map.212.refs_1_, bf16[2,256,1024]{2,1,0:T(8,128)(2,1)S(1)} %collective-permute-done.23.refs_2_, ...), custom_call_target="tpu_custom_call" | custom-call | tf_op jit(solution)/shard_map/pallas_call | solution.py:97
  511.0 10.3 %shard_map.215 = (f32[24,1024,128]{2,1,0:T(8,128)}, f32[24,1024,128]{2,1,0:T(8,128)}) custom-call(s32[1]{0:T(128)} %bitcast.55.base, s32[8]{0:T(128)S(1)} %and_select_fusion.source, s32[8]{0:T(128)S(1)} %broadcast.231.entry, s32[8]{0:T(128)S(1)} %compare_convert_fusion.filled, ...), custom_call_target="tpu_custom_call", output_to_operand_aliasing={{0}: (8, {}), {1}: (9, {})} | custom-call | tf_op jit(solution)/shard_map/pallas_call | solution.py:212
  521.7 2.4 collective-permute-done.26.refs_1_
  527.0 1.5 collective-permute-done.36.refs_3_
  528.5 3.7 shard_map.216
  (206 shorter events, 45.6 us)
Async XLA Ops:
  14.4 4.7 copy-start.7
  18.6 19.7 %collective-permute-start = (bf16[8,256,1024]{2,1,0:T(8,128)(2,1)}, bf16[8,256,1024]{2,1,0:T(8,128)(2,1)}, u32[]{:S(2)}, u32[]{:S(2)}) collective-permute-start(bf16[8,256,1024]{2,1,0:T(8,128)(2,1)} %shard_map.197), channel_id=1, source_target_pairs={{0,1},{1,0},{2,3},{3,2},{4,5},{5,4},{6,7},{7,6},{8,9},{9,8},{10,11... | collective-permute-start | bytes 12582920 | tf_op jit(solution)/shard_map/ppermute | solution.py:447
  27.7 31.6 %all-to-all-start = ((bf16[8,4,256,128]{3,2,1,0:T(8,128)(2,1)}), bf16[8,4,256,128]{3,2,1,0:T(8,128)(2,1)S(1)}, u32[]{:S(2)}, u32[]{:S(2)}) async-start(bf16[8,4,256,128]{3,2,1,0:T(8,128)(2,1)} %bitcast.109), calls=%async_computation | async-start | bytes 4194304 | tf_op jit(solution)/shard_map/all_to_all | solution.py:543
  32.6 184.8 %all-gather.5.cloned.1.call-start = ((), (), s32[]{:S(2)}) async-start(), calls=%async_computation.6 | async-start | bytes 5242880 | tf_op jit(solution)/shard_map/all_gather | solution.py:570
  45.7 35.1 %collective-permute-start.2 = (bf16[2,2,128,1024]{3,2,1,0:T(8,128)(2,1)}, bf16[2,2,128,1024]{3,2,1,0:T(8,128)(2,1)}, u32[]{:S(2)}, u32[]{:S(2)}) collective-permute-start(bf16[2,2,128,1024]{3,2,1,0:T(8,128)(2,1)} %get-tuple-element.76), channel_id=1, source_target_pairs={{0,4},{2,6},{4,0},{6,2},{1,5},{3,7},{5,1},{7,3},{8,12},{10,14},{12... | collective-permute-start | bytes 3145736 | tf_op jit(solution)/shard_map/ppermute | solution.py:443
  59.3 3.3 copy-start
  60.2 7.1 %copy-start.27 = (bf16[2,2,128,1024]{3,2,1,0:T(8,128)(2,1)S(1)}, bf16[2,2,128,1024]{3,2,1,0:T(8,128)(2,1)}, u32[]{:S(2)}) copy-start(bf16[2,2,128,1024]{3,2,1,0:T(8,128)(2,1)} %copy-done.26) | copy-start | bytes 3145732
  60.2 20.6 %copy-start.15 = (bf16[2,2,128,1024]{3,2,1,0:T(8,128)(2,1)S(1)}, bf16[2,2,128,1024]{3,2,1,0:T(8,128)(2,1)}, u32[]{:S(2)}) copy-start(bf16[2,2,128,1024]{3,2,1,0:T(8,128)(2,1)} %copy-done.14) | copy-start | bytes 3145732
  60.2 35.3 %collective-permute-start.3 = (bf16[6,4,256,128]{3,2,1,0:T(8,128)(2,1)S(1)}, bf16[6,4,256,128]{3,2,1,0:T(8,128)(2,1)S(1)}, u32[]{:S(2)}, u32[]{:S(2)}) collective-permute-start(bf16[6,4,256,128]{3,2,1,0:T(8,128)(2,1)S(1)} %bitcast.112), channel_id=1, source_target_pairs={{8,0},{16,8},{24,16},{9,1},{17,9},{25,17},{10,2},{18,10},{26,18},{... | collective-permute-start | bytes 4718600 | tf_op jit(solution)/shard_map/ppermute | solution.py:321
  62.6 35.0 %collective-permute-start.4 = (bf16[6,4,256,128]{3,2,1,0:T(8,128)(2,1)S(1)}, bf16[6,4,256,128]{3,2,1,0:T(8,128)(2,1)S(1)}, u32[]{:S(2)}, u32[]{:S(2)}) collective-permute-start(bf16[6,4,256,128]{3,2,1,0:T(8,128)(2,1)S(1)} %bitcast.113), channel_id=1, source_target_pairs={{0,8},{8,16},{16,24},{1,9},{9,17},{17,25},{2,10},{10,18},{18,26},{... | collective-permute-start | bytes 4718600 | tf_op jit(solution)/shard_map/ppermute | solution.py:321
  67.2 46.6 %collective-permute-start.7 = (bf16[8,256,1024]{2,1,0:T(8,128)(2,1)}, bf16[8,256,1024]{2,1,0:T(8,128)(2,1)}, u32[]{:S(2)}, u32[]{:S(2)}) collective-permute-start(bf16[8,256,1024]{2,1,0:T(8,128)(2,1)} %shard_map.200), channel_id=1, source_target_pairs={{0,1},{1,0},{2,3},{3,2},{4,5},{5,4},{6,7},{7,6},{8,9},{9,8},{10,11... | collective-permute-start | bytes 12582920 | tf_op jit(solution)/shard_map/ppermute | solution.py:447
  67.3 25.6 %collective-permute-start.1 = (bf16[2,2,128,1024]{3,2,1,0:T(8,128)(2,1)S(1)}, bf16[2,2,128,1024]{3,2,1,0:T(8,128)(2,1)S(1)}, u32[]{:S(2)}, u32[]{:S(2)}) collective-permute-start(bf16[2,2,128,1024]{3,2,1,0:T(8,128)(2,1)S(1)} %copy-done.27), channel_id=1, source_target_pairs={{0,2},{2,0},{4,6},{6,4},{1,3},{3,1},{5,7},{7,5},{8,10},{10,8},{12,... | collective-permute-start | bytes 3145736 | tf_op jit(solution)/shard_map/ppermute | solution.py:443
  95.5 17.0 %copy-start.3 = (bf16[6,4,256,128]{3,2,1,0:T(8,128)(2,1)}, bf16[6,4,256,128]{3,2,1,0:T(8,128)(2,1)S(1)}, u32[]{:S(2)}) copy-start(bf16[6,4,256,128]{3,2,1,0:T(8,128)(2,1)S(1)} %collective-permute-done.3.refs_1_) | copy-start | bytes 4718596
  97.6 14.9 %copy-start.28 = (bf16[6,4,256,128]{3,2,1,0:T(8,128)(2,1)}, bf16[6,4,256,128]{3,2,1,0:T(8,128)(2,1)S(1)}, u32[]{:S(2)}) copy-start(bf16[6,4,256,128]{3,2,1,0:T(8,128)(2,1)S(1)} %collective-permute-done.4.refs_4_) | copy-start | bytes 4718596
  97.6 10.1 %collective-permute-start.5 = (bf16[2,128,1024]{2,1,0:T(8,128)(2,1)S(1)}, bf16[2,128,1024]{2,1,0:T(8,128)(2,1)S(1)}, u32[]{:S(2)}, u32[]{:S(2)}) collective-permute-start(bf16[2,128,1024]{2,1,0:T(8,128)(2,1)S(1)} %slice_bitcast_fusion.5), channel_id=1, source_target_pairs={{0,4},{2,6},{4,0},{6,2},{1,5},{3,7},{5,1},{7,3},{8,12},{10,14},{12... | collective-permute-start | bytes 1572872 | tf_op jit(solution)/shard_map/ppermute | solution.py:443
  99.1 13.2 %collective-permute-start.6 = (bf16[2,128,1024]{2,1,0:T(8,128)(2,1)S(1)}, bf16[2,128,1024]{2,1,0:T(8,128)(2,1)S(1)}, u32[]{:S(2)}, u32[]{:S(2)}) collective-permute-start(bf16[2,128,1024]{2,1,0:T(8,128)(2,1)S(1)} %slice_bitcast_fusion.4), channel_id=1, source_target_pairs={{0,2},{2,0},{4,6},{6,4},{1,3},{3,1},{5,7},{7,5},{8,10},{10,8},{12,... | collective-permute-start | bytes 1572872 | tf_op jit(solution)/shard_map/ppermute | solution.py:443
  113.8 8.9 %copy-start.8 = (bf16[32,256,128]{2,1,0:T(8,128)(2,1)S(1)}, bf16[32,256,128]{2,1,0:T(8,128)(2,1)}, u32[]{:S(2)}) copy-start(bf16[32,256,128]{2,1,0:T(8,128)(2,1)} %blocks.3) | copy-start | bytes 6291460
  119.2 26.4 %collective-permute-start.8 = (bf16[2,2,128,1024]{3,2,1,0:T(8,128)(2,1)}, bf16[2,2,128,1024]{3,2,1,0:T(8,128)(2,1)}, u32[]{:S(2)}, u32[]{:S(2)}) collective-permute-start(bf16[2,2,128,1024]{3,2,1,0:T(8,128)(2,1)} %get-tuple-element.83), channel_id=1, source_target_pairs={{0,2},{2,0},{4,6},{6,4},{1,3},{3,1},{5,7},{7,5},{8,10},{10,8},{12,... | collective-permute-start | bytes 3145736 | tf_op jit(solution)/shard_map/ppermute | solution.py:443
  121.0 28.0 %collective-permute-start.10 = (bf16[2,2,128,1024]{3,2,1,0:T(8,128)(2,1)S(1)}, bf16[2,2,128,1024]{3,2,1,0:T(8,128)(2,1)}, u32[]{:S(2)}, u32[]{:S(2)}) collective-permute-start(bf16[2,2,128,1024]{3,2,1,0:T(8,128)(2,1)S(1)} %get-tuple-element.85), channel_id=1, source_target_pairs={{0,4},{2,6},{4,0},{6,2},{1,5},{3,7},{5,1},{7,3},{8,12},{10,14},{12... | collective-permute-start | bytes 3145736 | tf_op jit(solution)/shard_map/ppermute | solution.py:443
  127.9 53.0 %all-to-all-start.1 = ((bf16[8,4,256,128]{3,2,1,0:T(8,128)(2,1)}), bf16[8,4,256,128]{3,2,1,0:T(8,128)(2,1)}, u32[]{:S(2)}, u32[]{:S(2)}) async-start(bf16[8,4,256,128]{3,2,1,0:T(8,128)(2,1)} %bitcast.18), calls=%async_computation.1 | async-start | bytes 4194304 | tf_op jit(solution)/shard_map/all_to_all | solution.py:543
  147.3 30.2 %collective-permute-start.9 = (bf16[2,128,1024]{2,1,0:T(8,128)(2,1)S(1)}, bf16[2,128,1024]{2,1,0:T(8,128)(2,1)S(1)}, u32[]{:S(2)}, u32[]{:S(2)}) collective-permute-start(bf16[2,128,1024]{2,1,0:T(8,128)(2,1)S(1)} %slice_bitcast_fusion.2), channel_id=1, source_target_pairs={{0,4},{2,6},{4,0},{6,2},{1,5},{3,7},{5,1},{7,3},{8,12},{10,14},{12... | collective-permute-start | bytes 1572872 | tf_op jit(solution)/shard_map/ppermute | solution.py:443
  150.8 26.9 %collective-permute-start.11 = (bf16[2,128,1024]{2,1,0:T(8,128)(2,1)S(1)}, bf16[2,128,1024]{2,1,0:T(8,128)(2,1)S(1)}, u32[]{:S(2)}, u32[]{:S(2)}) collective-permute-start(bf16[2,128,1024]{2,1,0:T(8,128)(2,1)S(1)} %slice_bitcast_fusion), channel_id=1, source_target_pairs={{0,2},{2,0},{4,6},{6,4},{1,3},{3,1},{5,7},{7,5},{8,10},{10,8},{12,... | collective-permute-start | bytes 1572872 | tf_op jit(solution)/shard_map/ppermute | solution.py:443
  180.9 4.5 copy-start.4
  180.9 36.5 %all-to-all-start.2 = ((bf16[8,4,256,128]{3,2,1,0:T(8,128)(2,1)}), bf16[8,4,256,128]{3,2,1,0:T(8,128)(2,1)}, u32[]{:S(2)}, u32[]{:S(2)}) async-start(bf16[8,4,256,128]{3,2,1,0:T(8,128)(2,1)} %bitcast_bitcast_fusion), calls=%async_computation.2 | async-start | bytes 4194304 | tf_op jit(solution)/shard_map/all_to_all | solution.py:543
  185.4 2.3 copy-start.29
  186.4 30.9 %collective-permute-start.12 = (bf16[4,4,256,128]{3,2,1,0:T(8,128)(2,1)}, bf16[4,4,256,128]{3,2,1,0:T(8,128)(2,1)S(1)}, u32[]{:S(2)}, u32[]{:S(2)}) collective-permute-start(bf16[4,4,256,128]{3,2,1,0:T(8,128)(2,1)} %slice.213), channel_id=1, source_target_pairs={{8,0},{16,8},{24,16},{9,1},{17,9},{25,17},{10,2},{18,10},{26,18},{... | collective-permute-start | bytes 3145736 | tf_op jit(solution)/shard_map/ppermute | solution.py:321
  188.8 28.6 %collective-permute-start.13 = (bf16[4,4,256,128]{3,2,1,0:T(8,128)(2,1)}, bf16[4,4,256,128]{3,2,1,0:T(8,128)(2,1)}, u32[]{:S(2)}, u32[]{:S(2)}) collective-permute-start(bf16[4,4,256,128]{3,2,1,0:T(8,128)(2,1)} %slice.214), channel_id=1, source_target_pairs={{0,8},{8,16},{16,24},{1,9},{9,17},{17,25},{2,10},{10,18},{18,26},{... | collective-permute-start | bytes 3145736 | tf_op jit(solution)/shard_map/ppermute | solution.py:321
  231.5 153.3 %all-to-all-start.3 = ((bf16[8,2,2,1024,128]{4,3,2,1,0:T(8,128)(2,1)}), bf16[8,2,2,1024,128]{4,3,2,1,0:T(8,128)(2,1)}, u32[]{:S(2)}, u32[]{:S(2)}) async-start(bf16[8,2,2,1024,128]{4,3,2,1,0:T(8,128)(2,1)} %shard_map.206), calls=%async_computation.3 | async-start | bytes 16777216 | tf_op jit(solution)/shard_map/all_to_all | solution.py:588
  236.6 133.3 %all-gather.7.cloned.1.call-start = ((), (), s32[]{:S(2)}) async-start(), calls=%async_computation.7 | async-start | bytes 5242880 | tf_op jit(solution)/shard_map/all_gather | solution.py:570
  238.1 98.0 %collective-permute-start.14 = (bf16[2,4,256,128]{3,2,1,0:T(8,128)(2,1)}, bf16[2,4,256,128]{3,2,1,0:T(8,128)(2,1)S(1)}, u32[]{:S(2)}, u32[]{:S(2)}) collective-permute-start(bf16[2,4,256,128]{3,2,1,0:T(8,128)(2,1)} %slice.215), channel_id=1, source_target_pairs={{8,0},{16,8},{24,16},{9,1},{17,9},{25,17},{10,2},{18,10},{26,18},{... | collective-permute-start | bytes 1572872 | tf_op jit(solution)/shard_map/ppermute | solution.py:321
  241.3 11.7 %copy-start.39 = (s32[32]{0:T(128)S(1)}, s32[32]{0:T(128)}, u32[]{:S(2)}) copy-start(s32[32]{0:T(128)} %param.25) | copy-start | bytes 388
  241.3 96.0 %collective-permute-start.15 = (bf16[2,4,256,128]{3,2,1,0:T(8,128)(2,1)}, bf16[2,4,256,128]{3,2,1,0:T(8,128)(2,1)}, u32[]{:S(2)}, u32[]{:S(2)}) collective-permute-start(bf16[2,4,256,128]{3,2,1,0:T(8,128)(2,1)} %slice.216), channel_id=1, source_target_pairs={{0,8},{8,16},{16,24},{1,9},{9,17},{17,25},{2,10},{10,18},{18,26},{... | collective-permute-start | bytes 1572872 | tf_op jit(solution)/shard_map/ppermute | solution.py:321
  250.4 2.8 collective-permute-start.16
  250.5 85.4 %collective-permute-start.17 = (bf16[1,1024,128]{2,1,0:T(8,128)(2,1)}, bf16[1,1024,128]{2,1,0:T(8,128)(2,1)}, u32[]{:S(2)}, u32[]{:S(2)}) collective-permute-start(bf16[1,1024,128]{2,1,0:T(8,128)(2,1)} %bitcast.32), channel_id=1, source_target_pairs={{0,2},{1,3},{2,0},{3,1},{4,6},{5,7},{6,4},{7,5},{8,10},{9,11},{10,... | collective-permute-start | bytes 786440 | tf_op jit(solution)/shard_map/ppermute | solution.py:594
  253.0 113.2 %collective-permute-start.18 = (bf16[1,1024,128]{2,1,0:T(8,128)(2,1)}, bf16[1,1024,128]{2,1,0:T(8,128)(2,1)S(1)}, u32[]{:S(2)}, u32[]{:S(2)}) collective-permute-start(bf16[1,1024,128]{2,1,0:T(8,128)(2,1)} %bitcast.130), channel_id=1, source_target_pairs={{0,3},{1,2},{2,1},{3,0},{4,7},{5,6},{6,5},{7,4},{8,11},{9,10},{10,... | collective-permute-start | bytes 786440 | tf_op jit(solution)/shard_map/ppermute | solution.py:594
  253.2 113.8 %collective-permute-start.19 = (bf16[1,1024,128]{2,1,0:T(8,128)(2,1)}, bf16[1,1024,128]{2,1,0:T(8,128)(2,1)S(1)}, u32[]{:S(2)}, u32[]{:S(2)}) collective-permute-start(bf16[1,1024,128]{2,1,0:T(8,128)(2,1)} %bitcast.129), channel_id=1, source_target_pairs={{0,4},{1,5},{2,6},{3,7},{4,0},{5,1},{6,2},{7,3},{8,12},{9,13},{10,... | collective-permute-start | bytes 786440 | tf_op jit(solution)/shard_map/ppermute | solution.py:594
  335.8 31.9 %collective-permute-start.20 = (bf16[1,1024,128]{2,1,0:T(8,128)(2,1)}, bf16[1,1024,128]{2,1,0:T(8,128)(2,1)S(1)}, u32[]{:S(2)}, u32[]{:S(2)}) collective-permute-start(bf16[1,1024,128]{2,1,0:T(8,128)(2,1)} %bitcast.128), channel_id=1, source_target_pairs={{0,5},{1,4},{2,7},{3,6},{4,1},{5,0},{6,3},{7,2},{8,13},{9,12},{10,... | collective-permute-start | bytes 786440 | tf_op jit(solution)/shard_map/ppermute | solution.py:594
  336.1 32.3 %collective-permute-start.21 = (bf16[1,1024,128]{2,1,0:T(8,128)(2,1)}, bf16[1,1024,128]{2,1,0:T(8,128)(2,1)S(1)}, u32[]{:S(2)}, u32[]{:S(2)}) collective-permute-start(bf16[1,1024,128]{2,1,0:T(8,128)(2,1)} %bitcast.127), channel_id=1, source_target_pairs={{0,6},{1,7},{2,4},{3,5},{4,2},{5,3},{6,0},{7,1},{8,14},{9,15},{10,... | collective-permute-start | bytes 786440 | tf_op jit(solution)/shard_map/ppermute | solution.py:594
  337.3 31.8 %collective-permute-start.22 = (bf16[1,1024,128]{2,1,0:T(8,128)(2,1)}, bf16[1,1024,128]{2,1,0:T(8,128)(2,1)S(1)}, u32[]{:S(2)}, u32[]{:S(2)}) collective-permute-start(bf16[1,1024,128]{2,1,0:T(8,128)(2,1)} %bitcast.126), channel_id=1, source_target_pairs={{0,7},{1,6},{2,5},{3,4},{4,3},{5,2},{6,1},{7,0},{8,15},{9,14},{10,... | collective-permute-start | bytes 786440 | tf_op jit(solution)/shard_map/ppermute | solution.py:594
  397.6 5.2 copy-start.13
  397.6 5.2 copy-start.17
  397.6 5.2 copy-start.19
  397.6 5.2 copy-start.21
  397.6 5.2 copy-start.23
  397.6 113.3 %all-to-all-start.5 = ((bf16[8,1,2,1024,128]{4,3,2,1,0:T(8,128)(2,1)}), bf16[8,1,2,1024,128]{4,3,2,1,0:T(8,128)(2,1)}, u32[]{:S(2)}, u32[]{:S(2)}) async-start(bf16[8,1,2,1024,128]{4,3,2,1,0:T(8,128)(2,1)} %copy-done.2), calls=%async_computation.5 | async-start | bytes 8388608 | tf_op jit(solution)/shard_map/all_to_all | solution.py:628
  403.7 4.1 copy-start.11
  406.0 67.4 %collective-permute-start.24 = (bf16[2,256,1024]{2,1,0:T(8,128)(2,1)S(1)}, bf16[2,256,1024]{2,1,0:T(8,128)(2,1)}, u32[]{:S(2)}, u32[]{:S(2)}) collective-permute-start(bf16[2,256,1024]{2,1,0:T(8,128)(2,1)S(1)} %shard_map.212.refs_1_), channel_id=1, source_target_pairs={{0,4},{2,6},{4,0},{6,2},{1,5},{3,7},{5,1},{7,3},{8,12},{10,14},{12... | collective-permute-start | bytes 3145736 | tf_op jit(solution)/shard_map/ppermute | solution.py:443
  410.1 63.3 %collective-permute-start.23 = (bf16[2,256,1024]{2,1,0:T(8,128)(2,1)S(1)}, bf16[2,256,1024]{2,1,0:T(8,128)(2,1)S(1)}, u32[]{:S(2)}, u32[]{:S(2)}) collective-permute-start(bf16[2,256,1024]{2,1,0:T(8,128)(2,1)S(1)} %shard_map.211.refs_0_), channel_id=1, source_target_pairs={{0,2},{2,0},{4,6},{6,4},{1,3},{3,1},{5,7},{7,5},{8,10},{10,8},{12,... | collective-permute-start | bytes 3145736 | tf_op jit(solution)/shard_map/ppermute | solution.py:443
  411.6 83.9 %collective-permute-start.27 = (bf16[2,256,1024]{2,1,0:T(8,128)(2,1)S(1)}, bf16[2,256,1024]{2,1,0:T(8,128)(2,1)}, u32[]{:S(2)}, u32[]{:S(2)}) collective-permute-start(bf16[2,256,1024]{2,1,0:T(8,128)(2,1)S(1)} %shard_map.212.refs_1_), channel_id=1, source_target_pairs={{0,2},{2,0},{4,6},{6,4},{1,3},{3,1},{5,7},{7,5},{8,10},{10,8},{12,... | collective-permute-start | bytes 3145736 | tf_op jit(solution)/shard_map/ppermute | solution.py:443
  412.2 83.3 %collective-permute-start.30 = (bf16[2,256,1024]{2,1,0:T(8,128)(2,1)S(1)}, bf16[2,256,1024]{2,1,0:T(8,128)(2,1)S(1)}, u32[]{:S(2)}, u32[]{:S(2)}) collective-permute-start(bf16[2,256,1024]{2,1,0:T(8,128)(2,1)S(1)} %shard_map.212.refs_1_), channel_id=1, source_target_pairs={{0,1},{1,0},{2,3},{3,2},{4,5},{5,4},{6,7},{7,6},{8,9},{9,8},{10,11... | collective-permute-start | bytes 3145736 | tf_op jit(solution)/shard_map/ppermute | solution.py:447
  431.6 64.4 %collective-permute-start.28 = (bf16[2,256,1024]{2,1,0:T(8,128)(2,1)S(1)}, bf16[2,256,1024]{2,1,0:T(8,128)(2,1)}, u32[]{:S(2)}, u32[]{:S(2)}) collective-permute-start(bf16[2,256,1024]{2,1,0:T(8,128)(2,1)S(1)} %shard_map.211.refs_0_), channel_id=1, source_target_pairs={{0,4},{2,6},{4,0},{6,2},{1,5},{3,7},{5,1},{7,3},{8,12},{10,14},{12... | collective-permute-start | bytes 3145736 | tf_op jit(solution)/shard_map/ppermute | solution.py:443
  473.4 22.7 %collective-permute-start.29 = (bf16[2,256,1024]{2,1,0:T(8,128)(2,1)S(1)}, bf16[2,256,1024]{2,1,0:T(8,128)(2,1)S(1)}, u32[]{:S(2)}, u32[]{:S(2)}) collective-permute-start(bf16[2,256,1024]{2,1,0:T(8,128)(2,1)S(1)} %shard_map.211.refs_0_), channel_id=1, source_target_pairs={{0,1},{1,0},{2,3},{3,2},{4,5},{5,4},{6,7},{7,6},{8,9},{9,8},{10,11... | collective-permute-start | bytes 3145736 | tf_op jit(solution)/shard_map/ppermute | solution.py:447
  473.4 24.2 %collective-permute-start.31 = (bf16[2,256,1024]{2,1,0:T(8,128)(2,1)S(1)}, bf16[2,256,1024]{2,1,0:T(8,128)(2,1)S(1)}, u32[]{:S(2)}, u32[]{:S(2)}) collective-permute-start(bf16[2,256,1024]{2,1,0:T(8,128)(2,1)S(1)} %collective-permute-done.23.refs_2_), channel_id=1, source_target_pairs={{0,1},{1,0},{2,3},{3,2},{4,5},{5,4},{6,7},{7,6},{8,9},{9,8},{10,11... | collective-permute-start | bytes 3145736 | tf_op jit(solution)/shard_map/ppermute | solution.py:447
  495.5 5.3 collective-permute-start.34
  495.5 5.3 collective-permute-start.32
  496.0 5.5 %collective-permute-start.33 = (bf16[2,256,1024]{2,1,0:T(8,128)(2,1)}, bf16[2,256,1024]{2,1,0:T(8,128)(2,1)}, u32[]{:S(2)}, u32[]{:S(2)}) collective-permute-start(bf16[2,256,1024]{2,1,0:T(8,128)(2,1)} %collective-permute-done.28.refs_4_), channel_id=1, source_target_pairs={{0,1},{1,0},{2,3},{3,2},{4,5},{5,4},{6,7},{7,6},{8,9},{9,8},{10,11... | collective-permute-start | bytes 3145736 | tf_op jit(solution)/shard_map/ppermute | solution.py:447
  496.1 25.6 %collective-permute-start.25 = (bf16[2,256,1024]{2,1,0:T(8,128)(2,1)S(1)}, bf16[2,256,1024]{2,1,0:T(8,128)(2,1)}, u32[]{:S(2)}, u32[]{:S(2)}) collective-permute-start(bf16[2,256,1024]{2,1,0:T(8,128)(2,1)S(1)} %collective-permute-done.23.refs_2_), channel_id=1, source_target_pairs={{0,4},{2,6},{4,0},{6,2},{1,5},{3,7},{5,1},{7,3},{8,12},{10,14},{12... | collective-permute-start | bytes 3145736 | tf_op jit(solution)/shard_map/ppermute | solution.py:443
  498.6 25.5 %collective-permute-start.26 = (bf16[2,256,1024]{2,1,0:T(8,128)(2,1)}, bf16[2,256,1024]{2,1,0:T(8,128)(2,1)}, u32[]{:S(2)}, u32[]{:S(2)}) collective-permute-start(bf16[2,256,1024]{2,1,0:T(8,128)(2,1)} %collective-permute-done.24.refs_5_), channel_id=1, source_target_pairs={{0,2},{2,0},{4,6},{6,4},{1,3},{3,1},{5,7},{7,5},{8,10},{10,8},{12,... | collective-permute-start | bytes 3145736 | tf_op jit(solution)/shard_map/ppermute | solution.py:443
  511.0 13.8 %copy-start.35 = (f32[208,256]{1,0:T(8,128)S(1)}, f32[208,256]{1,0:T(8,128)}, u32[]{:S(2)}) copy-start(f32[208,256]{1,0:T(8,128)} %param.26) | copy-start | bytes 638980
  511.0 13.8 %copy-start.36 = (f32[208,256]{1,0:T(8,128)S(1)}, f32[208,256]{1,0:T(8,128)}, u32[]{:S(2)}) copy-start(f32[208,256]{1,0:T(8,128)} %param.28) | copy-start | bytes 638980
  511.0 13.8 %copy-start.37 = (f32[208,256]{1,0:T(8,128)S(1)}, f32[208,256]{1,0:T(8,128)}, u32[]{:S(2)}) copy-start(f32[208,256]{1,0:T(8,128)} %param.29) | copy-start | bytes 638980
  511.0 13.8 %copy-start.38 = (bf16[208,256]{1,0:T(8,128)(2,1)S(1)}, bf16[208,256]{1,0:T(8,128)(2,1)}, u32[]{:S(2)}) copy-start(bf16[208,256]{1,0:T(8,128)(2,1)} %param.27) | copy-start | bytes 319492
  524.1 2.9 collective-permute-start.35
  524.1 4.4 collective-permute-start.36
  (20 other events, 23.8 us)
Sparse Core Ops, SparseCore 0:
  113.8 86.1 all-gather.4
  239.0 87.4 all-gather.6

commit v4 on v3

--- a/solution.py
+++ b/solution.py
@@ -589,17 +589,19 @@
     adam_m_new, adam_v_new, adam_total = adam(
         tiles.reshape(blocks, rows, cols), place, adam_m, adam_v
     )
+    pieces = [precondition(left_dealt, 0, grad_blocks[0], rights)]
+    adam_total, pieces[0], weights_sent = lax.optimization_barrier(
+        (adam_total, pieces[0], weights_sent)
+    )
     away = weights_sent.reshape(group, per * rows, cols)
     away = [away[:1]] + [
         lax.ppermute(away[k : k + 1], GROUP, [(g, g ^ k) for g in range(group)])
         for k in range(1, group)
     ]
-    pieces = [precondition(left_dealt, 0, grad_blocks[0], rights)]
     if early:
-        grad_blocks[1], adam_total, pieces[0], away = lax.optimization_barrier(
-            (grad_blocks[1], adam_total, pieces[0], away)
+        grad_blocks[1], adam_total, pieces[0] = lax.optimization_barrier(
+            (grad_blocks[1], adam_total, pieces[0])
         )
-    if early:
         pieces.append(precondition(left_dealt, early, grad_blocks[1], rights))
     entry = jnp.where(is_heavy, early, own_entry) - early
     last_slabs = grams(grad_blocks[-1], jnp.clip(entry, 0, per - 1 - early).reshape(1))
@@ -615,7 +617,9 @@
     shampoo_part = jnp.sum(jnp.sum(precond_total, axis=(1, 2))[:, None] * own_onehot, axis=0)
     parts = jnp.pad(jnp.stack([adam_part, shampoo_part]), ((0, 6), (0, LANES - MATS)))
     if early:
-        received, last_slabs, parts = lax.optimization_barrier((received, last_slabs, parts))
+        received, last_slabs, parts, away = lax.optimization_barrier(
+            (received, last_slabs, parts, away)
+        )
     devices = owner_count * group
     parts = lax.all_to_all(
         jnp.broadcast_to(parts[None], (devices,) + parts.shape), ALL, 0, 0, tiled=True

time: 541 us -> 510 us (0.943)
  waiting for transfers between devices: 249 us -> 224 us
  local copies, waits for them, and re-layouts: 31.3 us -> 25.7 us
    ppermute x7, waiting for transfers between devices: 80.9 us -> 7.71 us  [shards(): lax.ppermute(away[k:k + 1], GROUP, [(g, g ^ k) for g in range(group)])]
    all_gather x2, waiting for transfers between devices: 0.01 us -> 47 us  [shards(): grad_blocks = [lax.all_gather(part, 'shard', axis=0) for part in gradient]]
    unnamed x80 -> x70, local copies, waits for them, and re-layouts: 19 us -> 15.2 us
  transfers between devices with their start and end apart: 44 -> 44, of which waited for: 18 -> 20; matrix products, arithmetic and copies ran while one was open for 4% -> 4% of each run, Pallas kernels for 22% -> 23%
where the time goes in v4:
time: 510 us; the launch traced here: 508 us
  waiting for transfers between devices  224 us (44%)
  Pallas kernels  137 us (27%)
  starting transfers between devices  74.5 us (15%)
  local copies, waits for them, and re-layouts  25.7 us (5%)
  other arithmetic  17.6 us (3%)
  between operations  16.1 us (3%)
  blocking collectives  13.6 us (3%)
    ppermute x14, waiting for transfers between devices, swap(): return lax.ppermute(array, 'tensor', [(t, t ^ bit) for t in range(devices)])  137 us
    all_gather x2, waiting for transfers between devices, shards(): grad_blocks = [lax.all_gather(part, 'shard', axis=0) for part in gradient]  47 us
    pallas_call x7, Pallas kernels, reorder(): pl.pallas_call(reorder_kernel, grid_spec=pltpu.PrefetchScalarGridSpec(num...  29.8 us
    pallas_call x2, Pallas kernels, refresh(): pl.pallas_call(stat_kernel, grid_spec=pltpu.PrefetchScalarGridSpec(num_sc...  29.7 us
    ppermute x14, starting transfers between devices, swap(): return lax.ppermute(array, 'tensor', [(t, t ^ bit) for t in range(devices)])  21.5 us
    pallas_call x1, Pallas kernels, adam(): pl.pallas_call(adam_kernel, grid_spec=pltpu.PrefetchScalarGridSpec(num_sc...  20.5 us
    pallas_call x2, Pallas kernels, grams(): pl.pallas_call(gram_kernel, grid_spec=pltpu.PrefetchScalarGridSpec(num_sc...  18.1 us
    ppermute x3, starting transfers between devices, hop(): lax.ppermute(moved[1], 'shard', up)  16.6 us
  transfers between devices with their start and end apart: 44, of which 20 were waited for; matrix products, arithmetic and copies ran while one was open for 4% of the time, Pallas kernels for 23%

profile of v4, /device:TPU:0, one launch (start us, length us, event | category | flops | bytes accessed | tf_op | source)
XLA Modules:
  0.0 508.3 jit_solution(17170859877932803121)
XLA Ops:
  10.5 2.0 fusion.18
  14.4 4.2 shard_map.197
  19.1 7.3 %shard_map.199 = bf16[32,256,128]{2,1,0:T(8,128)(2,1)S(1)} custom-call(s32[32]{0:T(128)S(1)} %select_reduce_fusion.order, bf16[32,256,128]{2,1,0:T(8,128)(2,1)S(1)} %copy-done.8), custom_call_target="tpu_custom_call" | custom-call | tf_op jit(solution)/shard_map/pallas_call | solution.py:72
  27.7 4.8 all-to-all-start
  34.2 4.1 shard_map.200
  38.3 5.4 %shard_map.198 = (bf16[2,2,128,1024]{3,2,1,0:T(8,128)(2,1)S(1)}, bf16[2,2,128,1024]{3,2,1,0:T(8,128)(2,1)S(1)}, bf16[2,2,128,1024]{3,2,1,0:T(8,128)(2,1)}, bf16[2,2,128,1024]{3,2,1,0:T(8,128)(2,1)S(1)}) custom-call(s32[8]{0:T(128)S(1)} %reshape.214.picked, bf16[32,256,1024]{2,1,0:T(8,128)(2,1)} %bitcast.116, bf16[32,256,1024]{2,1,0:T(8,128)(2,1)} %bitcast.117, ...), custom_call_target="tpu_custom_call" | custom-call | tf_op jit(solution)/shard_map/pallas_call | solution.py:422
  45.7 2.0 collective-permute-start.2
  47.7 11.6 %all-to-all-done.refs_0_ = bf16[8,4,256,128]{3,2,1,0:T(8,128)(2,1)S(1)} async-done(((bf16[8,4,256,128]{3,2,1,0:T(8,128)(2,1)}), bf16[8,4,256,128]{3,2,1,0:T(8,128)(2,1)S(1)}, u32[]{:S(2)}, u32[]{:S(2)}) %all-to-all-start) | async-done | bytes 2097184 | tf_op jit(solution)/shard_map/all_to_all | solution.py:543
  62.6 4.6 collective-permute-start.4
  67.8 13.0 %collective-permute-done.2 = bf16[2,2,128,1024]{3,2,1,0:T(8,128)(2,1)} collective-permute-done((bf16[2,2,128,1024]{3,2,1,0:T(8,128)(2,1)}, bf16[2,2,128,1024]{3,2,1,0:T(8,128)(2,1)}, u32[]{:S(2)}, u32[]{:S(2)}) %collective-permute-start.2) | collective-permute-done | bytes 1048608 | tf_op jit(solution)/shard_map/ppermute | solution.py:443
  80.8 1.6 add_convert_fusion.2
  82.5 10.4 %collective-permute-done.1 = bf16[2,2,128,1024]{3,2,1,0:T(8,128)(2,1)S(1)} collective-permute-done((bf16[2,2,128,1024]{3,2,1,0:T(8,128)(2,1)S(1)}, bf16[2,2,128,1024]{3,2,1,0:T(8,128)(2,1)S(1)}, u32[]{:S(2)}, u32[]{:S(2)}) %collective-permute-start.1) | collective-permute-done | bytes 1048608 | tf_op jit(solution)/shard_map/ppermute | solution.py:443
  93.3 2.2 collective-permute-done.3.refs_1_
  95.5 2.1 collective-permute-done.4.refs_4_
  99.1 2.6 collective-permute-start.6
  101.7 6.0 %collective-permute-done.5 = bf16[2,128,1024]{2,1,0:T(8,128)(2,1)S(1)} collective-permute-done((bf16[2,128,1024]{2,1,0:T(8,128)(2,1)S(1)}, bf16[2,128,1024]{2,1,0:T(8,128)(2,1)S(1)}, u32[]{:S(2)}, u32[]{:S(2)}) %collective-permute-start.5) | collective-permute-done | bytes 524320 | tf_op jit(solution)/shard_map/ppermute | solution.py:443
  107.9 4.4 collective-permute-done.6
  113.8 5.4 %shard_map.205 = (bf16[2,2,128,1024]{3,2,1,0:T(8,128)(2,1)}, bf16[2,2,128,1024]{3,2,1,0:T(8,128)(2,1)S(1)}, bf16[2,2,128,1024]{3,2,1,0:T(8,128)(2,1)S(1)}, bf16[2,2,128,1024]{3,2,1,0:T(8,128)(2,1)S(1)}) custom-call(s32[8]{0:T(128)S(1)} %reshape.223.picked, bf16[32,256,1024]{2,1,0:T(8,128)(2,1)} %bitcast.120, bf16[32,256,1024]{2,1,0:T(8,128)(2,1)} %bitcast.121, ...), custom_call_target="tpu_custom_call" | custom-call | tf_op jit(solution)/shard_map/pallas_call | solution.py:422
  119.2 1.8 collective-permute-start.8
  121.0 1.6 collective-permute-start.10
  122.7 5.2 %shard_map.203 = bf16[32,256,128]{2,1,0:T(8,128)(2,1)} custom-call(s32[32]{0:T(128)S(1)} %select_reduce_fusion.order, bf16[32,256,128]{2,1,0:T(8,128)(2,1)S(1)} %copy-done.9), custom_call_target="tpu_custom_call" | custom-call | tf_op jit(solution)/shard_map/pallas_call | solution.py:72
  127.9 4.4 all-to-all-start.1
  132.2 13.4 %collective-permute-done.8 = bf16[2,2,128,1024]{3,2,1,0:T(8,128)(2,1)} collective-permute-done((bf16[2,2,128,1024]{3,2,1,0:T(8,128)(2,1)}, bf16[2,2,128,1024]{3,2,1,0:T(8,128)(2,1)}, u32[]{:S(2)}, u32[]{:S(2)}) %collective-permute-start.8) | collective-permute-done | bytes 1048608 | tf_op jit(solution)/shard_map/ppermute | solution.py:443
  145.6 1.6 add_convert_fusion.1
  147.3 1.8 collective-permute-start.9
  149.1 1.6 add_convert_fusion
  150.8 3.5 collective-permute-start.11
  154.3 23.2 %collective-permute-done.9 = bf16[2,128,1024]{2,1,0:T(8,128)(2,1)S(1)} collective-permute-done((bf16[2,128,1024]{2,1,0:T(8,128)(2,1)S(1)}, bf16[2,128,1024]{2,1,0:T(8,128)(2,1)S(1)}, u32[]{:S(2)}, u32[]{:S(2)}) %collective-permute-start.9) | collective-permute-done | bytes 524320 | tf_op jit(solution)/shard_map/ppermute | solution.py:443
  179.0 1.9 bitcast_bitcast_fusion
  180.9 4.5 all-to-all-start.2
  188.8 6.0 %collective-permute-start.13 = (bf16[4,4,256,128]{3,2,1,0:T(8,128)(2,1)}, bf16[4,4,256,128]{3,2,1,0:T(8,128)(2,1)}, u32[]{:S(2)}, u32[]{:S(2)}) collective-permute-start(bf16[4,4,256,128]{3,2,1,0:T(8,128)(2,1)} %slice.214), channel_id=1, source_target_pairs={{0,8},{8,16},{16,24},{1,9},{9,17},{17,25},{2,10},{10,18},{18,26},{... | collective-permute-start | bytes 3145736 | tf_op jit(solution)/shard_map/ppermute | solution.py:321
  195.5 1.6 copy-done.10
  197.1 7.3 %shard_map.204 = bf16[32,256,128]{2,1,0:T(8,128)(2,1)S(1)} custom-call(s32[32]{0:T(128)S(1)} %reshape.222.order, bf16[32,256,128]{2,1,0:T(8,128)(2,1)S(1)} %copy-done.10), custom_call_target="tpu_custom_call" | custom-call | tf_op jit(solution)/shard_map/pallas_call | solution.py:72
  205.7 11.7 %collective-permute-done.12.refs_2_ = bf16[4,4,256,128]{3,2,1,0:T(8,128)(2,1)S(1)} collective-permute-done((bf16[4,4,256,128]{3,2,1,0:T(8,128)(2,1)}, bf16[4,4,256,128]{3,2,1,0:T(8,128)(2,1)S(1)}, u32[]{:S(2)}, u32[]{:S(2)}) %collective-permute-start.12) | collective-permute-done | bytes 1048608 | tf_op jit(solution)/shard_map/ppermute | solution.py:321
  217.4 2.2 copy-done.1
  219.6 12.0 %shard_map.206 = bf16[8,2,2,1024,128]{4,3,2,1,0:T(8,128)(2,1)} custom-call(s32[2]{0:T(128)S(1)} %iota.55.chosen, bf16[4,2,256,1024]{3,2,1,0:T(8,128)(2,1)S(1)} %bitcast.108), custom_call_target="tpu_custom_call" | custom-call | tf_op jit(solution)/shard_map/pallas_call | solution.py:177
  231.5 5.0 all-to-all-start.3
  239.4 1.9 slice.216
  241.3 6.0 %collective-permute-start.15 = (bf16[2,4,256,128]{3,2,1,0:T(8,128)(2,1)}, bf16[2,4,256,128]{3,2,1,0:T(8,128)(2,1)}, u32[]{:S(2)}, u32[]{:S(2)}) collective-permute-start(bf16[2,4,256,128]{3,2,1,0:T(8,128)(2,1)} %slice.216), channel_id=1, source_target_pairs={{0,8},{8,16},{16,24},{1,9},{9,17},{17,25},{2,10},{10,18},{18,26},{... | collective-permute-start | bytes 1572872 | tf_op jit(solution)/shard_map/ppermute | solution.py:321
  248.0 20.5 %shard_map.207 = (f32[32,256,128]{2,1,0:T(8,128)}, f32[32,256,128]{2,1,0:T(8,128)}, f32[32,1,128]{2,1,0:T(1,128)S(1)}) custom-call(s32[32]{0:T(128)S(1)} %fusion.12.place, bf16[32,256,128]{2,1,0:T(8,128)(2,1)} %bitcast.28.grad, f32[32,256,128]{2,1,0:T(8,128)} %moment.1, f32[32,256,128]{2,1,0:T(8,128)} %second.1), custom_call_target="tpu_custom_call" | custom-call | tf_op jit(solution)/shard_map/pallas_call | solution.py:125
  268.5 5.2 %shard_map.208 = (bf16[2,256,1024]{2,1,0:T(8,128)(2,1)S(1)}, f32[2,1,128]{2,1,0:T(1,128)S(1)}) custom-call(s32[1]{0:T(128)} %bitcast.29.me, bf16[8,4,256,128]{3,2,1,0:T(8,128)(2,1)} %all-to-all-done.1.left, bf16[4,2,256,1024]{3,2,1,0:T(8,128)(2,1)} %bitcast.107, bf16[8,4,256,128]{3,2,1,0:T(8,128)(2,1)} %copy-done, bf16[6,4,256,128]{3,2,1,0:T(8,128)(2,1)S(1)} %copy-done.4, ...), custom_call_target="tpu_custom_call" | custom-call | tf_op jit(solution)/shard_map/pallas_call | solution.py:343
  275.4 1.8 collective-permute-start.17
  277.5 1.7 collective-permute-start.19
  279.2 47.0 %all-gather.7.cloned.1.call-done = bf16[8,256,1024]{2,1,0:T(8,128)(2,1)} async-done(((bf16[2,256,1024]{2,1,0:T(8,128)(2,1)}), bf16[8,256,1024]{2,1,0:T(8,128)(2,1)}) %all-gather.7.cloned.1.call-update) | async-done | bytes 4194320 | tf_op jit(solution)/shard_map/all_gather | solution.py:570
  326.6 2.6 collective-permute-start.21
  329.2 6.6 %collective-permute-done.17.refs_2_ = bf16[1,1024,128]{2,1,0:T(8,128)(2,1)} collective-permute-done((bf16[1,1024,128]{2,1,0:T(8,128)(2,1)}, bf16[1,1024,128]{2,1,0:T(8,128)(2,1)}, u32[]{:S(2)}, u32[]{:S(2)}) %collective-permute-start.17) | collective-permute-done | bytes 262176 | tf_op jit(solution)/shard_map/ppermute | solution.py:598
  336.2 6.1 %shard_map.209 = bf16[8,1,2,1024,128]{4,3,2,1,0:T(8,128)(2,1)S(1)} custom-call(s32[1]{0:T(128)} %bitcast.26.chosen, bf16[4,2,256,1024]{3,2,1,0:T(8,128)(2,1)} %bitcast.124), custom_call_target="tpu_custom_call" | custom-call | tf_op jit(solution)/shard_map/pallas_call | solution.py:177
  342.3 2.0 copy-done.2
  344.4 5.0 shard_map.210
  353.2 13.6 %all_to_all.30 = f32[32,8,128]{2,1,0:T(8,128)S(1)} all-to-all(f32[32,8,128]{2,1,0:T(8,128)S(1)} %broadcast_in_dim.47), channel_id=1, replica_groups=mesh['shard'=4,'tensor'=4,'section'=2] {'shard','tensor','section'}, dimensions={0} | all-to-all | bytes 262144 | tf_op jit(solution)/shard_map/all_to_all | solution.py:624
  366.8 4.9 all-to-all-start.5
  372.0 2.2 shard_map.212.refs_1_
  374.2 1.8 collective-permute-start.24
  376.0 2.2 shard_map.211.refs_0_
  378.2 1.6 collective-permute-start.23
  380.3 19.4 %shard_map.213 = (f32[24,1024,128]{2,1,0:T(8,128)}, f32[24,1024,128]{2,1,0:T(8,128)}) custom-call(s32[1]{0:T(128)} %bitcast.42.base, s32[16]{0:T(128)S(1)} %get-tuple-element.198.source, s32[16]{0:T(128)S(1)} %get-tuple-element.197.entry, s32[16]{0:T(128)S(1)} %mul.136.filled, f32[24,1024,128]{2,1,0:T(8,128)} %left_stat.3, f32[24,1024,128]{2,1,0:T(8,128)} %right_stat.3, ...), custom_call_target="tpu_custom_call" | custom-call | tf_op jit(solution)/shard_map/pallas_call | solution.py:212
  400.0 42.6 %collective-permute-done.24.refs_5_ = bf16[2,256,1024]{2,1,0:T(8,128)(2,1)} collective-permute-done((bf16[2,256,1024]{2,1,0:T(8,128)(2,1)S(1)}, bf16[2,256,1024]{2,1,0:T(8,128)(2,1)}, u32[]{:S(2)}, u32[]{:S(2)}) %collective-permute-start.24) | collective-permute-done | bytes 1048608 | tf_op jit(solution)/shard_map/ppermute | solution.py:443
  443.1 21.6 %collective-permute-done.27.refs_3_ = bf16[2,256,1024]{2,1,0:T(8,128)(2,1)} collective-permute-done((bf16[2,256,1024]{2,1,0:T(8,128)(2,1)S(1)}, bf16[2,256,1024]{2,1,0:T(8,128)(2,1)}, u32[]{:S(2)}, u32[]{:S(2)}) %collective-permute-start.27) | collective-permute-done | bytes 1048608 | tf_op jit(solution)/shard_map/ppermute | solution.py:443
  465.3 1.5 collective-permute-start.25
  470.7 9.4 %shard_map.214.refs_4_ = bf16[32,256,1024]{2,1,0:T(8,128)(2,1)} custom-call(s32[24]{0:T(128)S(1)} %concatenate.23.target, bf16[2,256,1024]{2,1,0:T(8,128)(2,1)S(1)} %shard_map.211.refs_0_, bf16[2,256,1024]{2,1,0:T(8,128)(2,1)S(1)} %shard_map.212.refs_1_, bf16[2,256,1024]{2,1,0:T(8,128)(2,1)S(1)} %collective-permute-done.23.refs_2_, ...), custom_call_target="tpu_custom_call" | custom-call | tf_op jit(solution)/shard_map/pallas_call | solution.py:97
  480.2 10.3 %shard_map.215 = (f32[24,1024,128]{2,1,0:T(8,128)}, f32[24,1024,128]{2,1,0:T(8,128)}) custom-call(s32[1]{0:T(128)} %bitcast.55.base, s32[8]{0:T(128)S(1)} %and_select_fusion.source, s32[8]{0:T(128)S(1)} %broadcast.231.entry, s32[8]{0:T(128)S(1)} %compare_convert_fusion.filled, ...), custom_call_target="tpu_custom_call", output_to_operand_aliasing={{0}: (8, {}), {1}: (9, {})} | custom-call | tf_op jit(solution)/shard_map/pallas_call | solution.py:212
  490.9 2.4 collective-permute-done.26.refs_1_
  496.2 1.5 collective-permute-done.36.refs_3_
  497.7 3.7 shard_map.216
  (196 shorter events, 43.0 us)
Async XLA Ops:
  14.4 4.7 copy-start.8
  18.6 19.7 %collective-permute-start = (bf16[8,256,1024]{2,1,0:T(8,128)(2,1)}, bf16[8,256,1024]{2,1,0:T(8,128)(2,1)}, u32[]{:S(2)}, u32[]{:S(2)}) collective-permute-start(bf16[8,256,1024]{2,1,0:T(8,128)(2,1)} %shard_map.197), channel_id=1, source_target_pairs={{0,1},{1,0},{2,3},{3,2},{4,5},{5,4},{6,7},{7,6},{8,9},{9,8},{10,11... | collective-permute-start | bytes 12582920 | tf_op jit(solution)/shard_map/ppermute | solution.py:447
  27.7 31.6 %all-to-all-start = ((bf16[8,4,256,128]{3,2,1,0:T(8,128)(2,1)}), bf16[8,4,256,128]{3,2,1,0:T(8,128)(2,1)S(1)}, u32[]{:S(2)}, u32[]{:S(2)}) async-start(bf16[8,4,256,128]{3,2,1,0:T(8,128)(2,1)} %bitcast.109), calls=%async_computation | async-start | bytes 4194304 | tf_op jit(solution)/shard_map/all_to_all | solution.py:543
  32.6 184.8 %all-gather.5.cloned.1.call-start = ((), (), s32[]{:S(2)}) async-start(), calls=%async_computation.6 | async-start | bytes 5242880 | tf_op jit(solution)/shard_map/all_gather | solution.py:570
  45.7 35.1 %collective-permute-start.2 = (bf16[2,2,128,1024]{3,2,1,0:T(8,128)(2,1)}, bf16[2,2,128,1024]{3,2,1,0:T(8,128)(2,1)}, u32[]{:S(2)}, u32[]{:S(2)}) collective-permute-start(bf16[2,2,128,1024]{3,2,1,0:T(8,128)(2,1)} %get-tuple-element.80), channel_id=1, source_target_pairs={{0,4},{2,6},{4,0},{6,2},{1,5},{3,7},{5,1},{7,3},{8,12},{10,14},{12... | collective-permute-start | bytes 3145736 | tf_op jit(solution)/shard_map/ppermute | solution.py:443
  59.3 3.3 copy-start
  60.2 7.1 %copy-start.22 = (bf16[2,2,128,1024]{3,2,1,0:T(8,128)(2,1)S(1)}, bf16[2,2,128,1024]{3,2,1,0:T(8,128)(2,1)}, u32[]{:S(2)}) copy-start(bf16[2,2,128,1024]{3,2,1,0:T(8,128)(2,1)} %copy-done.21) | copy-start | bytes 3145732
  60.2 20.6 %copy-start.16 = (bf16[2,2,128,1024]{3,2,1,0:T(8,128)(2,1)S(1)}, bf16[2,2,128,1024]{3,2,1,0:T(8,128)(2,1)}, u32[]{:S(2)}) copy-start(bf16[2,2,128,1024]{3,2,1,0:T(8,128)(2,1)} %copy-done.15) | copy-start | bytes 3145732
  60.2 35.3 %collective-permute-start.3 = (bf16[6,4,256,128]{3,2,1,0:T(8,128)(2,1)S(1)}, bf16[6,4,256,128]{3,2,1,0:T(8,128)(2,1)S(1)}, u32[]{:S(2)}, u32[]{:S(2)}) collective-permute-start(bf16[6,4,256,128]{3,2,1,0:T(8,128)(2,1)S(1)} %bitcast.112), channel_id=1, source_target_pairs={{8,0},{16,8},{24,16},{9,1},{17,9},{25,17},{10,2},{18,10},{26,18},{... | collective-permute-start | bytes 4718600 | tf_op jit(solution)/shard_map/ppermute | solution.py:321
  62.6 35.0 %collective-permute-start.4 = (bf16[6,4,256,128]{3,2,1,0:T(8,128)(2,1)S(1)}, bf16[6,4,256,128]{3,2,1,0:T(8,128)(2,1)S(1)}, u32[]{:S(2)}, u32[]{:S(2)}) collective-permute-start(bf16[6,4,256,128]{3,2,1,0:T(8,128)(2,1)S(1)} %bitcast.113), channel_id=1, source_target_pairs={{0,8},{8,16},{16,24},{1,9},{9,17},{17,25},{2,10},{10,18},{18,26},{... | collective-permute-start | bytes 4718600 | tf_op jit(solution)/shard_map/ppermute | solution.py:321
  67.2 46.6 %collective-permute-start.7 = (bf16[8,256,1024]{2,1,0:T(8,128)(2,1)}, bf16[8,256,1024]{2,1,0:T(8,128)(2,1)}, u32[]{:S(2)}, u32[]{:S(2)}) collective-permute-start(bf16[8,256,1024]{2,1,0:T(8,128)(2,1)} %shard_map.200), channel_id=1, source_target_pairs={{0,1},{1,0},{2,3},{3,2},{4,5},{5,4},{6,7},{7,6},{8,9},{9,8},{10,11... | collective-permute-start | bytes 12582920 | tf_op jit(solution)/shard_map/ppermute | solution.py:447
  67.3 25.6 %collective-permute-start.1 = (bf16[2,2,128,1024]{3,2,1,0:T(8,128)(2,1)S(1)}, bf16[2,2,128,1024]{3,2,1,0:T(8,128)(2,1)S(1)}, u32[]{:S(2)}, u32[]{:S(2)}) collective-permute-start(bf16[2,2,128,1024]{3,2,1,0:T(8,128)(2,1)S(1)} %copy-done.22), channel_id=1, source_target_pairs={{0,2},{2,0},{4,6},{6,4},{1,3},{3,1},{5,7},{7,5},{8,10},{10,8},{12,... | collective-permute-start | bytes 3145736 | tf_op jit(solution)/shard_map/ppermute | solution.py:443
  95.5 17.0 %copy-start.3 = (bf16[6,4,256,128]{3,2,1,0:T(8,128)(2,1)}, bf16[6,4,256,128]{3,2,1,0:T(8,128)(2,1)S(1)}, u32[]{:S(2)}) copy-start(bf16[6,4,256,128]{3,2,1,0:T(8,128)(2,1)S(1)} %collective-permute-done.3.refs_1_) | copy-start | bytes 4718596
  97.6 14.9 %copy-start.23 = (bf16[6,4,256,128]{3,2,1,0:T(8,128)(2,1)}, bf16[6,4,256,128]{3,2,1,0:T(8,128)(2,1)S(1)}, u32[]{:S(2)}) copy-start(bf16[6,4,256,128]{3,2,1,0:T(8,128)(2,1)S(1)} %collective-permute-done.4.refs_4_) | copy-start | bytes 4718596
  97.6 10.1 %collective-permute-start.5 = (bf16[2,128,1024]{2,1,0:T(8,128)(2,1)S(1)}, bf16[2,128,1024]{2,1,0:T(8,128)(2,1)S(1)}, u32[]{:S(2)}, u32[]{:S(2)}) collective-permute-start(bf16[2,128,1024]{2,1,0:T(8,128)(2,1)S(1)} %slice_bitcast_fusion.5), channel_id=1, source_target_pairs={{0,4},{2,6},{4,0},{6,2},{1,5},{3,7},{5,1},{7,3},{8,12},{10,14},{12... | collective-permute-start | bytes 1572872 | tf_op jit(solution)/shard_map/ppermute | solution.py:443
  99.1 13.2 %collective-permute-start.6 = (bf16[2,128,1024]{2,1,0:T(8,128)(2,1)S(1)}, bf16[2,128,1024]{2,1,0:T(8,128)(2,1)S(1)}, u32[]{:S(2)}, u32[]{:S(2)}) collective-permute-start(bf16[2,128,1024]{2,1,0:T(8,128)(2,1)S(1)} %slice_bitcast_fusion.4), channel_id=1, source_target_pairs={{0,2},{2,0},{4,6},{6,4},{1,3},{3,1},{5,7},{7,5},{8,10},{10,8},{12,... | collective-permute-start | bytes 1572872 | tf_op jit(solution)/shard_map/ppermute | solution.py:443
  113.8 8.9 %copy-start.9 = (bf16[32,256,128]{2,1,0:T(8,128)(2,1)S(1)}, bf16[32,256,128]{2,1,0:T(8,128)(2,1)}, u32[]{:S(2)}) copy-start(bf16[32,256,128]{2,1,0:T(8,128)(2,1)} %blocks.3) | copy-start | bytes 6291460
  119.2 26.4 %collective-permute-start.8 = (bf16[2,2,128,1024]{3,2,1,0:T(8,128)(2,1)}, bf16[2,2,128,1024]{3,2,1,0:T(8,128)(2,1)}, u32[]{:S(2)}, u32[]{:S(2)}) collective-permute-start(bf16[2,2,128,1024]{3,2,1,0:T(8,128)(2,1)} %get-tuple-element.87), channel_id=1, source_target_pairs={{0,2},{2,0},{4,6},{6,4},{1,3},{3,1},{5,7},{7,5},{8,10},{10,8},{12,... | collective-permute-start | bytes 3145736 | tf_op jit(solution)/shard_map/ppermute | solution.py:443
  121.0 28.1 %collective-permute-start.10 = (bf16[2,2,128,1024]{3,2,1,0:T(8,128)(2,1)S(1)}, bf16[2,2,128,1024]{3,2,1,0:T(8,128)(2,1)}, u32[]{:S(2)}, u32[]{:S(2)}) collective-permute-start(bf16[2,2,128,1024]{3,2,1,0:T(8,128)(2,1)S(1)} %get-tuple-element.89), channel_id=1, source_target_pairs={{0,4},{2,6},{4,0},{6,2},{1,5},{3,7},{5,1},{7,3},{8,12},{10,14},{12... | collective-permute-start | bytes 3145736 | tf_op jit(solution)/shard_map/ppermute | solution.py:443
  127.9 53.1 %all-to-all-start.1 = ((bf16[8,4,256,128]{3,2,1,0:T(8,128)(2,1)}), bf16[8,4,256,128]{3,2,1,0:T(8,128)(2,1)}, u32[]{:S(2)}, u32[]{:S(2)}) async-start(bf16[8,4,256,128]{3,2,1,0:T(8,128)(2,1)} %bitcast.18), calls=%async_computation.1 | async-start | bytes 4194304 | tf_op jit(solution)/shard_map/all_to_all | solution.py:543
  147.3 30.2 %collective-permute-start.9 = (bf16[2,128,1024]{2,1,0:T(8,128)(2,1)S(1)}, bf16[2,128,1024]{2,1,0:T(8,128)(2,1)S(1)}, u32[]{:S(2)}, u32[]{:S(2)}) collective-permute-start(bf16[2,128,1024]{2,1,0:T(8,128)(2,1)S(1)} %slice_bitcast_fusion.2), channel_id=1, source_target_pairs={{0,4},{2,6},{4,0},{6,2},{1,5},{3,7},{5,1},{7,3},{8,12},{10,14},{12... | collective-permute-start | bytes 1572872 | tf_op jit(solution)/shard_map/ppermute | solution.py:443
  150.8 26.9 %collective-permute-start.11 = (bf16[2,128,1024]{2,1,0:T(8,128)(2,1)S(1)}, bf16[2,128,1024]{2,1,0:T(8,128)(2,1)S(1)}, u32[]{:S(2)}, u32[]{:S(2)}) collective-permute-start(bf16[2,128,1024]{2,1,0:T(8,128)(2,1)S(1)} %slice_bitcast_fusion), channel_id=1, source_target_pairs={{0,2},{2,0},{4,6},{6,4},{1,3},{3,1},{5,7},{7,5},{8,10},{10,8},{12,... | collective-permute-start | bytes 1572872 | tf_op jit(solution)/shard_map/ppermute | solution.py:443
  180.9 4.5 copy-start.4
  180.9 36.4 %all-to-all-start.2 = ((bf16[8,4,256,128]{3,2,1,0:T(8,128)(2,1)}), bf16[8,4,256,128]{3,2,1,0:T(8,128)(2,1)}, u32[]{:S(2)}, u32[]{:S(2)}) async-start(bf16[8,4,256,128]{3,2,1,0:T(8,128)(2,1)} %bitcast_bitcast_fusion), calls=%async_computation.2 | async-start | bytes 4194304 | tf_op jit(solution)/shard_map/all_to_all | solution.py:543
  185.4 2.3 copy-start.24
  186.5 30.8 %collective-permute-start.12 = (bf16[4,4,256,128]{3,2,1,0:T(8,128)(2,1)}, bf16[4,4,256,128]{3,2,1,0:T(8,128)(2,1)S(1)}, u32[]{:S(2)}, u32[]{:S(2)}) collective-permute-start(bf16[4,4,256,128]{3,2,1,0:T(8,128)(2,1)} %slice.213), channel_id=1, source_target_pairs={{8,0},{16,8},{24,16},{9,1},{17,9},{25,17},{10,2},{18,10},{26,18},{... | collective-permute-start | bytes 3145736 | tf_op jit(solution)/shard_map/ppermute | solution.py:321
  188.8 28.5 %collective-permute-start.13 = (bf16[4,4,256,128]{3,2,1,0:T(8,128)(2,1)}, bf16[4,4,256,128]{3,2,1,0:T(8,128)(2,1)}, u32[]{:S(2)}, u32[]{:S(2)}) collective-permute-start(bf16[4,4,256,128]{3,2,1,0:T(8,128)(2,1)} %slice.214), channel_id=1, source_target_pairs={{0,8},{8,16},{16,24},{1,9},{9,17},{17,25},{2,10},{10,18},{18,26},{... | collective-permute-start | bytes 3145736 | tf_op jit(solution)/shard_map/ppermute | solution.py:321
  217.4 2.2 copy-start.1
  231.5 121.7 %all-to-all-start.3 = ((bf16[8,2,2,1024,128]{4,3,2,1,0:T(8,128)(2,1)}), bf16[8,2,2,1024,128]{4,3,2,1,0:T(8,128)(2,1)}, u32[]{:S(2)}, u32[]{:S(2)}) async-start(bf16[8,2,2,1024,128]{4,3,2,1,0:T(8,128)(2,1)} %shard_map.206), calls=%async_computation.3 | async-start | bytes 16777216 | tf_op jit(solution)/shard_map/all_to_all | solution.py:588
  236.5 11.4 %copy-start.34 = (s32[32]{0:T(128)S(1)}, s32[32]{0:T(128)}, u32[]{:S(2)}) copy-start(s32[32]{0:T(128)} %param.25) | copy-start | bytes 388
  236.5 89.7 %all-gather.7.cloned.1.call-start = ((), (), s32[]{:S(2)}) async-start(), calls=%async_computation.7 | async-start | bytes 5242880 | tf_op jit(solution)/shard_map/all_gather | solution.py:570
  238.1 30.4 %collective-permute-start.14 = (bf16[2,4,256,128]{3,2,1,0:T(8,128)(2,1)}, bf16[2,4,256,128]{3,2,1,0:T(8,128)(2,1)S(1)}, u32[]{:S(2)}, u32[]{:S(2)}) collective-permute-start(bf16[2,4,256,128]{3,2,1,0:T(8,128)(2,1)} %slice.215), channel_id=1, source_target_pairs={{8,0},{16,8},{24,16},{9,1},{17,9},{25,17},{10,2},{18,10},{26,18},{... | collective-permute-start | bytes 1572872 | tf_op jit(solution)/shard_map/ppermute | solution.py:321
  241.3 27.2 %collective-permute-start.15 = (bf16[2,4,256,128]{3,2,1,0:T(8,128)(2,1)}, bf16[2,4,256,128]{3,2,1,0:T(8,128)(2,1)}, u32[]{:S(2)}, u32[]{:S(2)}) collective-permute-start(bf16[2,4,256,128]{3,2,1,0:T(8,128)(2,1)} %slice.216), channel_id=1, source_target_pairs={{0,8},{8,16},{16,24},{1,9},{9,17},{17,25},{2,10},{10,18},{18,26},{... | collective-permute-start | bytes 1572872 | tf_op jit(solution)/shard_map/ppermute | solution.py:321
  268.5 5.2 %copy-start.6 = (bf16[32,256,128]{2,1,0:T(8,128)(2,1)S(1)}, bf16[32,256,128]{2,1,0:T(8,128)(2,1)}, u32[]{:S(2)}) copy-start(bf16[32,256,128]{2,1,0:T(8,128)(2,1)} %copy-done.5) | copy-start | bytes 6291460
  275.3 51.2 %collective-permute-start.16 = (bf16[1,1024,128]{2,1,0:T(8,128)(2,1)}, bf16[1,1024,128]{2,1,0:T(8,128)(2,1)}, u32[]{:S(2)}, u32[]{:S(2)}) collective-permute-start(bf16[1,1024,128]{2,1,0:T(8,128)(2,1)} %bitcast.33), channel_id=1, source_target_pairs={{0,1},{1,0},{2,3},{3,2},{4,5},{5,4},{6,7},{7,6},{8,9},{9,8},{10,11... | collective-permute-start | bytes 786440 | tf_op jit(solution)/shard_map/ppermute | solution.py:598
  275.4 60.4 %collective-permute-start.17 = (bf16[1,1024,128]{2,1,0:T(8,128)(2,1)}, bf16[1,1024,128]{2,1,0:T(8,128)(2,1)}, u32[]{:S(2)}, u32[]{:S(2)}) collective-permute-start(bf16[1,1024,128]{2,1,0:T(8,128)(2,1)} %bitcast.34), channel_id=1, source_target_pairs={{0,2},{1,3},{2,0},{3,1},{4,6},{5,7},{6,4},{7,5},{8,10},{9,11},{10,... | collective-permute-start | bytes 786440 | tf_op jit(solution)/shard_map/ppermute | solution.py:598
  277.4 73.3 %collective-permute-start.18 = (bf16[1,1024,128]{2,1,0:T(8,128)(2,1)}, bf16[1,1024,128]{2,1,0:T(8,128)(2,1)}, u32[]{:S(2)}, u32[]{:S(2)}) collective-permute-start(bf16[1,1024,128]{2,1,0:T(8,128)(2,1)} %bitcast.35), channel_id=1, source_target_pairs={{0,3},{1,2},{2,1},{3,0},{4,7},{5,6},{6,5},{7,4},{8,11},{9,10},{10,... | collective-permute-start | bytes 786440 | tf_op jit(solution)/shard_map/ppermute | solution.py:598
  277.5 73.2 %collective-permute-start.19 = (bf16[1,1024,128]{2,1,0:T(8,128)(2,1)}, bf16[1,1024,128]{2,1,0:T(8,128)(2,1)}, u32[]{:S(2)}, u32[]{:S(2)}) collective-permute-start(bf16[1,1024,128]{2,1,0:T(8,128)(2,1)} %bitcast.36), channel_id=1, source_target_pairs={{0,4},{1,5},{2,6},{3,7},{4,0},{5,1},{6,2},{7,3},{8,12},{9,13},{10,... | collective-permute-start | bytes 786440 | tf_op jit(solution)/shard_map/ppermute | solution.py:598
  279.2 71.5 %collective-permute-start.20 = (bf16[1,1024,128]{2,1,0:T(8,128)(2,1)}, bf16[1,1024,128]{2,1,0:T(8,128)(2,1)}, u32[]{:S(2)}, u32[]{:S(2)}) collective-permute-start(bf16[1,1024,128]{2,1,0:T(8,128)(2,1)} %bitcast.37), channel_id=1, source_target_pairs={{0,5},{1,4},{2,7},{3,6},{4,1},{5,0},{6,3},{7,2},{8,13},{9,12},{10,... | collective-permute-start | bytes 786440 | tf_op jit(solution)/shard_map/ppermute | solution.py:598
  326.6 24.1 %collective-permute-start.21 = (bf16[1,1024,128]{2,1,0:T(8,128)(2,1)}, bf16[1,1024,128]{2,1,0:T(8,128)(2,1)S(1)}, u32[]{:S(2)}, u32[]{:S(2)}) collective-permute-start(bf16[1,1024,128]{2,1,0:T(8,128)(2,1)} %bitcast.127), channel_id=1, source_target_pairs={{0,6},{1,7},{2,4},{3,5},{4,2},{5,3},{6,0},{7,1},{8,14},{9,15},{10,... | collective-permute-start | bytes 786440 | tf_op jit(solution)/shard_map/ppermute | solution.py:598
  335.8 16.7 %collective-permute-start.22 = (bf16[1,1024,128]{2,1,0:T(8,128)(2,1)}, bf16[1,1024,128]{2,1,0:T(8,128)(2,1)S(1)}, u32[]{:S(2)}, u32[]{:S(2)}) collective-permute-start(bf16[1,1024,128]{2,1,0:T(8,128)(2,1)} %bitcast.126), channel_id=1, source_target_pairs={{0,7},{1,6},{2,5},{3,4},{4,3},{5,2},{6,1},{7,0},{8,15},{9,14},{10,... | collective-permute-start | bytes 786440 | tf_op jit(solution)/shard_map/ppermute | solution.py:598
  366.8 5.1 %copy-start.14 = (bf16[2,256,1024]{2,1,0:T(8,128)(2,1)S(1)}, bf16[2,256,1024]{2,1,0:T(8,128)(2,1)}, u32[]{:S(2)}) copy-start(bf16[2,256,1024]{2,1,0:T(8,128)(2,1)} %copy-done.13) | copy-start | bytes 3145732
  366.8 5.1 %copy-start.18 = (bf16[1,1024,128]{2,1,0:T(8,128)(2,1)S(1)}, bf16[1,1024,128]{2,1,0:T(8,128)(2,1)}, u32[]{:S(2)}) copy-start(bf16[1,1024,128]{2,1,0:T(8,128)(2,1)} %copy-done.17) | copy-start | bytes 786436
  366.8 5.1 %copy-start.20 = (bf16[1,1024,128]{2,1,0:T(8,128)(2,1)S(1)}, bf16[1,1024,128]{2,1,0:T(8,128)(2,1)}, u32[]{:S(2)}) copy-start(bf16[1,1024,128]{2,1,0:T(8,128)(2,1)} %copy-done.19) | copy-start | bytes 786436
  366.8 113.3 %all-to-all-start.5 = ((bf16[8,1,2,1024,128]{4,3,2,1,0:T(8,128)(2,1)}), bf16[8,1,2,1024,128]{4,3,2,1,0:T(8,128)(2,1)}, u32[]{:S(2)}, u32[]{:S(2)}) async-start(bf16[8,1,2,1024,128]{4,3,2,1,0:T(8,128)(2,1)} %copy-done.2), calls=%async_computation.5 | async-start | bytes 8388608 | tf_op jit(solution)/shard_map/all_to_all | solution.py:632
  371.9 4.0 copy-start.12
  374.2 68.4 %collective-permute-start.24 = (bf16[2,256,1024]{2,1,0:T(8,128)(2,1)S(1)}, bf16[2,256,1024]{2,1,0:T(8,128)(2,1)}, u32[]{:S(2)}, u32[]{:S(2)}) collective-permute-start(bf16[2,256,1024]{2,1,0:T(8,128)(2,1)S(1)} %shard_map.212.refs_1_), channel_id=1, source_target_pairs={{0,4},{2,6},{4,0},{6,2},{1,5},{3,7},{5,1},{7,3},{8,12},{10,14},{12... | collective-permute-start | bytes 3145736 | tf_op jit(solution)/shard_map/ppermute | solution.py:443
  378.2 64.4 %collective-permute-start.23 = (bf16[2,256,1024]{2,1,0:T(8,128)(2,1)S(1)}, bf16[2,256,1024]{2,1,0:T(8,128)(2,1)S(1)}, u32[]{:S(2)}, u32[]{:S(2)}) collective-permute-start(bf16[2,256,1024]{2,1,0:T(8,128)(2,1)S(1)} %shard_map.211.refs_0_), channel_id=1, source_target_pairs={{0,2},{2,0},{4,6},{6,4},{1,3},{3,1},{5,7},{7,5},{8,10},{10,8},{12,... | collective-permute-start | bytes 3145736 | tf_op jit(solution)/shard_map/ppermute | solution.py:443
  379.7 84.9 %collective-permute-start.27 = (bf16[2,256,1024]{2,1,0:T(8,128)(2,1)S(1)}, bf16[2,256,1024]{2,1,0:T(8,128)(2,1)}, u32[]{:S(2)}, u32[]{:S(2)}) collective-permute-start(bf16[2,256,1024]{2,1,0:T(8,128)(2,1)S(1)} %shard_map.212.refs_1_), channel_id=1, source_target_pairs={{0,2},{2,0},{4,6},{6,4},{1,3},{3,1},{5,7},{7,5},{8,10},{10,8},{12,... | collective-permute-start | bytes 3145736 | tf_op jit(solution)/shard_map/ppermute | solution.py:443
  380.3 84.4 %collective-permute-start.30 = (bf16[2,256,1024]{2,1,0:T(8,128)(2,1)S(1)}, bf16[2,256,1024]{2,1,0:T(8,128)(2,1)S(1)}, u32[]{:S(2)}, u32[]{:S(2)}) collective-permute-start(bf16[2,256,1024]{2,1,0:T(8,128)(2,1)S(1)} %shard_map.212.refs_1_), channel_id=1, source_target_pairs={{0,1},{1,0},{2,3},{3,2},{4,5},{5,4},{6,7},{7,6},{8,9},{9,8},{10,11... | collective-permute-start | bytes 3145736 | tf_op jit(solution)/shard_map/ppermute | solution.py:447
  399.7 65.5 %collective-permute-start.28 = (bf16[2,256,1024]{2,1,0:T(8,128)(2,1)S(1)}, bf16[2,256,1024]{2,1,0:T(8,128)(2,1)}, u32[]{:S(2)}, u32[]{:S(2)}) collective-permute-start(bf16[2,256,1024]{2,1,0:T(8,128)(2,1)S(1)} %shard_map.211.refs_0_), channel_id=1, source_target_pairs={{0,4},{2,6},{4,0},{6,2},{1,5},{3,7},{5,1},{7,3},{8,12},{10,14},{12... | collective-permute-start | bytes 3145736 | tf_op jit(solution)/shard_map/ppermute | solution.py:443
  442.6 22.7 %collective-permute-start.29 = (bf16[2,256,1024]{2,1,0:T(8,128)(2,1)S(1)}, bf16[2,256,1024]{2,1,0:T(8,128)(2,1)S(1)}, u32[]{:S(2)}, u32[]{:S(2)}) collective-permute-start(bf16[2,256,1024]{2,1,0:T(8,128)(2,1)S(1)} %shard_map.211.refs_0_), channel_id=1, source_target_pairs={{0,1},{1,0},{2,3},{3,2},{4,5},{5,4},{6,7},{7,6},{8,9},{9,8},{10,11... | collective-permute-start | bytes 3145736 | tf_op jit(solution)/shard_map/ppermute | solution.py:447
  442.6 24.2 %collective-permute-start.31 = (bf16[2,256,1024]{2,1,0:T(8,128)(2,1)S(1)}, bf16[2,256,1024]{2,1,0:T(8,128)(2,1)S(1)}, u32[]{:S(2)}, u32[]{:S(2)}) collective-permute-start(bf16[2,256,1024]{2,1,0:T(8,128)(2,1)S(1)} %collective-permute-done.23.refs_2_), channel_id=1, source_target_pairs={{0,1},{1,0},{2,3},{3,2},{4,5},{5,4},{6,7},{7,6},{8,9},{9,8},{10,11... | collective-permute-start | bytes 3145736 | tf_op jit(solution)/shard_map/ppermute | solution.py:447
  464.7 5.3 %collective-permute-start.34 = (bf16[2,256,1024]{2,1,0:T(8,128)(2,1)}, bf16[2,256,1024]{2,1,0:T(8,128)(2,1)}, u32[]{:S(2)}, u32[]{:S(2)}) collective-permute-start(bf16[2,256,1024]{2,1,0:T(8,128)(2,1)} %collective-permute-done.24.refs_5_), channel_id=1, source_target_pairs={{0,1},{1,0},{2,3},{3,2},{4,5},{5,4},{6,7},{7,6},{8,9},{9,8},{10,11... | collective-permute-start | bytes 3145736 | tf_op jit(solution)/shard_map/ppermute | solution.py:447
  464.7 5.3 %collective-permute-start.32 = (bf16[2,256,1024]{2,1,0:T(8,128)(2,1)}, bf16[2,256,1024]{2,1,0:T(8,128)(2,1)}, u32[]{:S(2)}, u32[]{:S(2)}) collective-permute-start(bf16[2,256,1024]{2,1,0:T(8,128)(2,1)} %collective-permute-done.27.refs_3_), channel_id=1, source_target_pairs={{0,1},{1,0},{2,3},{3,2},{4,5},{5,4},{6,7},{7,6},{8,9},{9,8},{10,11... | collective-permute-start | bytes 3145736 | tf_op jit(solution)/shard_map/ppermute | solution.py:447
  465.2 5.5 %collective-permute-start.33 = (bf16[2,256,1024]{2,1,0:T(8,128)(2,1)}, bf16[2,256,1024]{2,1,0:T(8,128)(2,1)}, u32[]{:S(2)}, u32[]{:S(2)}) collective-permute-start(bf16[2,256,1024]{2,1,0:T(8,128)(2,1)} %collective-permute-done.28.refs_4_), channel_id=1, source_target_pairs={{0,1},{1,0},{2,3},{3,2},{4,5},{5,4},{6,7},{7,6},{8,9},{9,8},{10,11... | collective-permute-start | bytes 3145736 | tf_op jit(solution)/shard_map/ppermute | solution.py:447
  465.3 25.6 %collective-permute-start.25 = (bf16[2,256,1024]{2,1,0:T(8,128)(2,1)S(1)}, bf16[2,256,1024]{2,1,0:T(8,128)(2,1)}, u32[]{:S(2)}, u32[]{:S(2)}) collective-permute-start(bf16[2,256,1024]{2,1,0:T(8,128)(2,1)S(1)} %collective-permute-done.23.refs_2_), channel_id=1, source_target_pairs={{0,4},{2,6},{4,0},{6,2},{1,5},{3,7},{5,1},{7,3},{8,12},{10,14},{12... | collective-permute-start | bytes 3145736 | tf_op jit(solution)/shard_map/ppermute | solution.py:443
  467.8 25.5 %collective-permute-start.26 = (bf16[2,256,1024]{2,1,0:T(8,128)(2,1)}, bf16[2,256,1024]{2,1,0:T(8,128)(2,1)}, u32[]{:S(2)}, u32[]{:S(2)}) collective-permute-start(bf16[2,256,1024]{2,1,0:T(8,128)(2,1)} %collective-permute-done.24.refs_5_), channel_id=1, source_target_pairs={{0,2},{2,0},{4,6},{6,4},{1,3},{3,1},{5,7},{7,5},{8,10},{10,8},{12,... | collective-permute-start | bytes 3145736 | tf_op jit(solution)/shard_map/ppermute | solution.py:443
  480.1 13.8 %copy-start.30 = (f32[208,256]{1,0:T(8,128)S(1)}, f32[208,256]{1,0:T(8,128)}, u32[]{:S(2)}) copy-start(f32[208,256]{1,0:T(8,128)} %param.26) | copy-start | bytes 638980
  480.2 13.8 %copy-start.31 = (f32[208,256]{1,0:T(8,128)S(1)}, f32[208,256]{1,0:T(8,128)}, u32[]{:S(2)}) copy-start(f32[208,256]{1,0:T(8,128)} %param.28) | copy-start | bytes 638980
  480.2 13.8 %copy-start.32 = (f32[208,256]{1,0:T(8,128)S(1)}, f32[208,256]{1,0:T(8,128)}, u32[]{:S(2)}) copy-start(f32[208,256]{1,0:T(8,128)} %param.29) | copy-start | bytes 638980
  480.2 13.8 %copy-start.33 = (bf16[208,256]{1,0:T(8,128)(2,1)S(1)}, bf16[208,256]{1,0:T(8,128)(2,1)}, u32[]{:S(2)}) copy-start(bf16[208,256]{1,0:T(8,128)(2,1)} %param.27) | copy-start | bytes 319492
  493.3 2.9 collective-permute-start.35
  493.3 4.4 collective-permute-start.36
  (15 other events, 19.3 us)
Sparse Core Ops, SparseCore 0:
  113.7 86.1 all-gather.4
  239.0 87.2 all-gather.6
